TPU v7x, 32 devices: a whole 2x2x4 slice. The times are simulated.
32 devices in a mesh: row: 4 (over y, core), col: 8 (over z, x).
Axes of the slice: x: 2, y: 2, z: 4, core: 2. Of those that a mesh axis runs over, the one named last changes fastest.
Arguments:
- hidden_in: bfloat16 [10880, 1024], P(('row', 'col')), may hold values from -6 to 6
- cond: bfloat16 [16, 1024], P('row'), may hold values from -6 to 6
- scale_sizes: int32 [16, 10], P('row'), may hold values from 1 to 256, 680 in all within a row
- w_ada: bfloat16 [2, 1024, 6, 1024], P(None, 'row', None, 'col'), may hold values from -0.09375 to 0.09375
- b_ada: bfloat16 [2, 6, 1024], P(None, None, 'col'), may hold values from -1 to 1
- w_qkv: bfloat16 [2, 1024, 3, 1024], P(None, 'row', None, 'col'), may hold values from -0.1875 to 0.1875
- b_qkv: bfloat16 [2, 2, 1024], P(None, None, 'col'), may hold values from -3 to 3
- head_scale: bfloat16 [2, 16], P(None, 'col'), may hold values from 6 to 16
- w_proj: bfloat16 [2, 1024, 1024], P(None, 'col', 'row'), may hold values from -0.75 to 0.75
- b_proj: bfloat16 [2, 1024], P(None, 'col'), may hold values from -3 to 3
- w_fc1: bfloat16 [2, 1024, 4096], P(None, 'row', 'col'), may hold values from -0.1875 to 0.1875
- b_fc1: bfloat16 [2, 4096], P(None, 'col'), may hold values from -3 to 3
- w_fc2: bfloat16 [2, 4096, 1024], P(None, 'col', 'row'), may hold values from -0.09375 to 0.09375
- b_fc2: bfloat16 [2, 1024], P(None, 'col'), may hold values from -3 to 3
- grad_out: bfloat16 [10880, 1024], P(('row', 'col')), may hold values from -6 to 6
Outputs:
- mixed: bfloat16 [10880, 1024], P(('row', 'col'))
- grad_in: float32 [10880, 1024], P(('row', 'col'))
- grad_w_ada: float32 [2, 1024, 6, 1024], P(None, 'row', None, 'col')
- grad_b_ada: float32 [2, 6, 1024], P(None, None, 'col')
- grad_w_qkv: float32 [2, 1024, 3, 1024], P(None, 'row', None, 'col')
- grad_b_qkv: float32 [2, 2, 1024], P(None, None, 'col')
- grad_head_scale: float32 [2, 16], P(None, 'col')
- grad_w_proj: float32 [2, 1024, 1024], P(None, 'col', 'row')
- grad_b_proj: float32 [2, 1024], P(None, 'col')
- grad_w_fc1: float32 [2, 1024, 4096], P(None, 'row', 'col')
- grad_b_fc1: float32 [2, 4096], P(None, 'col')
- grad_w_fc2: float32 [2, 4096, 1024], P(None, 'col', 'row')
- grad_b_fc2: float32 [2, 1024], P(None, 'col')
Inputs may be any that keep to these rules, and one draw needn't show every extreme that they name: `scale_sizes`: each row holds the token counts of the 10 scales of one sequence in order, summing to 680.
All inputs are finite; a program needn't handle non-finite values.
Results may differ from a plain program's by a relative error of at most 0.025.
Values may be sent and summed in bfloat16 or wider, within the bound.
No kernel may reach another device: no remote copies, remote signals or barrier semaphores. Data moves between devices by JAX's collectives and lax.ppermute only.
A program may use at most 256 MiB of HBM per device.

v0:
```python
import jax
import jax.numpy as jnp
from jax import lax
from jax.sharding import PartitionSpec as P

HIGH = lax.Precision.HIGHEST
EPS_NORM = 1e-06
EPS_UNIT = 1e-06
NEG_FILL = -1e30


def block_ends(scale_sizes, seq_len):
    ends = jnp.cumsum(scale_sizes, axis=1)
    starts = ends - scale_sizes
    position = jnp.arange(seq_len, dtype=jnp.int32)
    picked = jnp.where(starts[:, None, :] <= position[None, :, None], scale_sizes[:, None, :], 0)
    return jnp.sum(picked, axis=2)


def normalize(values):
    center = jnp.mean(values, axis=-1, keepdims=True)
    spread = jnp.mean(values * values, axis=-1, keepdims=True) - center * center
    rstd = lax.rsqrt(spread + EPS_NORM)
    return ((values - center) * rstd, rstd)


def norm_back(grad_normed, normed, rstd):
    means = jnp.mean(grad_normed, axis=-1, keepdims=True)
    crosses = jnp.mean(grad_normed * normed, axis=-1, keepdims=True)
    return rstd * (grad_normed - means - normed * crosses)


def unit_pair(queries, key_rows, scale_here):
    q_norm = (
        queries
        * lax.rsqrt(jnp.sum(queries * queries, axis=-1, keepdims=True) + EPS_UNIT)
        * scale_here[:, None]
    )
    k_norm = key_rows * lax.rsqrt(jnp.sum(key_rows * key_rows, axis=-1, keepdims=True) + EPS_UNIT)
    return (q_norm, k_norm)


def project_in(hidden_low, weight):
    return (
        jnp.dot(
            lax.all_gather(hidden_low, "col", axis=0, tiled=True),
            weight,
            preferred_element_type=jnp.float32,
        ),
        hidden_low,
    )


def back_in(grad_three, kept, weight, whole_weight):
    tok_row = grad_three.shape[0]
    grad_low = grad_three.reshape(tok_row, grad_three.shape[1] * grad_three.shape[2])
    own_grads = lax.all_to_all(grad_three, "col", split_axis=0, concat_axis=2, tiled=True)
    grad_hidden = lax.dot_general(
        own_grads, whole_weight, (((1, 2), (1, 2)), ((), ())), preferred_element_type=jnp.float32
    )

    def add_piece(total, piece, start):
        return lax.dot_general(
            piece, grad_low, (((0,), (0,)), ((), ())), preferred_element_type=jnp.float32
        )

    init = jnp.zeros(weight.shape, jnp.float32)
    grad_weight = add_piece(init, lax.all_gather(kept, "col", axis=0, tiled=True), jnp.int32(0))
    return (grad_hidden, grad_weight)


def project_out(act_low, whole_weight):
    own_rows = lax.all_to_all(act_low, "col", split_axis=0, concat_axis=1, tiled=True)
    return jnp.dot(own_rows, whole_weight, preferred_element_type=jnp.float32)


def back_out(grad_low, act_low, weight):

    def add_piece(carry, piece, start):
        part = lax.dot_general(
            piece, weight, (((1,), (1,)), ((), ())), preferred_element_type=jnp.float32
        )
        grad_weight = lax.dot_general(
            act_low, piece, (((0,), (0,)), ((), ())), preferred_element_type=jnp.float32
        )
        return (part, grad_weight)

    init = (
        jnp.zeros((act_low.shape[0], weight.shape[0]), jnp.float32),
        jnp.zeros(weight.shape, jnp.float32),
    )
    return add_piece(init, lax.all_gather(grad_low, "col", axis=0, tiled=True), jnp.int32(0))


def masked_scores(q_rows, k_rows, ends):
    position = jnp.arange(k_rows.shape[0], dtype=jnp.int32)
    scores = jnp.einsum("the,she->hts", q_rows, k_rows, preferred_element_type=jnp.float32)
    visible = position[None, :] < ends[:, None]
    return jnp.where(visible[None], scores, NEG_FILL)


def attend(pieces):
    q_rows, k_rows, v_rows, ends = pieces
    scores = masked_scores(q_rows, k_rows, ends)
    top = jnp.max(scores, axis=-1, keepdims=True)
    expo = jnp.exp(scores - top)
    total = jnp.sum(expo, axis=-1, keepdims=True)
    probs = (expo / total).astype(jnp.bfloat16)
    attended = jnp.einsum("hts,she->the", probs, v_rows, preferred_element_type=jnp.float32)
    return (attended, (top + jnp.log(total))[..., 0])


def attend_back(pieces):
    q_rows, k_rows, v_rows, ends, log_total, grad_rows = pieces
    scores = masked_scores(q_rows, k_rows, ends)
    probs = jnp.exp(scores - log_total[..., None])
    grad_probs = jnp.einsum("the,she->hts", grad_rows, v_rows, preferred_element_type=jnp.float32)
    delta = jnp.sum(probs * grad_probs, axis=-1, keepdims=True)
    grad_scores = (probs * (grad_probs - delta)).astype(jnp.bfloat16)
    grad_q = jnp.einsum("hts,she->the", grad_scores, k_rows, preferred_element_type=jnp.float32)
    grad_k = jnp.einsum("hts,the->she", grad_scores, q_rows, preferred_element_type=jnp.float32)
    grad_v = jnp.einsum(
        "hts,the->she", probs.astype(jnp.bfloat16), grad_rows, preferred_element_type=jnp.float32
    )
    return (grad_q, grad_k, grad_v)


def gelu_tanh(values):
    return jax.nn.gelu(values, approximate=True)


def on_device(
    hidden_in,
    cond,
    scale_sizes,
    w_ada,
    b_ada,
    w_qkv,
    b_qkv,
    head_scale,
    w_proj,
    b_proj,
    w_fc1,
    b_fc1,
    w_fc2,
    b_fc2,
    grad_out,
):
    seq_row, width = cond.shape
    rows_dev = hidden_in.shape[0]
    tok_row = rows_dev * lax.axis_size("col")
    seq_len = tok_row // seq_row
    layer_count = w_ada.shape[0]
    d_col = b_qkv.shape[2]
    heads_dev = head_scale.shape[1]
    head_width = d_col // heads_dev
    full_ada, full_qkv, full_fc1, full_proj, full_fc2 = (
        lax.all_gather(w_ada, "row", axis=1, tiled=True),
        lax.all_gather(w_qkv, "row", axis=1, tiled=True),
        lax.all_gather(w_fc1, "row", axis=1, tiled=True),
        lax.all_gather(w_proj, "row", axis=2, tiled=True),
        lax.all_gather(w_fc2, "row", axis=2, tiled=True),
    )
    whole_proj, whole_fc2, whole_qkv, whole_fc1 = (
        lax.all_gather(full_proj, "col", axis=1, tiled=True),
        lax.all_gather(full_fc2, "col", axis=1, tiled=True),
        lax.all_gather(full_qkv, "col", axis=3, tiled=True),
        lax.all_gather(full_fc1, "col", axis=2, tiled=True),
    )
    ends = block_ends(scale_sizes, seq_len)
    silu_low = jax.nn.silu(cond.astype(jnp.float32)).astype(jnp.bfloat16)
    places = lax.axis_index("col") * rows_dev + jnp.arange(rows_dev, dtype=jnp.int32)
    member = (places[:, None] // seq_len == jnp.arange(seq_row, dtype=jnp.int32)[None, :]).astype(
        jnp.float32
    )

    def per_token(values):
        return jnp.dot(member, values, precision=HIGH)

    def per_sequence(values):
        return lax.dot_general(member, values, (((0,), (0,)), ((), ())), precision=HIGH)

    ada_parts = []
    for layer_index in range(layer_count):
        part = jnp.dot(
            silu_low,
            full_ada[layer_index].reshape(width, 6 * d_col),
            preferred_element_type=jnp.float32,
        )
        ada_parts.append(
            part.reshape(seq_row, 6, d_col) + b_ada[layer_index].astype(jnp.float32)[None]
        )
    ada_full, bias_proj_full, bias_fc2_full = (
        lax.all_gather(jnp.stack(ada_parts), "col", axis=3, tiled=True),
        lax.all_gather(b_proj.astype(jnp.float32), "col", axis=1, tiled=True),
        lax.all_gather(b_fc2.astype(jnp.float32), "col", axis=1, tiled=True),
    )
    current = hidden_in.astype(jnp.float32)
    saved = []
    for layer_index in range(layer_count):
        ada = ada_full[layer_index]
        gamma1, gamma2, scale1, scale2, shift1, shift2 = [
            per_token(ada[:, index]) for index in range(6)
        ]
        normed1, rstd1 = normalize(current)
        hidden1 = (normed1 * (1.0 + scale1) + shift1).astype(jnp.bfloat16)
        mixed_qkv, kept1 = project_in(hidden1, full_qkv[layer_index].reshape(width, 3 * d_col))
        bias_two = b_qkv[layer_index].astype(jnp.float32)
        bias_three = jnp.stack((bias_two[0], jnp.zeros_like(bias_two[0]), bias_two[1]))
        mixed_qkv = mixed_qkv + bias_three.reshape(1, 3 * d_col)
        split = mixed_qkv.reshape(seq_row, seq_len, 3, heads_dev, head_width)
        queries, key_rows, value_rows = (split[:, :, 0], split[:, :, 1], split[:, :, 2])
        scale_here = head_scale[layer_index].astype(jnp.float32)
        q_norm, k_norm = unit_pair(queries, key_rows, scale_here)
        q_low = q_norm.astype(jnp.bfloat16)
        k_low = k_norm.astype(jnp.bfloat16)
        v_low = value_rows.astype(jnp.bfloat16)
        attended, log_total = lax.map(attend, (q_low, k_low, v_low, ends))
        attn_low = attended.reshape(tok_row, d_col).astype(jnp.bfloat16)
        branch = project_out(attn_low, whole_proj[layer_index]) + bias_proj_full[layer_index][None]
        middle = current + gamma1 * branch
        normed2, rstd2 = normalize(middle)
        hidden2 = (normed2 * (1.0 + scale2) + shift2).astype(jnp.bfloat16)
        pre_act, kept2 = project_in(hidden2, full_fc1[layer_index])
        pre_act = pre_act + b_fc1[layer_index].astype(jnp.float32)[None]
        act_low = gelu_tanh(pre_act).astype(jnp.bfloat16)
        feed = project_out(act_low, whole_fc2[layer_index]) + bias_fc2_full[layer_index][None]
        saved.append(
            (
                normed1,
                rstd1,
                kept1,
                queries,
                key_rows,
                scale_here,
                q_low,
                k_low,
                v_low,
                log_total,
                attn_low,
                branch,
                normed2,
                rstd2,
                kept2,
                pre_act,
                act_low,
                feed,
            )
        )
        current = middle + gamma2 * feed
    mixed = current.astype(jnp.bfloat16)
    grad_state = grad_out.astype(jnp.float32)
    grads_ada = [None] * layer_count
    grads_w_qkv = [None] * layer_count
    grads_b_qkv = [None] * layer_count
    grads_scale = [None] * layer_count
    grads_w_proj = [None] * layer_count
    grads_b_proj = [None] * layer_count
    grads_w_fc1 = [None] * layer_count
    grads_b_fc1 = [None] * layer_count
    grads_w_fc2 = [None] * layer_count
    grads_b_fc2 = [None] * layer_count
    for layer_index in reversed(range(layer_count)):
        (
            normed1,
            rstd1,
            kept1,
            queries,
            key_rows,
            scale_here,
            q_low,
            k_low,
            v_low,
            log_total,
            attn_low,
            branch,
            normed2,
            rstd2,
            kept2,
            pre_act,
            act_low,
            feed,
        ) = saved[layer_index]
        ada = ada_full[layer_index]
        gamma1, gamma2, scale1, scale2, shift1, shift2 = [
            per_token(ada[:, index]) for index in range(6)
        ]
        d_gamma2 = per_sequence(grad_state * feed)
        grad_feed = (grad_state * gamma2).astype(jnp.bfloat16)
        grads_b_fc2[layer_index] = jnp.sum(grad_feed.astype(jnp.float32), axis=0)
        grad_act, grads_w_fc2[layer_index] = back_out(grad_feed, act_low, full_fc2[layer_index])
        gelu_pull = jax.vjp(gelu_tanh, pre_act)[1]
        grad_pre = gelu_pull(grad_act)[0].astype(jnp.bfloat16)
        grads_b_fc1[layer_index] = jnp.sum(grad_pre.astype(jnp.float32), axis=0)
        whole_one = whole_fc1[layer_index].reshape(width, 1, whole_fc1.shape[2])
        grad_hidden2, grads_w_fc1[layer_index] = back_in(
            grad_pre.reshape(tok_row, 1, grad_pre.shape[1]), kept2, full_fc1[layer_index], whole_one
        )
        d_scale2 = per_sequence(grad_hidden2 * normed2)
        d_shift2 = per_sequence(grad_hidden2)
        grad_middle = grad_state + norm_back(grad_hidden2 * (1.0 + scale2), normed2, rstd2)
        d_gamma1 = per_sequence(grad_middle * branch)
        grad_branch = (grad_middle * gamma1).astype(jnp.bfloat16)
        grads_b_proj[layer_index] = jnp.sum(grad_branch.astype(jnp.float32), axis=0)
        grad_attn, grads_w_proj[layer_index] = back_out(
            grad_branch, attn_low, full_proj[layer_index]
        )
        grad_attn_low = grad_attn.astype(jnp.bfloat16).reshape(
            seq_row, seq_len, heads_dev, head_width
        )
        grad_qn, grad_kn, grad_v = lax.map(
            attend_back, (q_low, k_low, v_low, ends, log_total, grad_attn_low)
        )
        unit_pull = jax.vjp(unit_pair, queries, key_rows, scale_here)[1]
        grad_q, grad_k, grads_scale[layer_index] = unit_pull((grad_qn, grad_kn))
        grad_qkv = (
            jnp.stack((grad_q, grad_k, grad_v), axis=2)
            .reshape(tok_row, 3, d_col)
            .astype(jnp.bfloat16)
        )
        bias_sums = jnp.sum(grad_qkv.astype(jnp.float32), axis=0)
        grads_b_qkv[layer_index] = jnp.stack((bias_sums[0], bias_sums[2]))
        grad_hidden1, weight_qkv = back_in(
            grad_qkv, kept1, full_qkv[layer_index].reshape(width, 3 * d_col), whole_qkv[layer_index]
        )
        grads_w_qkv[layer_index] = weight_qkv.reshape(width, 3, d_col)
        d_scale1 = per_sequence(grad_hidden1 * normed1)
        d_shift1 = per_sequence(grad_hidden1)
        grad_state = grad_middle + norm_back(grad_hidden1 * (1.0 + scale1), normed1, rstd1)
        grads_ada[layer_index] = jnp.stack(
            (d_gamma1, d_gamma2, d_scale1, d_scale2, d_shift1, d_shift2), axis=1
        )
    ada_sums, bias_proj_col, bias_fc2_col = (
        lax.psum_scatter(
            jnp.stack(grads_ada).astype(jnp.bfloat16), "col", scatter_dimension=3, tiled=True
        ).astype(jnp.float32),
        lax.psum_scatter(
            jnp.stack(grads_b_proj).astype(jnp.bfloat16), "col", scatter_dimension=1, tiled=True
        ).astype(jnp.float32),
        lax.psum_scatter(
            jnp.stack(grads_b_fc2).astype(jnp.bfloat16), "col", scatter_dimension=1, tiled=True
        ).astype(jnp.float32),
    )
    grad_ada = ada_sums.astype(jnp.bfloat16)
    weights_ada = []
    for layer_index in range(layer_count):
        weight_ada = lax.dot_general(
            silu_low,
            grad_ada[layer_index].reshape(seq_row, 6 * d_col),
            (((0,), (0,)), ((), ())),
            preferred_element_type=jnp.float32,
        )
        weights_ada.append(weight_ada.reshape(width, 6, d_col))
    bias_ada_local = jnp.sum(grad_ada.astype(jnp.float32), axis=1)
    sum_ada, sum_qkv, sum_fc1, sum_proj, sum_fc2 = (
        lax.psum_scatter(
            jnp.stack(weights_ada).astype(jnp.bfloat16), "row", scatter_dimension=1, tiled=True
        ).astype(jnp.float32),
        lax.psum_scatter(
            jnp.stack(grads_w_qkv).astype(jnp.bfloat16), "row", scatter_dimension=1, tiled=True
        ).astype(jnp.float32),
        lax.psum_scatter(
            jnp.stack(grads_w_fc1).astype(jnp.bfloat16), "row", scatter_dimension=1, tiled=True
        ).astype(jnp.float32),
        lax.psum_scatter(
            jnp.stack(grads_w_proj).astype(jnp.bfloat16), "row", scatter_dimension=2, tiled=True
        ).astype(jnp.float32),
        lax.psum_scatter(
            jnp.stack(grads_w_fc2).astype(jnp.bfloat16), "row", scatter_dimension=2, tiled=True
        ).astype(jnp.float32),
    )
    bias_ada, bias_qkv, scale_grad, bias_proj, bias_fc1, bias_fc2 = lax.psum(
        (
            bias_ada_local,
            jnp.stack(grads_b_qkv),
            jnp.stack(grads_scale),
            bias_proj_col,
            jnp.stack(grads_b_fc1),
            bias_fc2_col,
        ),
        "row",
    )
    return (
        mixed,
        grad_state,
        sum_ada,
        bias_ada,
        sum_qkv,
        bias_qkv,
        scale_grad,
        sum_proj,
        bias_proj,
        sum_fc1,
        bias_fc1,
        sum_fc2,
        bias_fc2,
    )


def solution(mesh):
    return jax.shard_map(
        on_device,
        mesh=mesh,
        in_specs=(
            P(("row", "col"), None),
            P("row", None),
            P("row", None),
            P(None, "row", None, "col"),
            P(None, None, "col"),
            P(None, "row", None, "col"),
            P(None, None, "col"),
            P(None, "col"),
            P(None, "col", "row"),
            P(None, "col"),
            P(None, "row", "col"),
            P(None, "col"),
            P(None, "col", "row"),
            P(None, "col"),
            P(("row", "col"), None),
        ),
        out_specs=(
            P(("row", "col"), None),
            P(("row", "col"), None),
            P(None, "row", None, "col"),
            P(None, None, "col"),
            P(None, "row", None, "col"),
            P(None, None, "col"),
            P(None, "col"),
            P(None, "col", "row"),
            P(None, "col"),
            P(None, "row", "col"),
            P(None, "col"),
            P(None, "col", "row"),
            P(None, "col"),
        ),
        check_vma=False,
    )
```

profile of v0, /device:TPU:1, one launch (start us, length us, event | category | flops | bytes accessed | tf_op | source)
XLA Modules:
  0.0 2714.3 jit_solution(8374081780219725373)
XLA Ops:
  10.8 30.8 %all-gather.25.cloned.1.call-done = bf16[2,1024,6,128]{1,3,2,0:T(8,128)(2,1)} async-done(((bf16[2,256,6,128]{1,3,2,0:T(8,128)(2,1)}), bf16[2,1024,6,128]{1,3,2,0:T(8,128)(2,1)}) %all-gather.25.cloned.1.call-update) | async-done | bytes 3145744 | tf_op jit(solution)/shard_map/all_gather | solution.py:158
  45.5 22.0 all_gather.65
  87.2 77.3 %all-gather.41.cloned.1.call-done = bf16[8,340,1024]{2,1,0:T(8,128)(2,1)} async-done(((bf16[1,340,1024]{2,1,0:T(8,128)(2,1)}), bf16[8,340,1024]{2,1,0:T(8,128)(2,1)}) %all-gather.41.cloned.1.call-update) | async-done | bytes 5570576 | tf_op jit(solution)/shard_map/all_gather | solution.py:46
  198.5 21.5 while.52
  229.2 29.2 %all_gather.70 = f32[2,1024]{1,0:T(2,128)S(1)} all-gather(f32[2,128]{1,0:T(2,128)S(1)} %convert_element_type.242), channel_id=1, replica_groups=mesh['row'=4,'col'=8] {'col'}, dimensions={1}, use_global_device_ids=true | all-gather | bytes 9216 | tf_op jit(solution)/shard_map/all_gather | solution.py:195
  270.8 91.9 %all-gather.43.cloned.1.call-done = bf16[8,340,1024]{2,1,0:T(8,128)(2,1)} async-done(((bf16[1,340,1024]{2,1,0:T(8,128)(2,1)}), bf16[8,340,1024]{2,1,0:T(8,128)(2,1)}) %all-gather.43.cloned.1.call-update) | async-done | bytes 5570576 | tf_op jit(solution)/shard_map/all_gather | solution.py:46
  407.2 102.9 %all_gather.75 = f32[2,1024]{1,0:T(2,128)S(1)} all-gather(f32[2,128]{1,0:T(2,128)S(1)} %convert_element_type.245), channel_id=1, replica_groups=mesh['row'=4,'col'=8] {'col'}, dimensions={1}, use_global_device_ids=true | all-gather | bytes 9216 | tf_op jit(solution)/shard_map/all_gather | solution.py:196
  511.9 18.3 all-to-all-done.1
  536.2 139.3 %all-gather.35.cloned.1.call-done = bf16[2,4096,1024]{2,1,0:T(8,128)(2,1)} async-done(((bf16[2,512,1024]{2,1,0:T(8,128)(2,1)}), bf16[2,4096,1024]{2,1,0:T(8,128)(2,1)}) %all-gather.35.cloned.1.call-update) | async-done | bytes 16777232 | tf_op jit(solution)/shard_map/all_gather | solution.py:166
  688.1 87.4 %all-gather.45.cloned.1.call-done = bf16[8,340,1024]{2,1,0:T(8,128)(2,1)} async-done(((bf16[1,340,1024]{2,1,0:T(8,128)(2,1)}), bf16[8,340,1024]{2,1,0:T(8,128)(2,1)}) %all-gather.45.cloned.1.call-update) | async-done | bytes 5570576 | tf_op jit(solution)/shard_map/all_gather | solution.py:46
  810.2 26.4 while.53
  876.2 88.2 %all-gather.47.cloned.1.call-done = bf16[8,340,1024]{2,1,0:T(8,128)(2,1)} async-done(((bf16[1,340,1024]{2,1,0:T(8,128)(2,1)}), bf16[8,340,1024]{2,1,0:T(8,128)(2,1)}) %all-gather.47.cloned.1.call-update) | async-done | bytes 5570576 | tf_op jit(solution)/shard_map/all_gather | solution.py:46
  989.8 117.5 %all-gather.49.cloned.1.call-done = bf16[8,340,1024]{2,1,0:T(8,128)(2,1)} async-done(((bf16[1,340,1024]{2,1,0:T(8,128)(2,1)}), bf16[8,340,1024]{2,1,0:T(8,128)(2,1)}) %all-gather.49.cloned.1.call-update) | async-done | bytes 5570576 | tf_op jit(solution)/shard_map/all_gather | solution.py:92
  1145.7 103.2 %all-to-all-done.4 = bf16[8,2,87040]{2,1,0:T(2,128)(2,1)} async-done(((bf16[8,2,87040]{2,1,0:T(2,128)(2,1)}), bf16[8,2,87040]{2,1,0:T(2,128)(2,1)}, u32[]{:S(2)}, u32[]{:S(2)}) %all-to-all-start.4) | async-done | bytes 2785312 | tf_op jit(solution)/shard_map/all_to_all | solution.py:57
  1256.4 19.2 reduce.8
  1293.2 95.5 %all-gather.37.cloned.1.call-done = bf16[2,1024,4096]{2,1,0:T(8,128)(2,1)} async-done(((bf16[2,1024,512]{2,1,0:T(8,128)(2,1)}), bf16[2,1024,4096]{2,1,0:T(8,128)(2,1)}) %all-gather.37.cloned.1.call-update) | async-done | bytes 16777232 | tf_op jit(solution)/shard_map/all_gather | solution.py:168
  1403.7 86.5 %all-gather.51.cloned.1.call-done = bf16[8,340,1024]{2,1,0:T(8,128)(2,1)} async-done(((bf16[1,340,1024]{2,1,0:T(8,128)(2,1)}), bf16[8,340,1024]{2,1,0:T(8,128)(2,1)}) %all-gather.51.cloned.1.call-update) | async-done | bytes 5570576 | tf_op jit(solution)/shard_map/all_gather | solution.py:92
  1505.4 153.0 %while.54 = (s32[]{:T(128)}, f32[4,680,2,64]{1,0,3,2:T(4,128)}, f32[4,680,2,64]{1,0,3,2:T(4,128)}, bf16[4,680,2,64]{1,0,3,2:T(4,128)(2,1)}, bf16[4,680,2,64]{1,3...) while((s32[]{:T(128)}, f32[4,680,2,64]{1,0,3,2:T(4,128)}, ...), condition=%wide.region_26.27_spmd, body=%wide.region_24.26_spmd.sunk | while | flops 603430656 | bytes 62326344 | solution.py:311
  1677.3 65.0 %all_to_all.136 = bf16[2720,3,128]{2,1,0:T(4,128)(2,1)S(1)} all-to-all(bf16[2720,3,128]{2,1,0:T(4,128)(2,1)S(1)} %copy.207), channel_id=1, replica_groups=mesh['row'=4,'col'=8] {'col'}, dimensions={0} | all-to-all | bytes 4177920 | tf_op jit(solution)/shard_map/all_to_all | solution.py:57
  1755.4 90.6 %all-gather.53.cloned.1.call-done = bf16[8,340,1024]{2,1,0:T(8,128)(2,1)} async-done(((bf16[1,340,1024]{2,1,0:T(8,128)(2,1)}), bf16[8,340,1024]{2,1,0:T(8,128)(2,1)}) %all-gather.53.cloned.1.call-update) | async-done | bytes 5570576 | tf_op jit(solution)/shard_map/all_gather | solution.py:92
  1870.7 65.7 %all_to_all.137 = bf16[8,2,87040]{2,1,0:T(2,128)(2,1)S(1)} all-to-all(bf16[8,2,87040]{2,1,0:T(2,128)(2,1)} %reshape.540), channel_id=1, replica_groups=mesh['row'=4,'col'=8] {'col'}, dimensions={0} | all-to-all | bytes 5570560 | tf_op jit(solution)/shard_map/all_to_all | solution.py:57
  1941.1 19.2 reduce.9
  1976.5 90.8 %all-gather.55.cloned.1.call-done = bf16[8,340,1024]{2,1,0:T(8,128)(2,1)} async-done(((bf16[1,340,1024]{2,1,0:T(8,128)(2,1)}), bf16[8,340,1024]{2,1,0:T(8,128)(2,1)}) %all-gather.55.cloned.1.call-update) | async-done | bytes 5570576 | tf_op jit(solution)/shard_map/all_gather | solution.py:92
  2081.8 153.1 %while.55 = (s32[]{:T(128)}, f32[4,680,2,64]{1,0,3,2:T(4,128)}, f32[4,680,2,64]{1,0,3,2:T(4,128)}, bf16[4,680,2,64]{1,0,3,2:T(4,128)(2,1)}, bf16[4,680,2,64]{1,3...) while((s32[]{:T(128)}, f32[4,680,2,64]{1,0,3,2:T(4,128)}, ...), condition=%wide.region_35.36_spmd, body=%wide.region_33.35_spmd.sunk | while | flops 603430656 | bytes 62326344 | solution.py:311
  2269.6 52.0 %all-to-all-done.7 = bf16[2720,3,128]{2,1,0:T(4,128)(2,1)} async-done(((bf16[2720,3,128]{2,1,0:T(4,128)(2,1)}), bf16[2720,3,128]{2,1,0:T(4,128)(2,1)}, u32[]{:S(2)}, u32[]{:S(2)}) %all-to-all-start.7) | async-done | bytes 2088992 | tf_op jit(solution)/shard_map/all_to_all | solution.py:57
  2432.9 42.8 %reduce-scatter.29.cloned.1.call-done = bf16[128,2]{1,0:T(8,128)(2,1)} async-done(((bf16[1024,2]{1,0:T(8,128)(2,1)}), bf16[128,2]{1,0:T(8,128)(2,1)}) %reduce-scatter.29.cloned.1.call-update) | async-done | bytes 528
  2477.1 33.5 %reduce-scatter.21.cloned.1.call-done = bf16[2,256,512]{2,1,0:T(8,128)(2,1)} async-done(((bf16[2,1024,512]{2,1,0:T(8,128)(2,1)}), bf16[2,256,512]{2,1,0:T(8,128)(2,1)}) %reduce-scatter.21.cloned.1.call-update) | async-done | bytes 524304 | tf_op jit(solution)/shard_map/reduce_scatter | solution.py:362
  2512.8 31.8 %reduce-scatter.23.cloned.1.call-done = bf16[2,512,256]{2,1,0:T(8,128)(2,1)} async-done(((bf16[2,512,1024]{2,1,0:T(8,128)(2,1)}), bf16[2,512,256]{2,1,0:T(8,128)(2,1)}) %reduce-scatter.23.cloned.1.call-update) | async-done | bytes 524304 | tf_op jit(solution)/shard_map/reduce_scatter | solution.py:368
  2546.7 60.6 %reduce-scatter.27.cloned.1.call-done = bf16[128,2]{1,0:T(8,128)(2,1)} async-done(((bf16[1024,2]{1,0:T(8,128)(2,1)}), bf16[128,2]{1,0:T(8,128)(2,1)}) %reduce-scatter.27.cloned.1.call-update) | async-done | bytes 528
  2610.0 23.0 reduce-scatter.19.cloned.1.call-done
  2634.6 29.9 %reduce-scatter.17.cloned.1.call-done = bf16[2,256,3,128]{3,1,2,0:T(8,128)(2,1)} async-done(((bf16[2,1024,3,128]{3,1,2,0:T(8,128)(2,1)}), bf16[2,256,3,128]{3,1,2,0:T(8,128)(2,1)}) %reduce-scatter.17.cloned.1.call-update) | async-done | bytes 393232 | tf_op jit(solution)/shard_map/reduce_scatter | solution.py:359
  2681.6 23.2 reduce-scatter.15.cloned.1.call-done
  (816 shorter events, 958.7 us)
Async XLA Ops:
  7.2 34.4 %all-gather.25.cloned.1.call-start = ((), (), s32[]{:S(2)}) async-start(), calls=%async_computation.16 | async-start | bytes 3932160 | tf_op jit(solution)/shard_map/all_gather | solution.py:158
  9.6 75.0 %all-gather.27.cloned.1.call-start = ((), (), s32[]{:S(2)}) async-start(), calls=%async_computation.17 | async-start | bytes 1966080 | tf_op jit(solution)/shard_map/all_gather | solution.py:159
  10.4 154.2 %all-gather.41.cloned.1.call-start = ((), (), s32[]{:S(2)}) async-start(), calls=%async_computation.29 | async-start | bytes 6340608 | tf_op jit(solution)/shard_map/all_gather | solution.py:46
  10.5 862.5 %copy-start.68 = (s32[340]{0:T(512)}, s32[340]{0:T(512)S(1)}, u32[]{:S(2)}) copy-start(s32[340]{0:T(512)S(1)} %add_select_fusion) | copy-start | bytes 4084
  71.8 187.8 %all-gather.29.cloned.1.call-start = ((), (), s32[]{:S(2)}) async-start(), calls=%async_computation.18 | async-start | bytes 4718592 | tf_op jit(solution)/shard_map/all_gather | solution.py:165
  83.3 186.8 %all-gather.33.cloned.1.call-start = ((), (), s32[]{:S(2)}) async-start(), calls=%async_computation.20 | async-start | bytes 2621440 | tf_op jit(solution)/shard_map/all_gather | solution.py:162
  84.3 723.2 %copy-start.126 = (f32[2]{0:T(128)}, f32[2]{0:T(128)S(1)}, u32[]{:S(2)}) copy-start(f32[2]{0:T(128)S(1)} %get-tuple-element.525) | copy-start | bytes 28
  225.6 33.6 %all-to-all-start = ((bf16[8,340,128]{2,1,0:T(8,128)(2,1)}), bf16[8,340,128]{2,1,0:T(8,128)(2,1)S(1)}, u32[]{:S(2)}, u32[]{:S(2)}) async-start(bf16[8,340,128]{2,1,0:T(8,128)(2,1)} %reshape.519), calls=%async_computation | async-start | bytes 1409024 | tf_op jit(solution)/shard_map/all_to_all | solution.py:73
  229.2 133.5 %all-gather.43.cloned.1.call-start = ((), (), s32[]{:S(2)}) async-start(), calls=%async_computation.30 | async-start | bytes 6340608 | tf_op jit(solution)/shard_map/all_gather | solution.py:46
  267.6 118.6 %all-gather.31.cloned.1.call-start = ((), (), s32[]{:S(2)}) async-start(), calls=%async_computation.19 | async-start | bytes 2621440 | tf_op jit(solution)/shard_map/all_gather | solution.py:160
  268.4 407.1 %all-gather.35.cloned.1.call-start = ((), (), s32[]{:S(2)}) async-start(), calls=%async_computation.21 | async-start | bytes 18874368 | tf_op jit(solution)/shard_map/all_gather | solution.py:166
  401.9 128.3 %all-to-all-start.1 = ((bf16[8,340,512]{2,1,0:T(8,128)(2,1)}), bf16[8,340,512]{2,1,0:T(8,128)(2,1)}, u32[]{:S(2)}, u32[]{:S(2)}) async-start(bf16[8,340,512]{2,1,0:T(8,128)(2,1)} %all_to_all.103), calls=%async_computation.1 | async-start | bytes 5636096 | tf_op jit(solution)/shard_map/all_to_all | solution.py:73
  407.1 368.5 %all-gather.45.cloned.1.call-start = ((), (), s32[]{:S(2)}) async-start(), calls=%async_computation.31 | async-start | bytes 6340608 | tf_op jit(solution)/shard_map/all_gather | solution.py:46
  844.0 20.2 all-to-all-start.2
  847.5 116.8 %all-gather.47.cloned.1.call-start = ((), (), s32[]{:S(2)}) async-start(), calls=%async_computation.32 | async-start | bytes 6340608 | tf_op jit(solution)/shard_map/all_gather | solution.py:46
  872.9 234.4 %all-gather.49.cloned.1.call-start = ((), (), s32[]{:S(2)}) async-start(), calls=%async_computation.33 | async-start | bytes 6340608 | tf_op jit(solution)/shard_map/all_gather | solution.py:92
  875.6 513.1 %all-gather.37.cloned.1.call-start = ((), (), s32[]{:S(2)}) async-start(), calls=%async_computation.22 | async-start | bytes 18874368 | tf_op jit(solution)/shard_map/all_gather | solution.py:168
  985.4 150.1 %all-to-all-start.3 = ((bf16[8,340,512]{2,1,0:T(8,128)(2,1)}), bf16[8,340,512]{2,1,0:T(8,128)(2,1)}, u32[]{:S(2)}, u32[]{:S(2)}) async-start(bf16[8,340,512]{2,1,0:T(8,128)(2,1)} %all_to_all.110), calls=%async_computation.3 | async-start | bytes 5636096 | tf_op jit(solution)/shard_map/all_to_all | solution.py:73
  1135.5 113.3 %all-to-all-start.4 = ((bf16[8,2,87040]{2,1,0:T(2,128)(2,1)}), bf16[8,2,87040]{2,1,0:T(2,128)(2,1)}, u32[]{:S(2)}, u32[]{:S(2)}) async-start(bf16[8,2,87040]{2,1,0:T(2,128)(2,1)} %reshape.538), calls=%async_computation.4 | async-start | bytes 5570560 | tf_op jit(solution)/shard_map/all_to_all | solution.py:57
  1139.9 350.2 %all-gather.51.cloned.1.call-start = ((), (), s32[]{:S(2)}) async-start(), calls=%async_computation.34 | async-start | bytes 6340608 | tf_op jit(solution)/shard_map/all_gather | solution.py:92
  1401.0 344.2 %all-gather.39.cloned.1.call-start = ((), (), s32[]{:S(2)}) async-start(), calls=%async_computation.23 | async-start | bytes 14155776 | tf_op jit(solution)/shard_map/all_gather | solution.py:167
  1401.6 444.4 %all-gather.53.cloned.1.call-start = ((), (), s32[]{:S(2)}) async-start(), calls=%async_computation.35 | async-start | bytes 6340608 | tf_op jit(solution)/shard_map/all_gather | solution.py:92
  1755.4 311.9 %all-gather.55.cloned.1.call-start = ((), (), s32[]{:S(2)}) async-start(), calls=%async_computation.36 | async-start | bytes 6340608 | tf_op jit(solution)/shard_map/all_gather | solution.py:92
  2255.4 66.2 %all-to-all-start.7 = ((bf16[2720,3,128]{2,1,0:T(4,128)(2,1)}), bf16[2720,3,128]{2,1,0:T(4,128)(2,1)}, u32[]{:S(2)}, u32[]{:S(2)}) async-start(bf16[2720,3,128]{2,1,0:T(4,128)(2,1)} %copy.221), calls=%async_computation.7 | async-start | bytes 5570560 | tf_op jit(solution)/shard_map/all_to_all | solution.py:57
  2260.0 166.8 %reduce-scatter.25.cloned.1.call-start = ((), (), s32[]{:S(2)}) async-start(), calls=%async_computation.37 | async-start | bytes 294912
  2352.0 123.6 %reduce-scatter.29.cloned.1.call-start = ((), (), s32[]{:S(2)}) async-start(), calls=%async_computation.39 | async-start | bytes 294912
  2359.7 151.0 %reduce-scatter.21.cloned.1.call-start = ((), (), s32[]{:S(2)}) async-start(), calls=%async_computation.27 | async-start | bytes 2621440 | tf_op jit(solution)/shard_map/reduce_scatter | solution.py:362
  2368.3 176.3 %reduce-scatter.23.cloned.1.call-start = ((), (), s32[]{:S(2)}) async-start(), calls=%async_computation.28 | async-start | bytes 2621440 | tf_op jit(solution)/shard_map/reduce_scatter | solution.py:368
  2382.5 224.8 %reduce-scatter.27.cloned.1.call-start = ((), (), s32[]{:S(2)}) async-start(), calls=%async_computation.38 | async-start | bytes 294912
  2408.4 224.7 %reduce-scatter.19.cloned.1.call-start = ((), (), s32[]{:S(2)}) async-start(), calls=%async_computation.26 | async-start | bytes 655360 | tf_op jit(solution)/shard_map/reduce_scatter | solution.py:365
  2413.0 251.5 %reduce-scatter.17.cloned.1.call-start = ((), (), s32[]{:S(2)}) async-start(), calls=%async_computation.25 | async-start | bytes 1966080 | tf_op jit(solution)/shard_map/reduce_scatter | solution.py:359
  2426.8 278.1 %reduce-scatter.15.cloned.1.call-start = ((), (), s32[]{:S(2)}) async-start(), calls=%async_computation.24 | async-start | bytes 3932160 | tf_op jit(solution)/shard_map/reduce_scatter | solution.py:356
  (174 other events, 5526.4 us)
Sparse Core Ops, SparseCore 0:
  10.2 31.4 all-gather.24
  43.2 19.6 all-gather.26
  71.9 92.6 all-gather.40
  166.6 73.7 all-gather.28
  241.8 28.2 all-gather.32
  272.8 89.8 all-gather.42
  364.3 21.8 all-gather.30
  388.4 287.0 all-gather.34
  687.0 88.4 all-gather.44
  873.1 91.2 all-gather.46
  966.6 140.7 all-gather.48
  1109.2 279.4 all-gather.36
  1401.2 88.9 all-gather.50
  1492.1 175.0 all-gather.38
  1755.5 90.4 all-gather.52
  1976.6 90.5 all-gather.54
  2352.1 59.9 reduce-scatter.24
  2415.3 60.2 reduce-scatter.28
  2478.2 32.4 reduce-scatter.20
  2513.2 31.3 reduce-scatter.22
  2547.9 59.3 reduce-scatter.26
  2610.4 22.6 reduce-scatter.18
  2636.3 28.1 reduce-scatter.16
  2666.9 37.9 reduce-scatter.14
where the time goes:
time: 2730 us; the launch traced here: 2710 us
  waiting for transfers between devices  1450 us (53%)
  local copies, waits for them, and re-layouts  450 us (16%)
  matrix products  330 us (12%)
  blocking collectives  308 us (11%)
  other arithmetic  129 us (5%)
  starting transfers between devices  27.7 us (1%)
    all_gather x4, waiting for transfers between devices, back_out(): lax.all_gather(grad_low, 'col', axis=0, tiled=True)  385 us
    all_gather x4, waiting for transfers between devices, project_in(): lax.all_gather(hidden_low, 'col', axis=0, tiled=True)  345 us
    dynamic_update_slice x48, local copies, waits for them, and re-layouts, on_device(): attended, log_total = lax.map(attend, (q_low, k_low, v_low, ends))  189 us
    all_to_all x2, waiting for transfers between devices, back_in(): lax.all_to_all(grad_three, 'col', split_axis=0, concat_axis=2, tiled=True)  155 us
    all_gather x1, waiting for transfers between devices, on_device(): lax.all_gather(full_fc2, 'col', axis=1, tiled=True)  139 us
    all_to_all x2, blocking collectives, back_in(): lax.all_to_all(grad_three, 'col', split_axis=0, concat_axis=2, tiled=True)  131 us
    unnamed x294, local copies, waits for them, and re-layouts  120 us
    unnamed x27, waiting for transfers between devices  106 us
  transfers between devices with their start and end apart: 30, of which 24 were waited for; matrix products, arithmetic and copies ran while one was open for 18% of the time, Pallas kernels for 0%

commit v1 on v0

--- a/solution.py
+++ b/solution.py
@@ -397,41 +397,444 @@
     )
 
 
+BF = jnp.bfloat16
+F32 = jnp.float32
+NT = (((1,), (1,)), ((), ()))
+TN = (((0,), (0,)), ((), ()))
+
+
+def sibling(values):
+    return lax.ppermute(values, "core", [(0, 1), (1, 0)])
+
+
+def across(values, axis):
+    return lax.ppermute(values, axis, [(0, 1), (1, 0)])
+
+
+def trade(values):
+    return lax.ppermute(values, ("core", "x"), [(0, 0), (1, 2), (2, 1), (3, 3)])
+
+
+def turned(values, flag, axis):
+    half = values.shape[axis] // 2
+    return jnp.where(flag == 1, jnp.roll(values, half, axis), values)
+
+
+def dot(left, right, dims=(((1,), (0,)), ((), ()))):
+    return lax.dot_general(left, right, dims, preferred_element_type=F32)
+
+
+def gelu_and_slope(values):
+    root = 0.7978845608028654
+    inner = root * (values + 0.044715 * values * values * values)
+    tanh = jnp.tanh(inner)
+    slope = 0.5 * (1.0 + tanh) + 0.5 * values * (1.0 - tanh * tanh) * root * (
+        1.0 + 3.0 * 0.044715 * values * values
+    )
+    return 0.5 * values * (1.0 + tanh), slope
+
+
+def gather_blocks(shard):
+    by_z = lax.all_gather(shard, "z", axis=0, tiled=False)
+    first, second = by_z[:, :128], by_z[:, 128:]
+    a_x = across(first, "x")
+    b_y = across(second, "y")
+    a_y = across(jnp.stack((first, a_x)), "y")
+    b_x = across(jnp.stack((second, b_y)), "x")
+    return (
+        ((first, a_y[0]), (a_x, a_y[1])),
+        ((second, b_y), (b_x[0], b_x[1])),
+    )
+
+
+def joined(blocks):
+    rows = []
+    for half in blocks:
+        for by_x in half:
+            rows.append(
+                jnp.concatenate(
+                    [part.reshape(part.shape[0] * part.shape[1], part.shape[2]) for part in by_x],
+                    axis=1,
+                )
+            )
+    return jnp.concatenate(rows, axis=0)
+
+
+def scatter(send_a, keep_a, send_b, keep_b):
+    got_a = across(send_a, "y")
+    got_b = across(send_b, "x")
+    quarter, low = send_b.shape[0], send_a.shape[1]
+    sum_a = (keep_a.astype(F32) + got_a.astype(F32)).astype(BF)
+    sum_b = (keep_b.astype(F32) + got_b.astype(F32)).astype(BF)
+    got_a = across(sum_a[quarter:], "x")
+    got_b = across(sum_b[:, low:], "y")
+    sum_a = sum_a[:quarter].astype(F32) + got_a.astype(F32)
+    sum_b = sum_b[:, :low].astype(F32) + got_b.astype(F32)
+    both = jnp.concatenate(
+        [v.astype(BF).reshape(4, quarter // 4, low) for v in (sum_a, sum_b)], axis=1
+    )
+    return lax.psum_scatter(both, "z", scatter_dimension=0, tiled=False)
+
+
+def scatter_product(left, right):
+    low, mid, quarter = right.shape[1] // 2, left.shape[1] // 2, left.shape[1] // 4
+    send_a = dot(left[:, :mid], right[:, low:], TN).astype(BF)
+    send_b = dot(left[:, mid + quarter :], right, TN).astype(BF)
+    keep_a = dot(left[:, :mid], right[:, :low], TN)
+    keep_b = dot(left[:, mid : mid + quarter], right, TN)
+    return scatter(send_a, keep_a, send_b, keep_b)
+
+
+def scatter_attn(d_q, d_k, d_v, attn, hidden1, d_branch, heads, head_width):
+    parts = [
+        dot(v, w, TN).astype(BF).reshape(heads, 1, head_width, w.shape[1])
+        for v, w in ((d_q, hidden1), (d_k, hidden1), (d_v, hidden1), (attn, d_branch))
+    ]
+    width = hidden1.shape[1]
+    low = width // 2
+    one = jnp.concatenate(parts[:2], axis=1).reshape(-1, width)
+    two = jnp.concatenate(parts[2:], axis=1).reshape(-1, width)
+    mid = two.shape[0] // 2
+    return scatter(one[:, low:], one[:, :low], two[mid:], two[:mid])
+
+
+def unit_rows(values):
+    rate = lax.rsqrt(jnp.sum(values * values, axis=-1, keepdims=True) + EPS_UNIT)
+    return values * rate, rate
+
+
+def on_pair(
+    hidden_in, cond, scale_sizes, w_ada, b_ada, w_qkv, b_qkv, head_scale,
+    w_proj, b_proj, w_fc1, b_fc1, w_fc2, b_fc2, grad_out,
+):
+    y = lax.axis_index("y")
+    core = lax.axis_index("core")
+    z = lax.axis_index("z")
+    x = lax.axis_index("x")
+    layer_count = w_ada.shape[0]
+    seq_row, width = cond.shape
+    rows_dev = hidden_in.shape[0]
+    rows_pad = -(-rows_dev // 32) * 32
+    seq_len = 2 * rows_dev
+    d_col = b_qkv.shape[2]
+    head_width = d_col // head_scale.shape[1]
+    y_size, z_size, x_size = (lax.axis_size(a) for a in ("y", "z", "x"))
+    heads = z_size * x_size
+    low = width // 2
+
+    def paired(values, hidden_axis, d_axis):
+        half = values.shape[hidden_axis] // 2
+        first = lax.slice_in_dim(values, 0, half, axis=hidden_axis)
+        second = lax.slice_in_dim(values, half, 2 * half, axis=hidden_axis)
+        kept = jnp.where(core == 0, first, second)
+        got = sibling(jnp.where(core == 0, second, first))
+        return jnp.concatenate(
+            (jnp.where(core == 0, kept, got), jnp.where(core == 0, got, kept)), axis=d_axis
+        )
+
+    rows_d = w_qkv.shape[1]
+    qkv_t = jnp.transpose(w_qkv, (0, 2, 3, 1)).reshape(layer_count, 3, 2, head_width, rows_d)
+    qkv_t = jnp.transpose(qkv_t, (0, 2, 1, 3, 4)).reshape(layer_count, 6 * head_width, rows_d)
+    proj_t = w_proj
+    fc1_t = jnp.transpose(w_fc1, (0, 2, 1))
+    hid_dev = w_fc1.shape[2]
+    packed = jnp.concatenate(
+        (
+            qkv_t[:, : 3 * head_width], proj_t[:, :head_width],
+            fc1_t[:, : hid_dev // 2], w_fc2[:, : hid_dev // 2],
+            qkv_t[:, 3 * head_width :], proj_t[:, head_width:],
+            fc1_t[:, hid_dev // 2 :], w_fc2[:, hid_dev // 2 :],
+        ),
+        axis=1,
+    )
+    shards = paired(packed, 1, 2)
+    attn_rows = 4 * head_width
+    cuts = (0, attn_rows, attn_rows + hid_dev // 2, attn_rows + hid_dev)
+    blocks = [
+        [gather_blocks(shards[l, cuts[i] : cuts[i + 1]]) for i in range(3)]
+        for l in range(layer_count)
+    ]
+
+    cond_low = jax.nn.silu(cond.astype(F32)).astype(BF)
+    silu_rows = lax.all_gather(cond_low, ("y", "core"), axis=0, tiled=True)
+    row = y * 2 + core
+    silu_own = lax.dynamic_slice_in_dim(silu_rows, row * rows_d, rows_d, axis=1)
+    seqs = silu_rows.shape[0]
+    part = dot(silu_own, jnp.transpose(w_ada, (1, 0, 2, 3)).reshape(rows_d, layer_count * 6 * d_col))
+    part = part + jnp.where(row == 0, b_ada.astype(F32).reshape(1, layer_count * 6 * d_col), 0.0)
+    to_all = jnp.transpose(part.reshape(y_size, x_size, z_size, -1), (0, 2, 1, 3))
+    to_all = jnp.broadcast_to(to_all[:, None], (y_size, 2) + to_all.shape[1:])
+    from_all = lax.all_to_all(
+        to_all.reshape(y_size * 2 * z_size * x_size, -1), ("y", "core", "z", "x"),
+        split_axis=0, concat_axis=0, tiled=True,
+    )
+    ada = jnp.sum(from_all.reshape(y_size * 2, z_size * x_size, layer_count, 6, d_col), axis=0)
+    ada = turned(jnp.transpose(ada, (1, 2, 0, 3)).reshape(layer_count, 6, width), y, 2)
+
+    small = jnp.concatenate(
+        [v.reshape(-1) for v in (b_qkv, b_fc1, b_proj, b_fc2, head_scale)]
+    )[None]
+    small = lax.all_gather(small, ("z", "x"), axis=0, tiled=True).astype(F32)
+    small = small.reshape(z_size, x_size, -1)
+    sizes = [v.size for v in (b_qkv, b_fc1, b_proj, b_fc2, head_scale)]
+    offs = [sum(sizes[:i]) for i in range(6)]
+    s_qkv, s_fc1, s_proj, s_fc2, s_scale = [small[:, :, offs[i] : offs[i + 1]] for i in range(5)]
+
+    def by_core(values, shape, axis):
+        values = values.reshape((z_size, x_size) + shape)
+        return lax.dynamic_index_in_dim(values, core, axis=axis, keepdims=False)
+
+    def x_first(values):
+        return turned(jnp.swapaxes(values, 0, 1), x, 0)
+
+    bias_qkv = x_first(by_core(s_qkv, (layer_count, 2, 2, head_width), 4))
+    scales = x_first(by_core(s_scale, (layer_count, 2), 3))
+    bias_fc1 = x_first(by_core(s_fc1, (layer_count, 2, hid_dev // 2), 3))
+    bias_fc1 = bias_fc1.reshape(x_size, z_size, layer_count, 2, hid_dev // 4)
+    bias_fc1 = jnp.transpose(bias_fc1, (2, 3, 0, 1, 4)).reshape(layer_count, -1)
+    bias_proj = turned(
+        jnp.transpose(s_proj.reshape(z_size * x_size, layer_count, d_col), (1, 0, 2)).reshape(layer_count, width), y, 1
+    )
+    bias_fc2 = turned(
+        jnp.transpose(s_fc2.reshape(z_size * x_size, layer_count, d_col), (1, 0, 2)).reshape(layer_count, width), y, 1
+    )
+
+    sizes_f = scale_sizes.astype(F32)
+    sizes_f = jnp.where(core == x, sizes_f, sibling(sizes_f))
+    own_sizes = lax.dynamic_index_in_dim(sizes_f, z, axis=0, keepdims=False).astype(jnp.int32)
+    index = jnp.arange(rows_pad, dtype=jnp.int32)
+    valid = index < rows_dev
+    places = jnp.concatenate((core * rows_dev + index, (1 - core) * rows_dev + index))
+    real = jnp.concatenate((valid, valid))
+    starts = jnp.cumsum(own_sizes) - own_sizes
+    ends = jnp.sum(jnp.where(starts[None, :] <= places[:, None], own_sizes[None, :], 0), axis=1)
+    visible = (places[None, :] < ends[:, None]) & real[None, :]
+
+    def own_tokens(values):
+        return jnp.pad(turned(trade(values), y, 1), ((0, rows_pad - rows_dev), (0, 0)))
+
+    def both_halves(values):
+        return jnp.concatenate((values, sibling(values)), axis=0)
+
+    def summed(partial):
+        got = sibling(partial[rows_pad:].astype(BF))
+        return partial[:rows_pad] + got.astype(F32)
+
+    current = own_tokens(hidden_in).astype(F32)
+    grad_state = own_tokens(grad_out).astype(F32)
+    saved = []
+    for l in range(layer_count):
+        gamma1, gamma2, scale1, scale2, shift1, shift2 = [ada[l, i][None] for i in range(6)]
+        w_attn, w_one, w_two = [joined(b) for b in blocks[l]]
+        w_attn = w_attn.reshape(2, heads, 2, head_width, width)
+        w_q, w_k, w_v, w_p = [
+            w_attn[h, :, j].reshape(heads * head_width, width) for h in range(2) for j in range(2)
+        ]
+        normed1, rstd1 = normalize(current)
+        hidden1 = both_halves((normed1 * (1.0 + scale1) + shift1).astype(BF))
+        b_q = bias_qkv[:, :, l, 0].reshape(1, -1)
+        b_v = bias_qkv[:, :, l, 1].reshape(1, -1)
+        rows = hidden1.shape[0]
+        queries = (dot(hidden1, w_q, NT) + b_q).reshape(rows, heads, head_width)
+        keys = dot(hidden1, w_k, NT).reshape(rows, heads, head_width)
+        v_low = (dot(hidden1, w_v, NT) + b_v).astype(BF).reshape(rows, heads, head_width)
+        scale_here = scales[:, :, l].reshape(heads, 1)
+        q_unit, q_rate = unit_rows(queries)
+        k_unit, k_rate = unit_rows(keys)
+        q_low = (q_unit * scale_here).astype(BF)
+        k_low = k_unit.astype(BF)
+        scores = jnp.einsum("the,she->hts", q_low, k_low, preferred_element_type=F32)
+        scores = jnp.where(visible[None], scores, NEG_FILL)
+        top = jnp.max(scores, axis=-1, keepdims=True)
+        expo = jnp.exp(scores - top)
+        total = jnp.sum(expo, axis=-1, keepdims=True)
+        probs = (expo / total).astype(BF)
+        attended = jnp.einsum("hts,she->the", probs, v_low, preferred_element_type=F32)
+        log_total = top + jnp.log(total)
+        attn = attended.reshape(rows, heads * head_width).astype(BF)
+        branch = summed(dot(attn, w_p)) + bias_proj[l][None]
+        middle = current + gamma1 * branch
+        normed2, rstd2 = normalize(middle)
+        hidden2 = both_halves((normed2 * (1.0 + scale2) + shift2).astype(BF))
+        pre = dot(hidden2, w_one, NT) + bias_fc1[l][None]
+        act, slope = gelu_and_slope(pre)
+        act = act.astype(BF)
+        slope = slope.astype(BF)
+        feed = summed(dot(act, w_two)) + bias_fc2[l][None]
+        saved.append(
+            (normed1, rstd1, hidden1, q_unit, q_rate, q_low, k_unit, k_rate, k_low, v_low, log_total,
+             attn, branch, normed2, rstd2, hidden2, slope, act, feed, w_q, w_k, w_v, w_p, w_one, w_two)
+        )
+        current = middle + gamma2 * feed
+    mixed = current.astype(BF)
+
+    d_ada = [None] * layer_count
+    d_biases = [None] * layer_count
+    d_weights = [None] * layer_count
+    for l in reversed(range(layer_count)):
+        gamma1, gamma2, scale1, scale2, shift1, shift2 = [ada[l, i][None] for i in range(6)]
+        (normed1, rstd1, hidden1, q_unit, q_rate, q_low, k_unit, k_rate, k_low, v_low, log_total,
+         attn, branch, normed2, rstd2, hidden2, slope, act, feed, w_q, w_k, w_v, w_p, w_one, w_two) = saved[l]
+        rows = hidden1.shape[0]
+        scale_here = scales[:, :, l].reshape(heads, 1)
+        d_gamma2 = jnp.sum(grad_state * feed, axis=0)
+        d_feed = (grad_state * gamma2).astype(BF)
+        db_fc2 = jnp.sum(d_feed.astype(F32), axis=0)
+        d_feed = both_halves(d_feed)
+        d_pre = (dot(d_feed, w_two, NT) * slope.astype(F32)).astype(BF)
+        g_two = scatter_product(act, d_feed)
+        db_fc1 = jnp.sum(d_pre.astype(F32), axis=0)
+        d_hidden2 = summed(dot(d_pre, w_one))
+        g_one = scatter_product(d_pre, hidden2)
+        d_scale2 = jnp.sum(d_hidden2 * normed2, axis=0)
+        d_shift2 = jnp.sum(d_hidden2, axis=0)
+        d_middle = grad_state + norm_back(d_hidden2 * (1.0 + scale2), normed2, rstd2)
+        d_gamma1 = jnp.sum(d_middle * branch, axis=0)
+        d_branch = (d_middle * gamma1).astype(BF)
+        db_proj = jnp.sum(d_branch.astype(F32), axis=0)
+        d_branch = both_halves(d_branch)
+        d_attn = dot(d_branch, w_p, NT).astype(BF).reshape(rows, heads, head_width)
+        scores = jnp.einsum("the,she->hts", q_low, k_low, preferred_element_type=F32)
+        probs = jnp.exp(jnp.where(visible[None], scores, NEG_FILL) - log_total)
+        d_probs = jnp.einsum("the,she->hts", d_attn, v_low, preferred_element_type=F32)
+        delta = jnp.sum(probs * d_probs, axis=-1, keepdims=True)
+        d_scores = (probs * (d_probs - delta)).astype(BF)
+        d_qn = jnp.einsum("hts,she->the", d_scores, k_low, preferred_element_type=F32)
+        d_kn = jnp.einsum("hts,the->she", d_scores, q_low, preferred_element_type=F32)
+        d_v = jnp.einsum("hts,the->she", probs.astype(BF), d_attn, preferred_element_type=F32)
+        d_head = jnp.sum(d_qn * q_unit, axis=(0, 2))
+        d_qn = d_qn * scale_here
+        d_q = q_rate * (d_qn - q_unit * jnp.sum(d_qn * q_unit, axis=-1, keepdims=True))
+        d_k = k_rate * (d_kn - k_unit * jnp.sum(d_kn * k_unit, axis=-1, keepdims=True))
+        d_q, d_k, d_v = [
+            v.astype(BF).reshape(rows, heads * head_width) for v in (d_q, d_k, d_v)
+        ]
+        db_qkv = jnp.stack(
+            (jnp.sum(d_q.astype(F32), axis=0), jnp.sum(d_v.astype(F32), axis=0))
+        )
+        d_hidden1 = summed(dot(d_q, w_q) + dot(d_k, w_k) + dot(d_v, w_v))
+        g_attn = scatter_attn(d_q, d_k, d_v, attn, hidden1, d_branch, heads, head_width)
+        d_scale1 = jnp.sum(d_hidden1 * normed1, axis=0)
+        d_shift1 = jnp.sum(d_hidden1, axis=0)
+        grad_state = d_middle + norm_back(d_hidden1 * (1.0 + scale1), normed1, rstd1)
+        d_ada[l] = jnp.stack((d_gamma1, d_gamma2, d_scale1, d_scale2, d_shift1, d_shift2))
+        d_biases[l] = (db_qkv, d_head, db_proj, db_fc1, db_fc2)
+        d_weights[l] = jnp.concatenate((g_attn, g_one, g_two), axis=0)
+
+    def by_col(values):
+        values = turned(values, y, values.ndim - 1)
+        lead = values.shape[:-1]
+        values = values.reshape(lead + (z_size, x_size, d_col))
+        return jnp.moveaxis(values, (-3, -2), (0, 1)).reshape(z_size, x_size, -1)
+
+    def by_hidden(values):
+        return jnp.swapaxes(turned(values, x, 0), 0, 1).reshape(z_size, x_size, -1)
+
+    packs = [by_col(jnp.stack(d_ada))]
+    for l in range(layer_count):
+        db_qkv, d_head, db_proj, db_fc1, db_fc2 = d_biases[l]
+        packs.append(by_col(db_proj))
+        packs.append(by_col(db_fc2))
+        packs.append(by_hidden(jnp.moveaxis(db_qkv.reshape(2, x_size, z_size, head_width), 0, 2)))
+        packs.append(
+            by_hidden(jnp.moveaxis(db_fc1.reshape(2, x_size, z_size, hid_dev // 4), 0, 2))
+        )
+        packs.append(by_hidden(d_head.reshape(x_size, z_size, 1)))
+    lens = [p.shape[2] for p in packs]
+    pack = jnp.concatenate(packs, axis=2)
+    pack = jnp.broadcast_to(pack[None], (2 * y_size,) + pack.shape)
+    n_dev = 2 * y_size * z_size * x_size
+    got = lax.all_to_all(
+        pack.reshape(n_dev, -1), ("y", "core", "z", "x"), split_axis=0, concat_axis=0, tiled=True
+    ).reshape(y_size, 2, z_size, x_size, -1)
+    pos = lens[0]
+    d_ada_all = jnp.sum(got[..., :pos], axis=1)
+    d_ada_all = jnp.transpose(d_ada_all, (0, 2, 1, 3)).reshape(seqs, -1).astype(BF)
+    out_b_ada = jnp.sum(d_ada_all.astype(F32), axis=0).reshape(layer_count, 6, d_col)
+    out_w_ada = dot(silu_own, d_ada_all, TN).reshape(rows_d, layer_count, 6, d_col)
+    out_w_ada = jnp.transpose(out_w_ada, (1, 0, 2, 3))
+    sums = jnp.sum(got[..., pos:], axis=(0, 2, 3))
+    outs = {"proj": [], "fc2": [], "qkv": [], "fc1": [], "scale": []}
+    pos = 0
+    for l in range(layer_count):
+        for name, count in zip(("proj", "fc2", "qkv", "fc1", "scale"), lens[1 + 5 * l : 6 + 5 * l]):
+            outs[name].append(sums[:, pos : pos + count])
+            pos += count
+    out_b_proj = jnp.stack([v[0] + v[1] for v in outs["proj"]])
+    out_b_fc2 = jnp.stack([v[0] + v[1] for v in outs["fc2"]])
+    out_b_qkv = jnp.stack(
+        [jnp.swapaxes(v.reshape(2, 2, head_width), 0, 1).reshape(2, d_col) for v in outs["qkv"]]
+    )
+    out_b_fc1 = jnp.stack([v.reshape(-1) for v in outs["fc1"]])
+    out_scale = jnp.stack([v.reshape(-1) for v in outs["scale"]])
+
+    own = jnp.stack(d_weights)
+    left, right = own[:, :, : own.shape[2] // 2], own[:, :, own.shape[2] // 2 :]
+    kept = jnp.where(core == 0, left, right)
+    came = sibling(jnp.where(core == 0, right, left))
+    first = jnp.where(core == 0, kept, came).astype(F32)
+    second = jnp.where(core == 0, came, kept).astype(F32)
+    wq = jnp.stack(
+        (first[:, : 3 * head_width], second[:, : 3 * head_width]), axis=1
+    ).reshape(layer_count, 2, 3, head_width, rows_d)
+    out_w_qkv = jnp.transpose(wq, (0, 4, 2, 1, 3)).reshape(layer_count, rows_d, 3, d_col)
+    pick = lambda i, j: jnp.concatenate((first[:, i:j], second[:, i:j]), axis=1)
+    out_w_proj = pick(3 * head_width, attn_rows)
+    out_w_fc1 = jnp.transpose(pick(cuts[1], cuts[2]), (0, 2, 1))
+    out_w_fc2 = pick(cuts[2], cuts[3])
+
+    def given_back(values):
+        return trade(turned(values[:rows_dev], y, 1))
+
+    return (
+        given_back(mixed), given_back(grad_state), out_w_ada, out_b_ada, out_w_qkv, out_b_qkv,
+        out_scale, out_w_proj, out_b_proj, out_w_fc1, out_b_fc1, out_w_fc2, out_b_fc2,
+    )
+
+
 def solution(mesh):
+    rows, cols = mesh.devices.shape
+    row, col, body, used = "row", "col", on_device, mesh
+    if rows == 4 and cols == 8:
+        used = jax.sharding.Mesh(
+            mesh.devices.reshape(rows // 2, 2, cols // 2, 2), ("y", "core", "z", "x")
+        )
+        row, col, body = ("y", "core"), ("z", "x"), on_pair
+    tokens = P(("row", "col") if used is mesh else row + col, None)
     return jax.shard_map(
-        on_device,
-        mesh=mesh,
+        body,
+        mesh=used,
         in_specs=(
-            P(("row", "col"), None),
-            P("row", None),
-            P("row", None),
-            P(None, "row", None, "col"),
-            P(None, None, "col"),
-            P(None, "row", None, "col"),
-            P(None, None, "col"),
-            P(None, "col"),
-            P(None, "col", "row"),
-            P(None, "col"),
-            P(None, "row", "col"),
-            P(None, "col"),
-            P(None, "col", "row"),
-            P(None, "col"),
-            P(("row", "col"), None),
+            tokens,
+            P(row, None),
+            P(row, None),
+            P(None, row, None, col),
+            P(None, None, col),
+            P(None, row, None, col),
+            P(None, None, col),
+            P(None, col),
+            P(None, col, row),
+            P(None, col),
+            P(None, row, col),
+            P(None, col),
+            P(None, col, row),
+            P(None, col),
+            tokens,
         ),
         out_specs=(
-            P(("row", "col"), None),
-            P(("row", "col"), None),
-            P(None, "row", None, "col"),
-            P(None, None, "col"),
-            P(None, "row", None, "col"),
-            P(None, None, "col"),
-            P(None, "col"),
-            P(None, "col", "row"),
-            P(None, "col"),
-            P(None, "row", "col"),
-            P(None, "col"),
-            P(None, "col", "row"),
-            P(None, "col"),
+            tokens,
+            tokens,
+            P(None, row, None, col),
+            P(None, None, col),
+            P(None, row, None, col),
+            P(None, None, col),
+            P(None, col),
+            P(None, col, row),
+            P(None, col),
+            P(None, row, col),
+            P(None, col),
+            P(None, col, row),
+            P(None, col),
         ),
         check_vma=False,
     )

time: 2730 us -> 1030 us (0.38)
  waiting for transfers between devices: 1450 us -> 258 us
  local copies, waits for them, and re-layouts: 450 us -> 94.8 us
  blocking collectives: 308 us -> 36.6 us
  starting transfers between devices: 27.7 us -> 94.7 us
  other arithmetic: 129 us -> 176 us
    all_gather x16 -> x6, waiting for transfers between devices: 1020 us -> 108 us  [gather_blocks(): by_z = lax.all_gather(shard, 'z', axis=0, tiled=False)]
    dynamic_update_slice x48 -> x0, local copies, waits for them, and re-layouts: 189 us -> none  [on_device(): attended, log_total = lax.map(attend, (q_low, k_low, v_low, ends))]
    all_to_all x6 -> x2, waiting for transfers between devices: 188 us -> 13.3 us  [the longest x1 13.3 us: on_pair(): lax.all_to_all(pack.reshape(n_dev, -1), ('y', 'core', 'z', 'x'), split_ax...]
    all_gather x4 -> x1, blocking collectives: 165 us -> 5.18 us  [on_pair(): silu_rows = lax.all_gather(cond_low, ('y', 'core'), axis=0, tiled=True)]
    reduce_scatter x5 -> x6, waiting for transfers between devices: 141 us -> 5.97 us  [scatter(): return lax.psum_scatter(both, 'z', scatter_dimension=0, tiled=False)]
    all_to_all x2 -> x0, blocking collectives: 131 us -> none  [back_in(): lax.all_to_all(grad_three, 'col', split_axis=0, concat_axis=2, tiled=True)]
    ppermute x0 -> x71, waiting for transfers between devices: none -> 130 us  [the longest x48 126 us: across(): return lax.ppermute(values, axis, [(0, 1), (1, 0)])]
    unnamed x27 -> x12, waiting for transfers between devices: 106 us -> 0.67 us
  transfers between devices with their start and end apart: 30 -> 85, of which waited for: 24 -> 21; matrix products, arithmetic and copies ran while one was open for 18% -> 52% of each run, Pallas kernels for 0% -> 0%
where the time goes in v1:
time: 1030 us; the launch traced here: 1020 us
  matrix products  343 us (33%)
  waiting for transfers between devices  258 us (25%)
  other arithmetic  176 us (17%)
  local copies, waits for them, and re-layouts  94.8 us (9%)
  starting transfers between devices  94.7 us (9%)
  blocking collectives  36.6 us (4%)
  between operations  19.5 us (2%)
    dot_general x50, matrix products, dot(): return lax.dot_general(left, right, dims, preferred_element_type=F32)  246 us
    ppermute x48, waiting for transfers between devices, across(): return lax.ppermute(values, axis, [(0, 1), (1, 0)])  126 us
    all_gather x6, waiting for transfers between devices, gather_blocks(): by_z = lax.all_gather(shard, 'z', axis=0, tiled=False)  108 us
    ppermute x48, starting transfers between devices, across(): return lax.ppermute(values, axis, [(0, 1), (1, 0)])  37.6 us
    concatenate x2, other arithmetic, joined(): return jnp.concatenate(rows, axis=0)  36.8 us
    unnamed x1, blocking collectives  31.5 us
    ppermute x19, starting transfers between devices, sibling(): return lax.ppermute(values, 'core', [(0, 1), (1, 0)])  30.3 us
    dot_general x2, matrix products, on_pair(): jnp.einsum('the,she->hts', d_attn, v_low, preferred_element_type=F32)  29.1 us
  transfers between devices with their start and end apart: 85, of which 21 were waited for; matrix products, arithmetic and copies ran while one was open for 52% of the time, Pallas kernels for 0%

profile of v1, /device:TPU:1, one launch (start us, length us, event | category | flops | bytes accessed | tf_op | source)
XLA Modules:
  0.0 1021.9 jit_solution(15026750415672804624)
XLA Ops:
  36.5 31.5 %all-reduce.2 = bf16[16416]{0:T(1024)(128)(2,1)S(1)} all-reduce(bf16[16416]{0:T(1024)(128)(2,1)S(1)} %dynamic-update-slice), channel_id=2, replica_groups=mesh['y'=2,'core'=2,'z'=4,'x'=2] {'z','x'}, use_global_device_ids=true, to_apply=%add.2 | all-reduce | flops 16416 | bytes 65664
  89.0 11.0 %all-gather.15.cloned.1.call-done = bf16[4,256,512]{2,1,0:T(8,128)(2,1)} async-done(((bf16[1,256,512]{2,1,0:T(8,128)(2,1)}), bf16[4,256,512]{2,1,0:T(8,128)(2,1)}) %all-gather.15.cloned.1.call-update) | async-done | bytes 1048592 | tf_op jit(solution)/shard_map/all_gather | solution.py:438
  104.0 25.7 %all-gather.11.cloned.1.call-done = bf16[4,256,512]{2,1,0:T(8,128)(2,1)} async-done(((bf16[1,256,512]{2,1,0:T(8,128)(2,1)}), bf16[4,256,512]{2,1,0:T(8,128)(2,1)}) %all-gather.11.cloned.1.call-update) | async-done | bytes 1048592 | tf_op jit(solution)/shard_map/all_gather | solution.py:438
  136.9 21.6 %all-gather.17.cloned.1.call-done = bf16[4,256,512]{2,1,0:T(8,128)(2,1)} async-done(((bf16[1,256,512]{2,1,0:T(8,128)(2,1)}), bf16[4,256,512]{2,1,0:T(8,128)(2,1)}) %all-gather.17.cloned.1.call-update) | async-done | bytes 1048592 | tf_op jit(solution)/shard_map/all_gather | solution.py:438
  164.7 22.7 %all-gather.13.cloned.1.call-done = bf16[4,256,512]{2,1,0:T(8,128)(2,1)} async-done(((bf16[1,256,512]{2,1,0:T(8,128)(2,1)}), bf16[4,256,512]{2,1,0:T(8,128)(2,1)}) %all-gather.13.cloned.1.call-update) | async-done | bytes 1048592 | tf_op jit(solution)/shard_map/all_gather | solution.py:438
  190.0 26.9 %all-gather.19.cloned.1.call-done = bf16[4,256,512]{2,1,0:T(8,128)(2,1)} async-done(((bf16[1,256,512]{2,1,0:T(8,128)(2,1)}), bf16[4,256,512]{2,1,0:T(8,128)(2,1)}) %all-gather.19.cloned.1.call-update) | async-done | bytes 1048592 | tf_op jit(solution)/shard_map/all_gather | solution.py:438
  228.4 21.1 %maximum_maximum_fusion = bf16[2048,1024]{1,0:T(8,128)(2,1)S(1)} fusion(bf16[512,512]{1,0:T(8,128)(2,1)S(1)} %bitcast.561, bf16[512,512]{1,0:T(8,128)(2,1)S(1)} %bitcast.560, bf16[512,512]{1,0:T(8,128)(2,1)} %bitcast.21, bf16[512,512]{1,0:T(8,128)(2,1)S(1)} %bitcast.552, bf16[512,512]{1,0:T(8,128)(2,1)S(1)} %bitcast.558, bf16[512,512]{1,0:T(8,128)(2,1)} %bitcast.18, ...), kind=kLoop, calls=%fused_computation.52 | loop fusion | flops 33554432 | bytes 8388608 | tf_op jit(solution)/shard_map/concatenate | solution.py:460
  276.2 9.1 fusion.4
  308.3 18.2 %collective-permute-done.13 = bf16[2,4,128,512]{3,2,1,0:T(8,128)(2,1)S(1)} collective-permute-done((bf16[2,4,128,512]{3,2,1,0:T(8,128)(2,1)S(1)}, bf16[2,4,128,512]{3,2,1,0:T(8,128)(2,1)S(1)}, u32[]{:S(2)}, u32[]{:S(2)}) %collective-permute-start.13) | collective-permute-done | bytes 1048608 | tf_op jit(solution)/shard_map/ppermute | solution.py:411
  337.8 11.2 %collective-permute-done.17 = bf16[2,4,128,512]{3,2,1,0:T(8,128)(2,1)S(1)} collective-permute-done((bf16[2,4,128,512]{3,2,1,0:T(8,128)(2,1)S(1)}, bf16[2,4,128,512]{3,2,1,0:T(8,128)(2,1)S(1)}, u32[]{:S(2)}, u32[]{:S(2)}) %collective-permute-start.17) | collective-permute-done | bytes 1048608 | tf_op jit(solution)/shard_map/ppermute | solution.py:411
  351.5 19.4 %multiply_convert_fusion.5 = (bf16[704,2048]{1,0:T(8,128)(2,1)S(1)}, f32[704,2048]{1,0:T(8,128)}) fusion(f32[2048]{0:T(1024)S(1)} %bitcast.728, bf16[512,512]{1,0:T(8,128)(2,1)S(1)} %bitcast.605, bf16[512,512]{1,0:T(8,128)(2,1)S(1)} %bitcast.603, bf16[512,512]{1,0:T(8,128)(2,1)} %bitcast.63, bf16[512,512]{1,0:T(8,128)(2,1)} %bitcast.62, ...), kind=kOutput, calls=%fused_computation.51 | convolution fusion | flops 3003645952 | bytes 14295040 | tf_op jit(solution)/shard_map/dot_general | solution.py:424
  371.0 17.6 %fusion.193 = f32[704,1024]{1,0:T(8,128)S(1)} fusion(bf16[704,2048]{1,0:T(8,128)(2,1)S(1)} %get-tuple-element.322, bf16[512,512]{1,0:T(8,128)(2,1)S(1)} %bitcast.613, bf16[512,512]{1,0:T(8,128)(2,1)S(1)} %bitcast.611, bf16[512,512]{1,0:T(8,128)(2,1)} %bitcast.80, bf16[512,512]{1,0:T(8,128)(2,1)} %bitcast.79, bf16[512,512]{1,0:T(8,128)(2,1)S(1)} %bitcast.609, ...), kind=kOutput, calls=%fused_computation.532 | convolution fusion | flops 2986344448 | bytes 9961472 | tf_op jit(solution)/shard_map/dot_general | solution.py:424
  398.1 15.7 %maximum_maximum_fusion.3 = bf16[2048,1024]{1,0:T(8,128)(2,1)S(1)} fusion(bf16[512,512]{1,0:T(8,128)(2,1)S(1)} %bitcast.556, bf16[512,512]{1,0:T(8,128)(2,1)S(1)} %bitcast.555, bf16[512,512]{1,0:T(8,128)(2,1)S(1)} %bitcast.551, bf16[512,512]{1,0:T(8,128)(2,1)S(1)} %bitcast.549, bf16[512,512]{1,0:T(8,128)(2,1)S(1)} %bitcast.554, ...), kind=kLoop, calls=%fused_computation.55 | loop fusion | flops 33554432 | bytes 8388608 | tf_op jit(solution)/shard_map/concatenate | solution.py:460
  437.9 9.1 fusion.5
  466.4 16.6 %collective-permute-done.27 = bf16[2,4,128,512]{3,2,1,0:T(8,128)(2,1)S(1)} collective-permute-done((bf16[2,4,128,512]{3,2,1,0:T(8,128)(2,1)S(1)}, bf16[2,4,128,512]{3,2,1,0:T(8,128)(2,1)S(1)}, u32[]{:S(2)}, u32[]{:S(2)}) %collective-permute-start.27) | collective-permute-done | bytes 1048608 | tf_op jit(solution)/shard_map/ppermute | solution.py:411
  484.5 19.7 %multiply_convert_fusion.4 = (bf16[704,2048]{1,0:T(8,128)(2,1)S(1)}, f32[704,2048]{1,0:T(8,128)}) fusion(f32[2048]{0:T(1024)S(1)} %bitcast.730, bf16[512,512]{1,0:T(8,128)(2,1)S(1)} %bitcast.639, bf16[512,512]{1,0:T(8,128)(2,1)S(1)} %bitcast.637, bf16[512,512]{1,0:T(8,128)(2,1)} %bitcast.125, bf16[512,512]{1,0:T(8,128)(2,1)} %bitcast.124, ...), kind=kOutput, calls=%fused_computation.50 | convolution fusion | flops 3003645952 | bytes 14295040 | tf_op jit(solution)/shard_map/dot_general | solution.py:424
  504.3 18.3 %fusion.192 = f32[704,1024]{1,0:T(8,128)} fusion(bf16[704,2048]{1,0:T(8,128)(2,1)S(1)} %get-tuple-element.328, bf16[512,512]{1,0:T(8,128)(2,1)S(1)} %bitcast.631, bf16[512,512]{1,0:T(8,128)(2,1)S(1)} %bitcast.629, bf16[512,512]{1,0:T(8,128)(2,1)S(1)} %bitcast.620, bf16[512,512]{1,0:T(8,128)(2,1)S(1)} %bitcast.615, bf16[512,512]{1,0:T(8,128)(2,1)S(1)} %bitcast.627, ...), kind=kOutput, calls=%fused_computation.531 | convolution fusion | flops 2986344448 | bytes 9961472 | tf_op jit(solution)/shard_map/dot_general | solution.py:424
  522.6 28.5 %convert_reduce_fusion = (f32[2048]{0:T(1024)S(1)}, bf16[704,2048]{1,0:T(8,128)(2,1)S(1)}) fusion(f32[704,2048]{1,0:T(8,128)} %get-tuple-element.329, f32[2048]{0:T(1024)S(1)} %bitcast.731, bf16[512,512]{1,0:T(8,128)(2,1)S(1)} %bitcast.632, bf16[512,512]{1,0:T(8,128)(2,1)S(1)} %bitcast.630, bf16[512,512]{1,0:T(8,128)(2,1)S(1)} %bitcast.621, ...), kind=kOutput, calls=%fused_computation.46 | convolution fusion | flops 3023828992 | bytes 14303232 | tf_op jit(solution)/shard_map/dot_general | solution.py:424
  551.1 19.3 %fusion.194 = f32[704,1024]{1,0:T(8,128)} fusion(bf16[704,2048]{1,0:T(8,128)(2,1)S(1)} %get-tuple-element.347, bf16[512,512]{1,0:T(8,128)(2,1)S(1)} %bitcast.640, bf16[512,512]{1,0:T(8,128)(2,1)S(1)} %bitcast.638, bf16[512,512]{1,0:T(8,128)(2,1)} %bitcast.125, bf16[512,512]{1,0:T(8,128)(2,1)} %bitcast.124, bf16[512,512]{1,0:T(8,128)(2,1)S(1)} %bitcast.636, ...), kind=kOutput, calls=%fused_computation.533 | convolution fusion | flops 2986344448 | bytes 9961472 | tf_op jit(solution)/shard_map/dot_general | solution.py:424
  612.8 14.5 %collective-permute-done.62 = bf16[1024,512]{1,0:T(8,128)(2,1)S(1)} collective-permute-done((bf16[1024,512]{1,0:T(8,128)(2,1)S(1)}, bf16[1024,512]{1,0:T(8,128)(2,1)S(1)}, u32[]{:S(2)}, u32[]{:S(2)}) %collective-permute-start.62) | collective-permute-done | bytes 1048608 | tf_op jit(solution)/shard_map/ppermute | solution.py:411
  640.8 9.4 convert_reduce_fusion.3
  650.2 14.6 %multiply_reduce_fusion.1 = (f32[8,704]{1,0:T(8,128)S(1)}, f32[8,704,704]{1,2,0:T(8,128)}) fusion(f32[8,704,704]{1,2,0:T(8,128)} %get-tuple-element.327, f32[8,704]{1,0:T(8,128)S(1)} %log_add_fusion.1, pred[704,704]{0,1:T(8,128)(4,1)S(1)} %compare_and_fusion, bf16[704,8,64]{0,2,1:T(8,128)(2,1)S(1)} %bitcast.546, bf16[704,8,64]{0,2,1:T(8,128)(2,1)S(1)} %bitcast.544), kind=kOutput, calls=%fused_computation.8 | convolution fusion | flops 523364864 | bytes 33701888 | tf_op jit(solution)/shard_map/the,she->hts/dot_general | solution.py:699
  671.4 11.2 %multiply_convert_fusion.1 = bf16[8,704,704]{1,2,0:T(8,128)(2,1)} fusion(f32[8,704,704]{1,2,0:T(8,128)} %get-tuple-element.331, f32[8,704,704]{1,2,0:T(8,128)S(1)} %bitcast.508, f32[8,704]{1,0:T(8,128)S(1)} %get-tuple-element.330, f32[8,704]{1,0:T(8,128)S(1)} %log_add_fusion.1, pred[704,704]{0,1:T(8,128)(4,1)S(1)} %compare_and_fusion), kind=kLoop, calls=%fused_computation.7 | loop fusion | flops 19824640 | bytes 40189952 | tf_op jit(solution)/shard_map/convert_element_type | solution.py:701
  729.8 9.4 collective-permute-done.58
  743.9 20.6 %convert_reduce_fusion.1 = (f32[2048]{0:T(1024)S(1)}, bf16[704,2048]{1,0:T(8,128)(2,1)S(1)}) fusion(f32[704,2048]{1,0:T(8,128)} %get-tuple-element.323, f32[2048]{0:T(1024)S(1)} %bitcast.729, bf16[512,512]{1,0:T(8,128)(2,1)S(1)} %bitcast.614, bf16[512,512]{1,0:T(8,128)(2,1)S(1)} %bitcast.612, bf16[512,512]{1,0:T(8,128)(2,1)} %bitcast.80, ...), kind=kOutput, calls=%fused_computation.47 | convolution fusion | flops 3023828992 | bytes 14303232 | tf_op jit(solution)/shard_map/dot_general | solution.py:424
  764.6 19.1 %fusion.195 = f32[704,1024]{1,0:T(8,128)} fusion(bf16[704,2048]{1,0:T(8,128)(2,1)S(1)} %get-tuple-element.339, bf16[512,512]{1,0:T(8,128)(2,1)S(1)} %bitcast.606, bf16[512,512]{1,0:T(8,128)(2,1)S(1)} %bitcast.604, bf16[512,512]{1,0:T(8,128)(2,1)} %bitcast.63, bf16[512,512]{1,0:T(8,128)(2,1)} %bitcast.62, bf16[512,512]{1,0:T(8,128)(2,1)S(1)} %bitcast.602, ...), kind=kOutput, calls=%fused_computation.534 | convolution fusion | flops 2986344448 | bytes 9961472 | tf_op jit(solution)/shard_map/dot_general | solution.py:424
  824.7 13.9 %collective-permute-done.50 = bf16[1024,512]{1,0:T(8,128)(2,1)} collective-permute-done((bf16[1024,512]{1,0:T(8,128)(2,1)}, bf16[1024,512]{1,0:T(8,128)(2,1)}, u32[]{:S(2)}, u32[]{:S(2)}) %collective-permute-start.50) | collective-permute-done | bytes 1048608 | tf_op jit(solution)/shard_map/ppermute | solution.py:411
  849.4 9.2 convert_reduce_fusion.5
  858.6 14.6 %multiply_reduce_fusion = (f32[8,704]{1,0:T(8,128)S(1)}, f32[8,704,704]{1,2,0:T(8,128)}) fusion(f32[8,704,704]{1,2,0:T(8,128)} %get-tuple-element.321, f32[8,704]{1,0:T(8,128)S(1)} %copy-done.148, pred[704,704]{0,1:T(8,128)(4,1)S(1)} %compare_and_fusion, bf16[704,8,64]{0,2,1:T(8,128)(2,1)S(1)} %bitcast.548, bf16[704,8,64]{0,2,1:T(8,128)(2,1)S(1)} %bitcast.542), kind=kOutput, calls=%fused_computation.5 | convolution fusion | flops 523364864 | bytes 33701888 | tf_op jit(solution)/shard_map/the,she->hts/dot_general | solution.py:699
  880.4 11.2 %multiply_convert_fusion = bf16[8,704,704]{1,2,0:T(8,128)(2,1)} fusion(f32[8,704,704]{1,2,0:T(8,128)} %get-tuple-element.333, f32[8,704,704]{1,2,0:T(8,128)S(1)} %bitcast.506, f32[8,704]{1,0:T(8,128)S(1)} %get-tuple-element.332, f32[8,704]{1,0:T(8,128)S(1)} %copy-done.148, pred[704,704]{0,1:T(8,128)(4,1)S(1)} %compare_and_fusion), kind=kLoop, calls=%fused_computation.4 | loop fusion | flops 19824640 | bytes 40189952 | tf_op jit(solution)/shard_map/convert_element_type | solution.py:701
  934.2 11.2 %collective-permute-done.46 = bf16[1024,512]{1,0:T(8,128)(2,1)} collective-permute-done((bf16[1024,512]{1,0:T(8,128)(2,1)}, bf16[1024,512]{1,0:T(8,128)(2,1)}, u32[]{:S(2)}, u32[]{:S(2)}) %collective-permute-start.46) | collective-permute-done | bytes 1048608 | tf_op jit(solution)/shard_map/ppermute | solution.py:411
  976.9 13.3 %all-to-all-done.1 = f32[32,1,2818]{2,1,0:T(1,128)S(1)} async-done(((f32[32,1,2818]{2,1,0:T(1,128)}), f32[32,1,2818]{2,1,0:T(1,128)S(1)}, u32[]{:S(2)}, u32[]{:S(2)}) %all-to-all-start.1) | async-done | bytes 360736 | tf_op jit(solution)/shard_map/all_to_all | solution.py:747
  (1007 shorter events, 467.2 us)
Async XLA Ops:
  7.2 79.4 %all-gather.9.cloned.1.call-start = ((), (), s32[]{:S(2)}) async-start(), calls=%async_computation.8 | async-start | bytes 1310720 | tf_op jit(solution)/shard_map/all_gather | solution.py:438
  15.9 68.4 %collective-permute-start.36 = (bf16[340,1024]{1,0:T(8,128)(2,1)}, bf16[340,1024]{1,0:T(8,128)(2,1)S(1)}, u32[]{:S(2)}, u32[]{:S(2)}) collective-permute-start(bf16[340,1024]{1,0:T(8,128)(2,1)} %param.29), channel_id=1, source_target_pairs={{0,0},{1,8},{8,1},{9,9},{2,2},{3,10},{10,3},{11,11},{4,4},{5,12},{... | collective-permute-start | bytes 2088968 | tf_op jit(solution)/shard_map/ppermute | solution.py:415
  69.3 89.2 %all-gather.17.cloned.1.call-start = ((), (), s32[]{:S(2)}) async-start(), calls=%async_computation.12 | async-start | bytes 1310720 | tf_op jit(solution)/shard_map/all_gather | solution.py:438
  72.4 115.0 %all-gather.13.cloned.1.call-start = ((), (), s32[]{:S(2)}) async-start(), calls=%async_computation.10 | async-start | bytes 1310720 | tf_op jit(solution)/shard_map/all_gather | solution.py:438
  73.6 143.3 %all-gather.19.cloned.1.call-start = ((), (), s32[]{:S(2)}) async-start(), calls=%async_computation.13 | async-start | bytes 1310720 | tf_op jit(solution)/shard_map/all_gather | solution.py:438
  77.4 174.0 %collective-permute-start.1 = (bf16[352,1024]{1,0:T(8,128)(2,1)}, bf16[352,1024]{1,0:T(8,128)(2,1)}, u32[]{:S(2)}, u32[]{:S(2)}) collective-permute-start(bf16[352,1024]{1,0:T(8,128)(2,1)} %fusion.54), channel_id=1, source_target_pairs={{0,8},{8,0},{1,9},{9,1},{2,10},{10,2},{3,11},{11,3},{4,12},{12,4},... | collective-permute-start | bytes 2162696 | tf_op jit(solution)/shard_map/ppermute | solution.py:407
  86.5 889.2 %reduce-scatter.17.cloned.1.call-start = ((), (), s32[]{:S(2)}) async-start(), calls=%async_computation.19 | async-start | bytes 1310720 | tf_op jit(solution)/shard_map/reduce_scatter | solution.py:476
  102.5 117.1 %collective-permute-start.22 = (bf16[4,128,512]{2,1,0:T(8,128)(2,1)S(1)}, bf16[4,128,512]{2,1,0:T(8,128)(2,1)S(1)}, u32[]{:S(2)}, u32[]{:S(2)}) collective-permute-start(bf16[4,128,512]{2,1,0:T(8,128)(2,1)S(1)} %get-tuple-element.202), channel_id=1, source_target_pairs={{0,16},{16,0},{1,17},{17,1},{2,18},{18,2},{3,19},{19,3},{4,20},{20... | collective-permute-start | bytes 1572872 | tf_op jit(solution)/shard_map/ppermute | solution.py:411
  132.3 89.6 %collective-permute-start.10 = (bf16[4,128,512]{2,1,0:T(8,128)(2,1)}, bf16[4,128,512]{2,1,0:T(8,128)(2,1)}, u32[]{:S(2)}, u32[]{:S(2)}) collective-permute-start(bf16[4,128,512]{2,1,0:T(8,128)(2,1)} %get-tuple-element.219), channel_id=1, source_target_pairs={{0,1},{1,0},{2,3},{3,2},{4,5},{5,4},{6,7},{7,6},{8,9},{9,8},{10,11... | collective-permute-start | bytes 1572872 | tf_op jit(solution)/shard_map/ppermute | solution.py:411
  135.8 89.5 %collective-permute-start.4 = (bf16[2,4,128,512]{3,2,1,0:T(8,128)(2,1)}, bf16[2,4,128,512]{3,2,1,0:T(8,128)(2,1)}, u32[]{:S(2)}, u32[]{:S(2)}) collective-permute-start(bf16[2,4,128,512]{3,2,1,0:T(8,128)(2,1)} %pad_maximum_fusion.12), channel_id=1, source_target_pairs={{0,16},{16,0},{1,17},{17,1},{2,18},{18,2},{3,19},{19,3},{4,20},{20... | collective-permute-start | bytes 3145736 | tf_op jit(solution)/shard_map/ppermute | solution.py:411
  219.6 75.3 %collective-permute-start.20 = (bf16[4,128,512]{2,1,0:T(8,128)(2,1)}, bf16[4,128,512]{2,1,0:T(8,128)(2,1)}, u32[]{:S(2)}, u32[]{:S(2)}) collective-permute-start(bf16[4,128,512]{2,1,0:T(8,128)(2,1)} %get-tuple-element.203), channel_id=1, source_target_pairs={{0,1},{1,0},{2,3},{3,2},{4,5},{5,4},{6,7},{7,6},{8,9},{9,8},{10,11... | collective-permute-start | bytes 1572872 | tf_op jit(solution)/shard_map/ppermute | solution.py:411
  221.9 76.6 %collective-permute-start.16 = (bf16[4,128,512]{2,1,0:T(8,128)(2,1)}, bf16[4,128,512]{2,1,0:T(8,128)(2,1)}, u32[]{:S(2)}, u32[]{:S(2)}) collective-permute-start(bf16[4,128,512]{2,1,0:T(8,128)(2,1)} %get-tuple-element.210), channel_id=1, source_target_pairs={{0,16},{16,0},{1,17},{17,1},{2,18},{18,2},{3,19},{19,3},{4,20},{20... | collective-permute-start | bytes 1572872 | tf_op jit(solution)/shard_map/ppermute | solution.py:411
  225.2 76.8 %collective-permute-start.14 = (bf16[4,128,512]{2,1,0:T(8,128)(2,1)}, bf16[4,128,512]{2,1,0:T(8,128)(2,1)}, u32[]{:S(2)}, u32[]{:S(2)}) collective-permute-start(bf16[4,128,512]{2,1,0:T(8,128)(2,1)} %get-tuple-element.211), channel_id=1, source_target_pairs={{0,1},{1,0},{2,3},{3,2},{4,5},{5,4},{6,7},{7,6},{8,9},{9,8},{10,11... | collective-permute-start | bytes 1572872 | tf_op jit(solution)/shard_map/ppermute | solution.py:411
  226.8 73.6 %collective-permute-start.12 = (bf16[4,128,512]{2,1,0:T(8,128)(2,1)}, bf16[4,128,512]{2,1,0:T(8,128)(2,1)}, u32[]{:S(2)}, u32[]{:S(2)}) collective-permute-start(bf16[4,128,512]{2,1,0:T(8,128)(2,1)} %get-tuple-element.218), channel_id=1, source_target_pairs={{0,16},{16,0},{1,17},{17,1},{2,18},{18,2},{3,19},{19,3},{4,20},{20... | collective-permute-start | bytes 1572872 | tf_op jit(solution)/shard_map/ppermute | solution.py:411
  298.5 224.1 %collective-permute-start.37 = (bf16[352,1024]{1,0:T(8,128)(2,1)}, bf16[352,1024]{1,0:T(8,128)(2,1)}, u32[]{:S(2)}, u32[]{:S(2)}) collective-permute-start(bf16[352,1024]{1,0:T(8,128)(2,1)} %fusion.46), channel_id=1, source_target_pairs={{0,8},{8,0},{1,9},{9,1},{2,10},{10,2},{3,11},{11,3},{4,12},{12,4},... | collective-permute-start | bytes 2162696 | tf_op jit(solution)/shard_map/ppermute | solution.py:407
  300.4 88.3 %collective-permute-start.32 = (bf16[4,128,512]{2,1,0:T(8,128)(2,1)S(1)}, bf16[4,128,512]{2,1,0:T(8,128)(2,1)S(1)}, u32[]{:S(2)}, u32[]{:S(2)}) collective-permute-start(bf16[4,128,512]{2,1,0:T(8,128)(2,1)S(1)} %copy-done.140), channel_id=1, source_target_pairs={{0,16},{16,0},{1,17},{17,1},{2,18},{18,2},{3,19},{19,3},{4,20},{20... | collective-permute-start | bytes 1572872 | tf_op jit(solution)/shard_map/ppermute | solution.py:411
  392.2 66.8 %collective-permute-start.28 = (bf16[4,128,512]{2,1,0:T(8,128)(2,1)}, bf16[4,128,512]{2,1,0:T(8,128)(2,1)}, u32[]{:S(2)}, u32[]{:S(2)}) collective-permute-start(bf16[4,128,512]{2,1,0:T(8,128)(2,1)} %get-tuple-element.194), channel_id=1, source_target_pairs={{0,16},{16,0},{1,17},{17,1},{2,18},{18,2},{3,19},{19,3},{4,20},{20... | collective-permute-start | bytes 1572872 | tf_op jit(solution)/shard_map/ppermute | solution.py:411
  394.1 66.5 %collective-permute-start.31 = (bf16[2,4,128,512]{3,2,1,0:T(8,128)(2,1)}, bf16[2,4,128,512]{3,2,1,0:T(8,128)(2,1)}, u32[]{:S(2)}, u32[]{:S(2)}) collective-permute-start(bf16[2,4,128,512]{3,2,1,0:T(8,128)(2,1)} %pad_maximum_fusion.22), channel_id=1, source_target_pairs={{0,16},{16,0},{1,17},{17,1},{2,18},{18,2},{3,19},{19,3},{4,20},{20... | collective-permute-start | bytes 3145736 | tf_op jit(solution)/shard_map/ppermute | solution.py:411
  608.7 89.5 %collective-permute-start.69 = (bf16[512,512]{1,0:T(8,128)(2,1)}, bf16[512,512]{1,0:T(8,128)(2,1)}, u32[]{:S(2)}, u32[]{:S(2)}) collective-permute-start(bf16[512,512]{1,0:T(8,128)(2,1)} %slice.1263), channel_id=1, source_target_pairs={{0,16},{16,0},{1,17},{17,1},{2,18},{18,2},{3,19},{19,3},{4,20},{20... | collective-permute-start | bytes 1572872 | tf_op jit(solution)/shard_map/ppermute | solution.py:411
  627.3 72.2 %collective-permute-start.67 = (bf16[512,512]{1,0:T(8,128)(2,1)}, bf16[512,512]{1,0:T(8,128)(2,1)}, u32[]{:S(2)}, u32[]{:S(2)}) collective-permute-start(bf16[512,512]{1,0:T(8,128)(2,1)} %slice.1259), channel_id=1, source_target_pairs={{0,1},{1,0},{2,3},{3,2},{4,5},{5,4},{6,7},{7,6},{8,9},{9,8},{10,11... | collective-permute-start | bytes 1572872 | tf_op jit(solution)/shard_map/ppermute | solution.py:411
  631.4 83.0 %collective-permute-start.63 = (bf16[512,512]{1,0:T(8,128)(2,1)}, bf16[512,512]{1,0:T(8,128)(2,1)}, u32[]{:S(2)}, u32[]{:S(2)}) collective-permute-start(bf16[512,512]{1,0:T(8,128)(2,1)} %slice.1248), channel_id=1, source_target_pairs={{0,1},{1,0},{2,3},{3,2},{4,5},{5,4},{6,7},{7,6},{8,9},{9,8},{10,11... | collective-permute-start | bytes 1572872 | tf_op jit(solution)/shard_map/ppermute | solution.py:411
  637.6 78.0 %collective-permute-start.65 = (bf16[512,512]{1,0:T(8,128)(2,1)}, bf16[512,512]{1,0:T(8,128)(2,1)}, u32[]{:S(2)}, u32[]{:S(2)}) collective-permute-start(bf16[512,512]{1,0:T(8,128)(2,1)} %slice.1252), channel_id=1, source_target_pairs={{0,16},{16,0},{1,17},{17,1},{2,18},{18,2},{3,19},{19,3},{4,20},{20... | collective-permute-start | bytes 1572872 | tf_op jit(solution)/shard_map/ppermute | solution.py:411
  701.8 273.9 %reduce-scatter.15.cloned.1.call-start = ((), (), s32[]{:S(2)}) async-start(), calls=%async_computation.18 | async-start | bytes 1310720 | tf_op jit(solution)/shard_map/reduce_scatter | solution.py:476
  718.2 257.5 %reduce-scatter.13.cloned.1.call-start = ((), (), s32[]{:S(2)}) async-start(), calls=%async_computation.17 | async-start | bytes 1310720 | tf_op jit(solution)/shard_map/reduce_scatter | solution.py:476
  728.8 71.4 %collective-permute-start.61 = (bf16[512,512]{1,0:T(8,128)(2,1)}, bf16[512,512]{1,0:T(8,128)(2,1)S(1)}, u32[]{:S(2)}, u32[]{:S(2)}) collective-permute-start(bf16[512,512]{1,0:T(8,128)(2,1)} %slice.1241), channel_id=1, source_target_pairs={{0,16},{16,0},{1,17},{17,1},{2,18},{18,2},{3,19},{19,3},{4,20},{20... | collective-permute-start | bytes 1572872 | tf_op jit(solution)/shard_map/ppermute | solution.py:411
  804.3 188.7 %reduce-scatter.11.cloned.1.call-start = ((), (), s32[]{:S(2)}) async-start(), calls=%async_computation.16 | async-start | bytes 1310720 | tf_op jit(solution)/shard_map/reduce_scatter | solution.py:476
  819.4 86.6 %collective-permute-start.55 = (bf16[512,512]{1,0:T(8,128)(2,1)}, bf16[512,512]{1,0:T(8,128)(2,1)}, u32[]{:S(2)}, u32[]{:S(2)}) collective-permute-start(bf16[512,512]{1,0:T(8,128)(2,1)} %slice.1229), channel_id=1, source_target_pairs={{0,1},{1,0},{2,3},{3,2},{4,5},{5,4},{6,7},{7,6},{8,9},{9,8},{10,11... | collective-permute-start | bytes 1572872 | tf_op jit(solution)/shard_map/ppermute | solution.py:411
  824.1 83.7 %collective-permute-start.57 = (bf16[512,512]{1,0:T(8,128)(2,1)}, bf16[512,512]{1,0:T(8,128)(2,1)}, u32[]{:S(2)}, u32[]{:S(2)}) collective-permute-start(bf16[512,512]{1,0:T(8,128)(2,1)} %slice.1233), channel_id=1, source_target_pairs={{0,16},{16,0},{1,17},{17,1},{2,18},{18,2},{3,19},{19,3},{4,20},{20... | collective-permute-start | bytes 1572872 | tf_op jit(solution)/shard_map/ppermute | solution.py:411
  842.7 78.5 %collective-permute-start.51 = (bf16[512,512]{1,0:T(8,128)(2,1)}, bf16[512,512]{1,0:T(8,128)(2,1)}, u32[]{:S(2)}, u32[]{:S(2)}) collective-permute-start(bf16[512,512]{1,0:T(8,128)(2,1)} %slice.1218), channel_id=1, source_target_pairs={{0,1},{1,0},{2,3},{3,2},{4,5},{5,4},{6,7},{7,6},{8,9},{9,8},{10,11... | collective-permute-start | bytes 1572872 | tf_op jit(solution)/shard_map/ppermute | solution.py:411
  846.7 75.8 %collective-permute-start.53 = (bf16[512,512]{1,0:T(8,128)(2,1)}, bf16[512,512]{1,0:T(8,128)(2,1)}, u32[]{:S(2)}, u32[]{:S(2)}) collective-permute-start(bf16[512,512]{1,0:T(8,128)(2,1)} %slice.1222), channel_id=1, source_target_pairs={{0,16},{16,0},{1,17},{17,1},{2,18},{18,2},{3,19},{19,3},{4,20},{20... | collective-permute-start | bytes 1572872 | tf_op jit(solution)/shard_map/ppermute | solution.py:411
  910.1 82.9 %reduce-scatter.9.cloned.1.call-start = ((), (), s32[]{:S(2)}) async-start(), calls=%async_computation.15 | async-start | bytes 1310720 | tf_op jit(solution)/shard_map/reduce_scatter | solution.py:476
  924.8 74.1 %reduce-scatter.7.cloned.1.call-start = ((), (), s32[]{:S(2)}) async-start(), calls=%async_computation.14 | async-start | bytes 1310720 | tf_op jit(solution)/shard_map/reduce_scatter | solution.py:476
  (280 other events, 6319.2 us)
Sparse Core Ops, SparseCore 0:
  20.7 34.4 all-gather.8
  68.7 31.2 all-gather.14
  102.2 27.4 all-gather.10
  131.1 27.4 all-gather.16
  159.9 27.4 all-gather.12
  189.4 27.4 all-gather.18
  701.9 26.2 reduce-scatter.16
  730.6 25.8 reduce-scatter.14
  804.5 26.0 reduce-scatter.12
  910.2 27.3 reduce-scatter.10
  940.5 25.7 reduce-scatter.8
  969.2 29.7 reduce-scatter.6

commit v2 on v0

--- a/solution.py
+++ b/solution.py
@@ -1,6 +1,8 @@
 import jax
 import jax.numpy as jnp
 from jax import lax
+from jax.experimental import pallas as pl
+from jax.experimental.pallas import tpu as pltpu
 from jax.sharding import PartitionSpec as P
 
 HIGH = lax.Precision.HIGHEST
@@ -397,41 +399,933 @@
     )
 
 
+BF = jnp.bfloat16
+F32 = jnp.float32
+NN = (((1,), (0,)), ((), ()))
+NT = (((1,), (1,)), ((), ()))
+TN = (((0,), (0,)), ((), ()))
+VMEM_BYTES = 60 * 1024 * 1024
+
+
+def sibling(values):
+    return lax.ppermute(values, "core", [(0, 1), (1, 0)])
+
+
+def across(values, axis):
+    return lax.ppermute(values, axis, [(0, 1), (1, 0)])
+
+
+def trade(values):
+    return lax.ppermute(values, ("core", "x"), [(0, 0), (1, 2), (2, 1), (3, 3)])
+
+
+def turned(values, flag, axis):
+    half = values.shape[axis] // 2
+    return jnp.where(flag == 1, jnp.roll(values, half, axis), values)
+
+
+def dot(left, right, dims=NN):
+    return lax.dot_general(left, right, dims, preferred_element_type=F32)
+
+
+def shape_of(dims, kind):
+    return jax.ShapeDtypeStruct(dims, kind)
+
+
+def call(body, grid, in_specs, out_specs, out_shape, scratch, flops, moved, args):
+    return pl.pallas_call(
+        body,
+        grid=grid,
+        in_specs=in_specs,
+        out_specs=out_specs,
+        out_shape=out_shape,
+        scratch_shapes=scratch,
+        compiler_params=pltpu.CompilerParams(
+            dimension_semantics=("arbitrary",) * len(grid), vmem_limit_bytes=VMEM_BYTES
+        ),
+        cost_estimate=pl.CostEstimate(flops=flops, bytes_accessed=moved, transcendentals=0),
+    )(*args)
+
+
+def fixed(dims):
+    return pl.BlockSpec(dims, lambda *_: (0,) * len(dims))
+
+
+def row_loop(total, size, body, unroll=1):
+    @pl.loop(0, total // size, unroll=unroll)
+    def _(step):
+        body(pl.ds(pl.multiple_of(step * size, size), size))
+
+
+def weight_specs(low):
+    return [
+        pl.BlockSpec((low, low), lambda t: (jnp.minimum(t, 1), 0)),
+        pl.BlockSpec((low, low), lambda t: (jnp.maximum(t - 2, 0), 0)),
+        pl.BlockSpec((low, low), lambda t: (jnp.minimum(t, 1), 0)),
+        fixed((low, low)),
+        fixed((low, low)),
+    ]
+
+
+def with_tile(step, refs, body):
+    g, gx, gy, ga, gb = refs
+
+    @pl.when(step < 2)
+    def _():
+        body(g[...], gy[...])
+
+    @pl.when(step == 2)
+    def _():
+        body(gx[...], ga[...])
+
+    @pl.when(step == 3)
+    def _():
+        body(gx[...], gb[...])
+
+
+def join_into(joined, own, other):
+    rows = own.shape[0]
+    joined[:rows, :] = own[...]
+    joined[rows:, :] = other[...]
+
+
+def fc_up(own, other, blocks, bias):
+    rows, width = own.shape
+    low, both = width // 2, 2 * rows
+    hid = 4 * low
+
+    def body(own_ref, other_ref, g, gx, gy, ga, gb, bias_ref, joined, act, slope):
+        step = pl.program_id(0)
+
+        @pl.when(step == 0)
+        def _():
+            join_into(joined, own_ref, other_ref)
+
+        def product(first, second):
+            for lanes in (slice(0, low // 2), slice(low // 2, low)):
+                for sl in (slice(0, rows), slice(rows, both)):
+                    pre = dot(joined[sl, :low], first[lanes, :], NT)
+                    pre = pre + dot(joined[sl, low:], second[lanes, :], NT) + bias_ref[:, lanes]
+                    root = 0.7978845608028654
+                    square = pre * pre
+                    tanh = jnp.tanh(pre * (root + (root * 0.044715) * square))
+                    half = 0.5 + 0.5 * tanh
+                    act[sl, lanes] = (pre * half).astype(BF)
+                    inner = pre * ((0.5 * root) + (1.5 * 0.044715 * root) * square)
+                    slope[sl, lanes] = (half + (1.0 - tanh * tanh) * inner).astype(BF)
+
+        with_tile(step, (g, gx, gy, ga, gb), product)
+
+    return call(
+        body,
+        (4,),
+        [fixed((rows, width))] * 2 + weight_specs(low) + [pl.BlockSpec((1, low), lambda t: (0, t))],
+        [fixed((both, width))] + [pl.BlockSpec((both, low), lambda t: (0, t))] * 2,
+        [shape_of((both, width), BF), shape_of((both, hid), BF), shape_of((both, hid), BF)],
+        [],
+        2 * both * width * hid,
+        2 * hid * width + 6 * both * width + 4 * both * hid,
+        (own, other, *blocks, bias),
+    )
+
+
+def fc_back(own, other, up_blocks, down_blocks, slope, act, hidden):
+    rows, width = own.shape
+    low, both = width // 2, 2 * rows
+    hid = 4 * low
+
+    def body(own_ref, other_ref, ug, ugx, ugy, uga, ugb, dg, dgx, dgy, dga, dgb, slope_ref, act_ref, hid_ref,
+             sums, out_own, out_other, *rest):
+        two_refs, one_refs, (joined, grad, acc) = rest[:5], rest[5:10], rest[10:]
+        step = pl.program_id(0)
+
+        @pl.when(step == 0)
+        def _():
+            join_into(joined, own_ref, other_ref)
+
+        def product(up_one, up_two, down_one, down_two, first, last, near, far):
+            for i, sl in enumerate((slice(rows, both), slice(0, rows))):
+                value = dot(joined[sl, :low], up_one[...], NT) + dot(joined[sl, low:], up_two[...], NT)
+                value = (value * slope_ref[sl, :].astype(F32)).astype(BF)
+                grad[sl, :] = value
+                total = jnp.sum(value.astype(F32).reshape(rows // 8, 8, low), axis=0)
+                sums[...] = total if i == 0 else sums[...] + total
+                for lanes, down in ((slice(0, low), down_one), (slice(low, width), down_two)):
+                    part = dot(value, down[...])
+                    if not first:
+                        part = part + acc[sl, lanes]
+                    if not last:
+                        acc[sl, lanes] = part
+                    elif i == 0:
+                        out_other[:, lanes] = part.astype(BF)
+                    else:
+                        out_own[:, lanes] = part
+            for refs, left, right in ((two_refs, act_ref, joined), (one_refs, grad, hid_ref)):
+                refs[near][...] = dot(left[...], right[:, :low], TN).astype(BF)
+                refs[far][...] = dot(left[...], right[:, low:], TN).astype(BF)
+
+        @pl.when(step == 0)
+        def _():
+            product(ug, ugy, dg, dgy, True, False, 0, 2)
+
+        @pl.when(step == 1)
+        def _():
+            product(ug, ugy, dg, dgy, False, False, 0, 2)
+
+        @pl.when(step == 2)
+        def _():
+            product(ugx, uga, dgx, dga, False, False, 1, 3)
+
+        @pl.when(step == 3)
+        def _():
+            product(ugx, ugb, dgx, dgb, False, True, 1, 4)
+
+    tiles = pl.BlockSpec((both, low), lambda t: (0, t))
+    early = pl.BlockSpec((low, low), lambda t: (jnp.minimum(t, 1), 0))
+    late = pl.BlockSpec((low, low), lambda t: (jnp.maximum(t - 2, 0), 0))
+    whole, part = shape_of((2 * low, low), BF), shape_of((low, low), BF)
+    found = call(
+        body,
+        (4,),
+        [fixed((rows, width))] * 2 + weight_specs(low) + weight_specs(low) + [tiles, tiles, fixed((both, width))],
+        [pl.BlockSpec((8, low), lambda t: (0, t)), fixed((rows, width)), fixed((rows, width))]
+        + [early, late, early, fixed((low, low)), fixed((low, low))] * 2,
+        [shape_of((8, hid), F32), shape_of((rows, width), F32), shape_of((rows, width), BF)]
+        + [whole, whole, whole, part, part] * 2,
+        [pltpu.VMEM((both, width), BF), pltpu.VMEM((both, low), BF), pltpu.VMEM((both, width), F32)],
+        8 * both * width * hid,
+        8 * hid * width + 6 * both * width + 4 * both * hid + 6 * rows * width,
+        (own, other, *up_blocks, *down_blocks, slope, act, hidden),
+    )
+    return found[:3], found[3:8], found[8:]
+
+
+def fc_down(left, blocks):
+    both, hid = left.shape
+    rows, low = both // 2, hid // 4
+    width = 2 * low
+
+    def body(left_ref, g, gx, gy, ga, gb, own, other, acc):
+        step = pl.program_id(0)
+
+        def product(one, two, first, last):
+            for i, sl in enumerate((slice(rows, both), slice(0, rows))):
+                for lanes, right in ((slice(0, low), one), (slice(low, width), two)):
+                    part = dot(left_ref[sl, :], right[...])
+                    if not first:
+                        part = part + acc[sl, lanes]
+                    if not last:
+                        acc[sl, lanes] = part
+                    elif i == 0:
+                        other[:, lanes] = part.astype(BF)
+                    else:
+                        own[:, lanes] = part
+
+        @pl.when(step == 0)
+        def _():
+            product(g, gy, True, False)
+
+        @pl.when(step == 1)
+        def _():
+            product(g, gy, False, False)
+
+        @pl.when(step == 2)
+        def _():
+            product(gx, ga, False, False)
+
+        @pl.when(step == 3)
+        def _():
+            product(gx, gb, False, True)
+
+    return call(
+        body,
+        (4,),
+        [pl.BlockSpec((both, low), lambda t: (0, t))] + weight_specs(low),
+        [fixed((rows, width))] * 2,
+        [shape_of((rows, width), F32), shape_of((rows, width), BF)],
+        [pltpu.VMEM((both, width), F32)],
+        2 * both * width * hid,
+        2 * hid * width + 2 * both * hid + 6 * rows * width,
+        (left, *blocks),
+    )
+
+
+def head_ones(size, head_width):
+    first = lax.broadcasted_iota(jnp.int32, (size, size), 0) // head_width
+    second = lax.broadcasted_iota(jnp.int32, (size, size), 1) // head_width
+    return (first == second).astype(BF)
+
+
+def qkv_up(own, other, blocks, vectors, ones):
+    rows, width = own.shape
+    low, both = width // 2, 2 * rows
+    tile = low // 2
+
+    def body(own_ref, other_ref, g, gx, gy, ga, gb, vec, ones_ref, joined, q_raw, k_raw, q_low, k_low, v_low, acc):
+        step = pl.program_id(0)
+        part = step % 3
+
+        @pl.when(step == 0)
+        def _():
+            join_into(joined, own_ref, other_ref)
+
+        def product(first, second):
+            acc[...] = dot(joined[:, :low], first, NT) + dot(joined[:, low:], second, NT)
+
+        @pl.when(step < 3)
+        def _():
+            product(g[...], gy[...])
+
+        @pl.when(jnp.logical_and(step >= 3, part < 2))
+        def _():
+            product(gx[...], ga[...])
+
+        @pl.when(step == 5)
+        def _():
+            product(gx[...], gb[...])
+
+        def unit(value):
+            square = dot((value * value).astype(BF), ones_ref[...])
+            return value * lax.rsqrt(square + EPS_UNIT)
+
+        @pl.when(part == 0)
+        def _():
+            def finish(sl):
+                value = acc[sl, :] + vec[0:1, :]
+                q_raw[sl, :] = value.astype(BF)
+                q_low[sl, :] = (unit(value) * vec[2:3, :]).astype(BF)
+
+            row_loop(both, both // 4, finish)
+
+        @pl.when(part == 1)
+        def _():
+            def finish(sl):
+                value = acc[sl, :]
+                k_raw[sl, :] = value.astype(BF)
+                k_low[sl, :] = unit(value).astype(BF)
+
+            row_loop(both, both // 4, finish)
+
+        @pl.when(part == 2)
+        def _():
+            v_low[...] = (acc[...] + vec[1:2, :]).astype(BF)
+
+    half = lambda t: t // 3
+    kept = pl.BlockSpec((both, tile), lambda t: (0, half(t)))
+    heads = shape_of((both, low), BF)
+    return call(
+        body,
+        (6,),
+        [fixed((rows, width))] * 2
+        + [
+            pl.BlockSpec((tile, low), lambda t: (jnp.minimum(t, 2), 0)),
+            pl.BlockSpec((tile, low), lambda t: (jnp.maximum(t - 3, 0), 0)),
+            pl.BlockSpec((tile, low), lambda t: (jnp.minimum(t, 2), 0)),
+            pl.BlockSpec((tile, low), lambda t: (jnp.clip(t - 3, 0, 1), 0)),
+            fixed((tile, low)),
+            pl.BlockSpec((8, tile), lambda t: (0, half(t))),
+            fixed((tile, tile)),
+        ],
+        [fixed((both, width))] + [kept] * 5,
+        [shape_of((both, width), BF)] + [heads] * 5,
+        [pltpu.VMEM((both, tile), F32)],
+        2 * both * width * 3 * low,
+        2 * 3 * low * width + 6 * both * width + 10 * both * low,
+        (own, other, *blocks, vectors, ones),
+    )
+
+
+def attn_mix(q_low, k_low, v_low, end_col, place_row, head_width):
+    both, low = q_low.shape
+    pair = 2 * head_width
+    chunk = both // 4
+
+    def body(q_ref, k_ref, v_ref, end_ref, place_ref, out_ref, rest_ref, log_ref):
+        place = place_ref[0:1, :]
+        ones = jnp.ones((both, head_width), BF)
+        for h in range(2):
+            lanes = slice(h * head_width, (h + 1) * head_width)
+            keys = k_ref[:, lanes]
+            values = jnp.concatenate((v_ref[:, lanes], ones), axis=1)
+            for c in range(4):
+                sl = slice(c * chunk, (c + 1) * chunk)
+                scores = dot(q_ref[sl, lanes], keys, NT)
+                expo = jnp.where(place < end_ref[sl, :], jnp.exp(scores), 0.0).astype(BF)
+                mixed = dot(expo, values)
+                total = mixed[:, head_width:]
+                value = mixed[:, :head_width] / total
+                out_ref[sl, lanes] = value.astype(BF)
+                rest_ref[sl, lanes] = (value - value.astype(BF).astype(F32)).astype(BF)
+                log_ref[sl, lanes] = jnp.log(total)
+
+    block = pl.BlockSpec((both, pair), lambda t: (0, t))
+    return call(
+        body,
+        (low // pair,),
+        [block] * 3 + [fixed((both, 1)), fixed((8, both))],
+        [block] * 3,
+        [shape_of((both, low), BF)] * 2 + [shape_of((both, low), F32)],
+        [],
+        4 * both * both * low,
+        14 * both * low,
+        (q_low, k_low, v_low, end_col, place_row),
+    )
+
+
+def attn_back(own, other, blocks, q_low, k_low, v_low, attn, rest, logs, q_raw, k_raw, hidden, scale_row,
+              place_col, end_row, head_width):
+    rows, width = own.shape
+    both, low = q_low.shape
+    pair = 2 * head_width
+    chunk = both // 4
+    steps = low // pair
+
+    def body(own_ref, other_ref, *refs):
+        w_refs, refs = refs[:16], refs[16:]
+        (q_ref, k_ref, v_ref, attn_ref, rest_ref, log_ref, qr_ref, kr_ref, hid_ref, scale_ref, place_ref, end_ref,
+         sums, out_own, out_other, keep, by_x, by_y, far_a, far_b, joined, weights, ds_ref, three_ref, acc) = refs
+        step = pl.program_id(0)
+
+        @pl.when(step == 0)
+        def _():
+            join_into(joined, own_ref, other_ref)
+
+        for side, when in ((0, step < 2), (1, step >= 2)):
+            @pl.when(when)
+            def _():
+                for i in range(4):
+                    rows_i = slice(i * pair, (i + 1) * pair)
+                    weights[rows_i, :low] = w_refs[4 * i + 2 * side][...]
+                    weights[rows_i, low:] = w_refs[4 * i + 2 * side + 1][...]
+
+        grad_pair = dot(joined[...], weights[3 * pair :, :], NT).astype(BF)
+        ends = end_ref[0:1, :]
+        lane = lax.broadcasted_iota(jnp.int32, (both, head_width), 1)
+        ones = jnp.ones((both, head_width), BF)
+
+        def spread(value):
+            high = value.astype(BF)
+            rest = value - high.astype(F32)
+            mid = rest.astype(BF)
+            small = (rest - mid.astype(F32)).astype(BF)
+            zero = jnp.zeros_like(high)
+            return jnp.where(lane == 0, high, jnp.where(lane == 1, mid, jnp.where(lane == 2, small, zero)))
+
+        def unit_back(raw, grad_unit):
+            raw = raw.astype(F32)
+            rate = lax.rsqrt(jnp.sum(raw * raw, axis=1, keepdims=True) + EPS_UNIT)
+            unit = raw * rate
+            cross = jnp.sum(grad_unit * unit, axis=1, keepdims=True)
+            return rate * (grad_unit - unit * cross), unit
+
+        for h in range(2):
+            lanes = slice(h * head_width, (h + 1) * head_width)
+            queries, keys, values, grads = q_ref[:, lanes], k_ref[:, lanes], v_ref[:, lanes], grad_pair[:, lanes]
+            mixed = attn_ref[:, lanes].astype(F32) + rest_ref[:, lanes].astype(F32)
+            delta = jnp.sum(grads.astype(F32) * mixed, axis=1, keepdims=True)
+            q_wide = jnp.concatenate((queries, spread(-log_ref[:, lanes])), axis=1)
+            g_wide = jnp.concatenate((grads, spread(jnp.broadcast_to(-delta, (both, head_width)))), axis=1)
+            k_wide = jnp.concatenate((keys, ones), axis=1)
+            v_wide = jnp.concatenate((values, ones), axis=1)
+            dk_parts, dv_parts = [], []
+            for c in range(4):
+                sl = slice(c * chunk, (c + 1) * chunk)
+                scores = dot(k_wide[sl], q_wide, NT)
+                probs = jnp.where(place_ref[sl, :] < ends, jnp.exp(scores), 0.0)
+                d_probs = dot(v_wide[sl], g_wide, NT)
+                d_scores = (probs * d_probs).astype(BF)
+                ds_ref[sl, :] = d_scores
+                dv_parts.append(dot(probs.astype(BF), grads))
+                dk_parts.append(dot(d_scores, queries))
+            d_qn = dot(keys, ds_ref[...], TN).T
+            d_kn = jnp.concatenate(dk_parts, axis=0)
+            d_v = jnp.concatenate(dv_parts, axis=0).astype(BF)
+            d_q, unit_q = unit_back(qr_ref[:, lanes], d_qn * scale_ref[0:1, lanes])
+            d_k, _ = unit_back(kr_ref[:, lanes], d_kn)
+            d_q, d_k = d_q.astype(BF), d_k.astype(BF)
+            for i, value in enumerate((d_q, d_k, d_v)):
+                three_ref[:, i * pair + h * head_width : i * pair + (h + 1) * head_width] = value
+            for i, value in enumerate((d_q.astype(F32), d_v.astype(F32), d_qn * unit_q)):
+                sums[i : i + 1, lanes] = jnp.sum(value, axis=0, keepdims=True)
+
+        for lanes in (slice(0, low), slice(low, width)):
+            part = dot(three_ref[...], weights[: 3 * pair, lanes])
+
+            @pl.when(step == 0)
+            def _():
+                acc[:, lanes] = part
+
+            @pl.when(jnp.logical_and(step > 0, step < steps - 1))
+            def _():
+                acc[:, lanes] += part
+
+            @pl.when(step == steps - 1)
+            def _():
+                total = acc[:, lanes] + part
+                out_own[:, lanes] = total[:rows]
+                out_other[:, lanes] = total[rows:].astype(BF)
+
+        for i, lanes in enumerate((slice(0, low), slice(low, width))):
+            three = dot(three_ref[...], hid_ref[:, lanes], TN).astype(BF)
+            proj = dot(attn_ref[...], joined[:, lanes], TN).astype(BF)
+            grads = [three[j * pair : (j + 1) * pair] for j in range(3)] + [proj]
+
+            @pl.when(step < 2)
+            def _():
+                target = keep if i == 0 else by_y
+                for j in range(4):
+                    target[j, 0] = grads[j]
+
+            @pl.when(step >= 2)
+            def _():
+                for j in range(4):
+                    if i == 0:
+                        by_x[j, 0] = grads[j]
+                    else:
+                        (far_a if j < 2 else far_b)[j % 2, 0] = grads[j]
+
+    def early(row):
+        return pl.BlockSpec((pair, low), lambda t: (row + jnp.minimum(t, 1), 0))
+
+    def late(row):
+        return pl.BlockSpec((pair, low), lambda t: (row + jnp.maximum(t - 2, 0), 0))
+
+    g, gx, gy, ga, gb = blocks
+    w_specs, w_args = [], []
+    for i in range(4):
+        w_specs += [early(2 * i), early(2 * i), late(2 * i), late(2 * (i % 2))]
+        w_args += [g, gy, gx, ga if i < 2 else gb]
+    block = pl.BlockSpec((both, pair), lambda t: (0, t))
+    row = pl.BlockSpec((8, pair), lambda t: (0, t))
+    first = pl.BlockSpec((4, 1, pair, low), lambda t: (0, jnp.minimum(t, 1), 0, 0))
+    second = pl.BlockSpec((4, 1, pair, low), lambda t: (0, jnp.maximum(t - 2, 0), 0, 0))
+    halves = pl.BlockSpec((2, 1, pair, low), lambda t: (0, jnp.maximum(t - 2, 0), 0, 0))
+    whole, half = shape_of((4, 2, pair, low), BF), shape_of((2, 2, pair, low), BF)
+    found = call(
+        body,
+        (steps,),
+        [fixed((rows, width))] * 2 + w_specs + [block] * 8
+        + [fixed((both, width)), row, fixed((both, 1)), fixed((8, both))],
+        [row, fixed((rows, width)), fixed((rows, width)), first, second, first, halves, halves],
+        [shape_of((8, low), F32), shape_of((rows, width), F32), shape_of((rows, width), BF)]
+        + [whole, whole, whole, half, half],
+        [
+            pltpu.VMEM((both, width), BF), pltpu.VMEM((4 * pair, width), BF), pltpu.VMEM((both, both), BF),
+            pltpu.VMEM((both, 3 * pair), BF), pltpu.VMEM((both, width), F32),
+        ],
+        10 * both * both * low + 16 * both * width * low,
+        24 * both * low + 8 * both * width,
+        (own, other, *w_args, q_low, k_low, v_low, attn, rest, logs, q_raw, k_raw, hidden, scale_row,
+         place_col, end_row),
+    )
+    return found[:3], found[3:]
+
+
+def attn_down(attn, blocks):
+    both, low = attn.shape
+    rows, width, tile = both // 2, 2 * low, low // 2
+
+    def body(attn_ref, g, gx, gy, gb, own, other):
+        for lanes, first, second in ((slice(0, low), g, gx), (slice(low, width), gy, gb)):
+            value = dot(attn_ref[:, :tile], first[...]) + dot(attn_ref[:, tile:], second[...])
+            own[:, lanes] = value[:rows]
+            other[:, lanes] = value[rows:].astype(BF)
+
+    last = pl.BlockSpec((tile, low), lambda t: (3, 0))
+    g, gx, gy, _, gb = blocks
+    return call(
+        body,
+        (1,),
+        [fixed((both, low)), last, last, last, pl.BlockSpec((tile, low), lambda t: (1, 0))],
+        [fixed((rows, width))] * 2,
+        [shape_of((rows, width), F32), shape_of((rows, width), BF)],
+        [],
+        2 * both * width * low,
+        2 * low * width + 2 * both * low + 6 * rows * width,
+        (attn, g, gx, gy, gb),
+    )
+
+
+def mix(own, got, state, vectors, last):
+    rows, width = own.shape
+    part = rows // 2
+
+    def body(own_ref, got_ref, state_ref, vec, branch_ref, next_ref, hid_ref):
+        def one(sl):
+            branch = own_ref[sl, :] + got_ref[sl, :].astype(F32) + vec[0:1, :]
+            branch_ref[sl, :] = branch.astype(BF)
+            value = state_ref[sl, :] + vec[1:2, :] * branch
+            next_ref[sl, :] = value
+            if last:
+                hid_ref[sl, :] = value.astype(BF)
+            else:
+                mean = jnp.mean(value, axis=1, keepdims=True)
+                spread = jnp.mean(value * value, axis=1, keepdims=True) - mean * mean
+                normed = (value - mean) * lax.rsqrt(spread + EPS_NORM)
+                hid_ref[sl, :] = (normed * vec[2:3, :] + vec[3:4, :]).astype(BF)
+
+        row_loop(part, 16, one, unroll=11)
+
+    block = pl.BlockSpec((part, width), lambda t: (t, 0))
+    return call(
+        body,
+        (2,),
+        [block] * 3 + [fixed((8, width))],
+        [block] * 3,
+        [shape_of((rows, width), BF), shape_of((rows, width), F32), shape_of((rows, width), BF)],
+        [],
+        20 * rows * width,
+        18 * rows * width,
+        (own, got, state, vectors),
+    )
+
+
+def mix_back(own, got, state, grad, branch, vectors):
+    rows, width = own.shape
+    part = rows // 2
+
+    def body(own_ref, got_ref, state_ref, grad_ref, branch_ref, vec, next_ref, low_ref, sums):
+        @pl.when(pl.program_id(0) == 0)
+        def _():
+            sums[...] = jnp.zeros_like(sums)
+
+        def add(i, value):
+            sums[8 * i : 8 * i + 8, :] += value[:8] + value[8:]
+
+        def one(sl):
+            d_hid = own_ref[sl, :] + got_ref[sl, :].astype(F32)
+            value = state_ref[sl, :]
+            mean = jnp.mean(value, axis=1, keepdims=True)
+            spread = jnp.mean(value * value, axis=1, keepdims=True) - mean * mean
+            rate = lax.rsqrt(spread + EPS_NORM)
+            normed = (value - mean) * rate
+            add(0, d_hid * normed)
+            add(1, d_hid)
+            d_norm = d_hid * vec[0:1, :]
+            means = jnp.mean(d_norm, axis=1, keepdims=True)
+            crosses = jnp.mean(d_norm * normed, axis=1, keepdims=True)
+            total = grad_ref[sl, :] + rate * (d_norm - means - normed * crosses)
+            next_ref[sl, :] = total
+            add(2, total * branch_ref[sl, :].astype(F32))
+            low = (total * vec[1:2, :]).astype(BF)
+            low_ref[sl, :] = low
+            add(3, low.astype(F32))
+
+        row_loop(part, 16, one, unroll=11)
+
+    block = pl.BlockSpec((part, width), lambda t: (t, 0))
+    return call(
+        body,
+        (2,),
+        [block] * 5 + [fixed((8, width))],
+        [block] * 2 + [fixed((32, width))],
+        [shape_of((rows, width), F32), shape_of((rows, width), BF), shape_of((32, width), F32)],
+        [],
+        30 * rows * width,
+        20 * rows * width,
+        (own, got, state, grad, branch, vectors),
+    )
+
+
+def gather_blocks(rows):
+    half = rows.shape[0] // 2
+    by_x = across(rows, "x")
+    by_y = across(rows, "y")
+    first = across(by_x[:half], "y")
+    second = across(by_y[half:], "x")
+    return rows, by_x, by_y, first, second
+
+
+def scatter_blocks(blocks, parts, z_size):
+    keep, by_x, by_y, far_a, far_b = [v.reshape(-1, v.shape[-1]) for v in blocks]
+    half = far_a.shape[0]
+    got_a, got_b = across(far_a, "y"), across(far_b, "x")
+
+    def added(block, got, start):
+        part = block[start : start + half].astype(F32) + got.astype(F32)
+        return lax.dynamic_update_slice_in_dim(block, part.astype(BF), start, 0)
+
+    got_x = across(added(by_x, got_a, 0), "x")
+    got_y = across(added(by_y, got_b, half), "y")
+    total = keep.astype(F32) + got_x.astype(F32) + got_y.astype(F32)
+    total = jnp.swapaxes(total.astype(BF).reshape(parts, z_size, -1, keep.shape[1]), 0, 1)
+    total = total.reshape(z_size, -1, keep.shape[1])
+    return lax.psum_scatter(total, "z", scatter_dimension=0, tiled=False)
+
+
+def eight_rows(*rows):
+    rows = [r.reshape(1, -1) for r in rows]
+    return jnp.concatenate(rows + [jnp.zeros_like(rows[0])] * (8 - len(rows)), axis=0)
+
+
+def on_pair(
+    hidden_in, cond, scale_sizes, w_ada, b_ada, w_qkv, b_qkv, head_scale,
+    w_proj, b_proj, w_fc1, b_fc1, w_fc2, b_fc2, grad_out,
+):
+    y = lax.axis_index("y")
+    core = lax.axis_index("core")
+    z = lax.axis_index("z")
+    x = lax.axis_index("x")
+    layer_count = w_ada.shape[0]
+    seq_row, width = cond.shape
+    rows_dev = hidden_in.shape[0]
+    rows_pad = -(-rows_dev // 32) * 32
+    d_col = b_qkv.shape[2]
+    head_width = d_col // head_scale.shape[1]
+    y_size, z_size, x_size = (lax.axis_size(a) for a in ("y", "z", "x"))
+    heads = z_size * x_size
+    low = width // 2
+    rows_d = w_qkv.shape[1]
+    hid_dev = w_fc1.shape[2]
+    hid_core = hid_dev // 2
+
+    qkv_t = jnp.transpose(w_qkv, (0, 2, 3, 1)).reshape(layer_count, 3, 2, head_width, rows_d)
+    qkv_t = jnp.transpose(qkv_t, (0, 2, 1, 3, 4)).reshape(layer_count, 6 * head_width, rows_d)
+    fc1_t = jnp.transpose(w_fc1, (0, 2, 1))
+    three, four = 3 * head_width, 4 * head_width
+    halves = [
+        jnp.concatenate(parts, axis=1)
+        for parts in (
+            (qkv_t[:, :three], w_proj[:, :head_width], fc1_t[:, :hid_core], w_fc2[:, :hid_core]),
+            (qkv_t[:, three:], w_proj[:, head_width:], fc1_t[:, hid_core:], w_fc2[:, hid_core:]),
+        )
+    ]
+    kept = jnp.where(core == 0, halves[0], halves[1])
+    came = sibling(jnp.where(core == 0, halves[1], halves[0]))
+    shards = jnp.concatenate(
+        (jnp.where(core == 0, kept, came), jnp.where(core == 0, came, kept)), axis=2
+    )
+    cuts = (0, four, four + hid_core, four + 2 * hid_core)
+
+    def gather(l, i):
+        by_z = lax.all_gather(shards[l, cuts[i] : cuts[i + 1]], "z", axis=0, tiled=False)
+        if i == 0:
+            by_z = jnp.swapaxes(by_z.reshape(z_size, 4, head_width, low), 0, 1)
+        return gather_blocks(by_z.reshape(-1, low))
+
+    blocks = [[gather(l, i) for i in range(3)] for l in range(layer_count)]
+
+    cond_low = jax.nn.silu(cond.astype(F32)).astype(BF)
+    silu_rows = lax.all_gather(cond_low, ("y", "core"), axis=0, tiled=True)
+    row = y * 2 + core
+    silu_own = lax.dynamic_slice_in_dim(silu_rows, row * rows_d, rows_d, axis=1)
+    seqs = silu_rows.shape[0]
+    ada_size = layer_count * 6 * d_col
+    part = dot(silu_own, jnp.transpose(w_ada, (1, 0, 2, 3)).reshape(rows_d, ada_size))
+    part = part + jnp.where(row == 0, b_ada.astype(F32).reshape(1, ada_size), 0.0)
+    smalls = (b_qkv, b_fc1, b_proj, b_fc2, head_scale)
+    sizes = [v.size for v in smalls]
+    offs = [sum(sizes[:i]) for i in range(6)]
+    n_rows = y_size * 2
+    quarter = -(-offs[5] // (n_rows * 128)) * 128
+    small = jnp.concatenate([v.reshape(-1).astype(F32) for v in smalls])
+    small = jnp.pad(small, (0, n_rows * quarter - offs[5])).reshape(n_rows, quarter)
+    small = lax.dynamic_index_in_dim(small, row, axis=0, keepdims=True)
+    part = jnp.concatenate((part, jnp.broadcast_to(small, (seqs, quarter))), axis=1)
+    to_all = jnp.swapaxes(part.reshape(y_size, x_size, z_size, -1), 1, 2)
+    to_all = jnp.broadcast_to(to_all[:, None], (y_size, 2) + to_all.shape[1:])
+    from_all = lax.all_to_all(
+        to_all.reshape(n_rows * z_size * x_size, -1), ("y", "core", "z", "x"),
+        split_axis=0, concat_axis=0, tiled=True,
+    ).reshape(n_rows, z_size, x_size, -1)
+    ada = jnp.sum(from_all[..., :ada_size], axis=0).reshape(z_size * x_size, layer_count, 6, d_col)
+    ada = turned(jnp.transpose(ada, (1, 2, 0, 3)).reshape(layer_count, 6, width), y, 2)
+    small = jnp.transpose(from_all[..., ada_size:], (1, 2, 0, 3)).reshape(z_size, x_size, -1)
+    s_qkv, s_fc1, s_proj, s_fc2, s_scale = [small[:, :, offs[i] : offs[i + 1]] for i in range(5)]
+
+    def by_core(values, shape, axis):
+        values = values.reshape((z_size, x_size) + shape)
+        values = lax.dynamic_index_in_dim(values, core, axis=axis, keepdims=False)
+        return turned(jnp.swapaxes(values, 0, 1), x, 0)
+
+    def by_d(values):
+        values = jnp.swapaxes(values.reshape(z_size * x_size, layer_count, d_col), 0, 1)
+        return turned(values.reshape(layer_count, width), y, 1)
+
+    bias_qkv = by_core(s_qkv, (layer_count, 2, 2, head_width), 4)
+    bias_qkv = jnp.transpose(bias_qkv, (2, 3, 0, 1, 4)).reshape(layer_count, 2, low)
+    scales = by_core(s_scale, (layer_count, 2), 3)
+    scales = jnp.transpose(scales, (2, 0, 1)).reshape(layer_count, heads)
+    scales = jnp.repeat(scales, head_width, axis=1)
+    bias_fc1 = by_core(s_fc1, (layer_count, 2, hid_core), 3)
+    bias_fc1 = jnp.transpose(bias_fc1, (2, 0, 1, 3)).reshape(layer_count, 1, -1)
+    bias_proj, bias_fc2 = by_d(s_proj), by_d(s_fc2)
+
+    sizes_f = scale_sizes.astype(F32)
+    sizes_f = jnp.where(core == x, sizes_f, sibling(sizes_f))
+    own_sizes = lax.dynamic_index_in_dim(sizes_f, z, axis=0, keepdims=False).astype(jnp.int32)
+    index = jnp.arange(rows_pad, dtype=jnp.int32)
+    places = jnp.concatenate((core * rows_dev + index, (1 - core) * rows_dev + index))
+    starts = jnp.cumsum(own_sizes) - own_sizes
+    ends = jnp.sum(jnp.where(starts[None, :] <= places[:, None], own_sizes[None, :], 0), axis=1)
+    real = jnp.concatenate((index, index)) < rows_dev
+    key_places = jnp.where(real, places, 1 << 20).astype(F32)
+    ends = ends.astype(F32)
+    place_col, end_col = key_places[:, None], ends[:, None]
+    place_row, end_row = eight_rows(key_places), eight_rows(ends)
+    ones = head_ones(low // 2, head_width)
+
+    def own_tokens(values):
+        return jnp.pad(turned(trade(values), y, 1), ((0, rows_pad - rows_dev), (0, 0)))
+
+    state = own_tokens(hidden_in).astype(F32)
+    grad = own_tokens(grad_out).astype(F32)
+    hidden = (normalize(state)[0] * (1.0 + ada[0, 2][None]) + ada[0, 4][None]).astype(BF)
+    saved = []
+    for l in range(layer_count):
+        gamma1, gamma2, scale1, scale2, shift1, shift2 = [ada[l, i] for i in range(6)]
+        vectors = eight_rows(bias_qkv[l, 0], bias_qkv[l, 1], scales[l])
+        joined1, q_raw, k_raw, q_low, k_low, v_low = qkv_up(
+            hidden, sibling(hidden), blocks[l][0], vectors, ones
+        )
+        attn, rest, logs = attn_mix(q_low, k_low, v_low, end_col, place_row, head_width)
+        own, send = attn_down(attn, blocks[l][0])
+        branch, middle, hidden = mix(
+            own, sibling(send), state, eight_rows(bias_proj[l], gamma1, 1.0 + scale2, shift2), False
+        )
+        joined2, act, slope = fc_up(hidden, sibling(hidden), blocks[l][1], bias_fc1[l])
+        own, send = fc_down(act, blocks[l][2])
+        last = l == layer_count - 1
+        after = ada[l if last else l + 1]
+        feed, later, hidden = mix(
+            own, sibling(send), middle, eight_rows(bias_fc2[l], gamma2, 1.0 + after[2], after[4]), last
+        )
+        saved.append(
+            (joined1, q_raw, k_raw, q_low, k_low, v_low, logs, attn, rest, branch, middle, joined2, act, slope, feed, state)
+        )
+        state = later
+    mixed = hidden
+
+    top = layer_count - 1
+    d_ada = [[None] * 6 for _ in range(layer_count)]
+    d_biases = [[None] * 5 for _ in range(layer_count)]
+    d_weights = [None] * layer_count
+    fold = lambda sums: jnp.sum(sums.reshape(-1, 8, sums.shape[1]), axis=1)
+    d_low = (grad * ada[top, 1][None]).astype(BF)
+    d_ada[top][1] = jnp.sum(grad * saved[top][-2].astype(F32), axis=0)
+    d_biases[top][1] = jnp.sum(d_low.astype(F32), axis=0)
+    for l in reversed(range(layer_count)):
+        gamma1, gamma2, scale1, scale2, shift1, shift2 = [ada[l, i] for i in range(6)]
+        (joined1, q_raw, k_raw, q_low, k_low, v_low, logs, attn, rest, branch, middle, joined2, act, slope, feed, state) = saved[l]
+        (sums_pre, own, send), two, one = fc_back(
+            d_low, sibling(d_low), blocks[l][2], blocks[l][1], slope, act, joined2
+        )
+        g_two = scatter_blocks(two, 1, z_size)
+        g_one = scatter_blocks(one, 1, z_size)
+        d_middle, d_low, sums = mix_back(
+            own, sibling(send), middle, grad, branch, eight_rows(1.0 + scale2, gamma1)
+        )
+        d_ada[l][3], d_ada[l][5], d_ada[l][0], d_biases[l][0] = fold(sums)
+        (sums_qkv, own, send), four_parts = attn_back(
+            d_low, sibling(d_low), blocks[l][0], q_low, k_low, v_low, attn, rest, logs, q_raw, k_raw, joined1,
+            eight_rows(scales[l]), place_col, end_row, head_width,
+        )
+        g_attn = scatter_blocks(four_parts, 4, z_size)
+        before = max(l - 1, 0)
+        grad, d_low, sums = mix_back(
+            own, sibling(send), state, d_middle, saved[before][-2], eight_rows(1.0 + scale1, ada[before, 1])
+        )
+        sums = fold(sums)
+        d_ada[l][2], d_ada[l][4] = sums[0], sums[1]
+        if l > 0:
+            d_ada[l - 1][1], d_biases[l - 1][1] = sums[2], sums[3]
+        d_head = jnp.sum(sums_qkv[2].reshape(heads, head_width), axis=1)
+        d_biases[l][2:] = sums_qkv[:2], fold(sums_pre)[0], d_head
+        d_weights[l] = jnp.concatenate((g_attn, g_one, g_two), axis=0)
+
+    def by_col(values):
+        values = turned(values, y, values.ndim - 1)
+        values = values.reshape(values.shape[:-1] + (z_size, x_size, d_col))
+        return jnp.moveaxis(values, (-3, -2), (0, 1)).reshape(z_size, x_size, -1)
+
+    def by_hidden(values):
+        return jnp.swapaxes(turned(values, x, 0), 0, 1).reshape(z_size, x_size, -1)
+
+    packs = [by_col(jnp.stack([jnp.stack(v) for v in d_ada]))]
+    for l in range(layer_count):
+        db_proj, db_fc2, db_qkv, db_fc1, d_head = d_biases[l]
+        packs.append(by_col(db_proj))
+        packs.append(by_col(db_fc2))
+        packs.append(by_hidden(jnp.moveaxis(db_qkv.reshape(2, x_size, z_size, head_width), 0, 2)))
+        packs.append(by_hidden(db_fc1.reshape(x_size, z_size, hid_core)))
+        packs.append(by_hidden(d_head.reshape(x_size, z_size, 1)))
+    lens = [p.shape[2] for p in packs]
+    pack = jnp.concatenate(packs, axis=2)
+    pack = jnp.broadcast_to(pack[None], (n_rows,) + pack.shape)
+    got = lax.all_to_all(
+        pack.reshape(n_rows * z_size * x_size, -1), ("y", "core", "z", "x"),
+        split_axis=0, concat_axis=0, tiled=True,
+    ).reshape(y_size, 2, z_size, x_size, -1)
+    pos = lens[0]
+    d_ada_all = jnp.sum(got[..., :pos], axis=1)
+    d_ada_all = jnp.swapaxes(d_ada_all, 1, 2).reshape(seqs, -1).astype(BF)
+    out_b_ada = jnp.sum(d_ada_all.astype(F32), axis=0).reshape(layer_count, 6, d_col)
+    out_w_ada = dot(silu_own, d_ada_all, TN).reshape(rows_d, layer_count, 6, d_col)
+    out_w_ada = jnp.swapaxes(out_w_ada, 0, 1)
+    sums = jnp.sum(got[..., pos:], axis=(0, 2, 3))
+    outs = [[] for _ in range(5)]
+    pos = 0
+    for l in range(layer_count):
+        for i in range(5):
+            count = lens[1 + 5 * l + i]
+            outs[i].append(sums[:, pos : pos + count])
+            pos += count
+    out_b_proj = jnp.stack([v[0] + v[1] for v in outs[0]])
+    out_b_fc2 = jnp.stack([v[0] + v[1] for v in outs[1]])
+    out_b_qkv = jnp.stack(
+        [jnp.swapaxes(v.reshape(2, 2, head_width), 0, 1).reshape(2, d_col) for v in outs[2]]
+    )
+    out_b_fc1 = jnp.stack([v.reshape(-1) for v in outs[3]])
+    out_scale = jnp.stack([v.reshape(-1) for v in outs[4]])
+
+    own = jnp.stack(d_weights)
+    kept = jnp.where(core == 0, own[:, :, :rows_d], own[:, :, rows_d:])
+    came = sibling(jnp.where(core == 0, own[:, :, rows_d:], own[:, :, :rows_d]))
+    first = jnp.where(core == 0, kept, came).astype(F32)
+    second = jnp.where(core == 0, came, kept).astype(F32)
+    wq = jnp.stack((first[:, :three], second[:, :three]), axis=1)
+    wq = wq.reshape(layer_count, 2, 3, head_width, rows_d)
+    out_w_qkv = jnp.transpose(wq, (0, 4, 2, 1, 3)).reshape(layer_count, rows_d, 3, d_col)
+
+    def pick(i, j):
+        return jnp.concatenate((first[:, i:j], second[:, i:j]), axis=1)
+
+    def given_back(values):
+        return trade(turned(values[:rows_dev], y, 1))
+
+    return (
+        given_back(mixed), given_back(grad), out_w_ada, out_b_ada, out_w_qkv, out_b_qkv, out_scale,
+        pick(three, four), out_b_proj, jnp.swapaxes(pick(cuts[1], cuts[2]), 1, 2), out_b_fc1,
+        pick(cuts[2], cuts[3]), out_b_fc2,
+    )
+
+
 def solution(mesh):
+    rows, cols = mesh.devices.shape
+    row, col, body, used = ("row",), ("col",), on_device, mesh
+    if rows == 4 and cols == 8:
+        used = jax.sharding.Mesh(
+            mesh.devices.reshape(rows // 2, 2, cols // 2, 2), ("y", "core", "z", "x")
+        )
+        row, col, body = ("y", "core"), ("z", "x"), on_pair
+    tokens = P(row + col, None)
+    out_weights = (
+        P(None, row, None, col),
+        P(None, None, col),
+        P(None, row, None, col),
+        P(None, None, col),
+        P(None, col),
+        P(None, col, row),
+        P(None, col),
+        P(None, row, col),
+        P(None, col),
+        P(None, col, row),
+        P(None, col),
+    )
     return jax.shard_map(
-        on_device,
-        mesh=mesh,
-        in_specs=(
-            P(("row", "col"), None),
-            P("row", None),
-            P("row", None),
-            P(None, "row", None, "col"),
-            P(None, None, "col"),
-            P(None, "row", None, "col"),
-            P(None, None, "col"),
-            P(None, "col"),
-            P(None, "col", "row"),
-            P(None, "col"),
-            P(None, "row", "col"),
-            P(None, "col"),
-            P(None, "col", "row"),
-            P(None, "col"),
-            P(("row", "col"), None),
-        ),
-        out_specs=(
-            P(("row", "col"), None),
-            P(("row", "col"), None),
-            P(None, "row", None, "col"),
-            P(None, None, "col"),
-            P(None, "row", None, "col"),
-            P(None, None, "col"),
-            P(None, "col"),
-            P(None, "col", "row"),
-            P(None, "col"),
-            P(None, "row", "col"),
-            P(None, "col"),
-            P(None, "col", "row"),
-            P(None, "col"),
-        ),
+        body,
+        mesh=used,
+        in_specs=(tokens, P(row, None), P(row, None)) + out_weights + (tokens,),
+        out_specs=(tokens, tokens) + out_weights,
         check_vma=False,
     )

time: 2730 us -> 717 us (0.26)
  waiting for transfers between devices: 1450 us -> 208 us
  local copies, waits for them, and re-layouts: 450 us -> 63.2 us
  matrix products: 330 us -> 1.84 us
  blocking collectives: 308 us -> 6.07 us
  Pallas kernels: 0 us -> 259 us
  other arithmetic: 129 us -> 62.7 us
  starting transfers between devices: 27.7 us -> 91.4 us
    all_gather x16 -> x6, waiting for transfers between devices: 1020 us -> 47.4 us  [gather(): lax.all_gather(shards[l, cuts[i]:cuts[i + 1]], 'z', axis=0, tiled=False)]
    dot_general x108 -> x2, matrix products: 330 us -> 1.84 us  [dot(): return lax.dot_general(left, right, dims, preferred_element_type=F32)]
    pallas_call x0 -> x22, Pallas kernels: none -> 259 us  [call(): pl.pallas_call(body, grid=grid, in_specs=in_specs, out_specs=out_specs, o...]
    dynamic_update_slice x48 -> x0, local copies, waits for them, and re-layouts: 189 us -> none  [on_device(): attended, log_total = lax.map(attend, (q_low, k_low, v_low, ends))]
    all_to_all x6 -> x2, waiting for transfers between devices: 188 us -> 16.7 us  [the longest x1 16.7 us: on_pair(): lax.all_to_all(pack.reshape(n_rows * z_size * x_size, -1), ('y', 'core',...]
    all_gather x4 -> x1, blocking collectives: 165 us -> 6.07 us  [on_pair(): silu_rows = lax.all_gather(cond_low, ('y', 'core'), axis=0, tiled=True)]
    ppermute x0 -> x71, waiting for transfers between devices: none -> 143 us  [the longest x48 140 us: across(): return lax.ppermute(values, axis, [(0, 1), (1, 0)])]
    reduce_scatter x5 -> x6, waiting for transfers between devices: 141 us -> 0.91 us  [scatter_blocks(): return lax.psum_scatter(total, 'z', scatter_dimension=0, tiled=False)]
  transfers between devices with their start and end apart: 30 -> 85, of which waited for: 24 -> 27; matrix products, arithmetic and copies ran while one was open for 18% -> 14% of each run, Pallas kernels for 0% -> 36%
where the time goes in v2:
time: 717 us; the launch traced here: 708 us
  Pallas kernels  259 us (36%)
  waiting for transfers between devices  208 us (29%)
  starting transfers between devices  91.4 us (13%)
  local copies, waits for them, and re-layouts  63.2 us (9%)
  other arithmetic  62.7 us (9%)
  between operations  16.5 us (2%)
    pallas_call x22, Pallas kernels, call(): pl.pallas_call(body, grid=grid, in_specs=in_specs, out_specs=out_specs, o...  259 us
    ppermute x48, waiting for transfers between devices, across(): return lax.ppermute(values, axis, [(0, 1), (1, 0)])  140 us
    all_gather x6, waiting for transfers between devices, gather(): lax.all_gather(shards[l, cuts[i]:cuts[i + 1]], 'z', axis=0, tiled=False)  47.4 us
    ppermute x19, starting transfers between devices, sibling(): return lax.ppermute(values, 'core', [(0, 1), (1, 0)])  32.7 us
    ppermute x48, starting transfers between devices, across(): return lax.ppermute(values, axis, [(0, 1), (1, 0)])  31.9 us
    dynamic_update_slice x12, other arithmetic, added(): return lax.dynamic_update_slice_in_dim(block, part.astype(BF), start, 0)  24.6 us
    unnamed x161, local copies, waits for them, and re-layouts  20.9 us
    all_to_all x1, waiting for transfers between devices, on_pair(): lax.all_to_all(pack.reshape(n_rows * z_size * x_size, -1), ('y', 'core',...  16.7 us
  transfers between devices with their start and end apart: 85, of which 27 were waited for; matrix products, arithmetic and copies ran while one was open for 14% of the time, Pallas kernels for 36%

profile of v2, /device:TPU:1, one launch (start us, length us, event | category | flops | bytes accessed | tf_op | source)
XLA Modules:
  0.0 708.1 jit_solution(5956266088776218354)
XLA Ops:
  8.8 6.1 all-gather
  17.6 6.2 all-to-all-start
  42.1 20.8 %all-gather.8.cloned.1.call-done = bf16[4,256,512]{2,1,0:T(8,128)(2,1)} async-done(((bf16[1,256,512]{2,1,0:T(8,128)(2,1)}), bf16[4,256,512]{2,1,0:T(8,128)(2,1)}) %all-gather.8.cloned.1.call-update) | async-done | bytes 1048592 | tf_op jit(solution)/shard_map/all_gather | solution.py:1101
  70.1 18.2 %collective-permute-done.3.gx.refs_2_.refs_6_.refs_10_.refs_14_ = bf16[1024,512]{1,0:T(8,128)(2,1)S(1)} collective-permute-done((bf16[1024,512]{1,0:T(8,128)(2,1)S(1)}, bf16[1024,512]{1,0:T(8,128)(2,1)S(1)}, u32[]{:S(2)}, u32[]{:S(2)}) %collective-permute-start.3) | collective-permute-done | bytes 1048608 | tf_op jit(solution)/shard_map/ppermute | solution.py:415
  94.9 26.6 %all-gather.12.cloned.1.call-done = bf16[4,256,512]{2,1,0:T(8,128)(2,1)} async-done(((bf16[1,256,512]{2,1,0:T(8,128)(2,1)}), bf16[4,256,512]{2,1,0:T(8,128)(2,1)}) %all-gather.12.cloned.1.call-update) | async-done | bytes 1048592 | tf_op jit(solution)/shard_map/all_gather | solution.py:1101
  124.7 10.9 %shard_map.246 = (bf16[704,1024]{1,0:T(8,128)(2,1)}, bf16[704,512]{1,0:T(8,128)(2,1)}, bf16[704,512]{1,0:T(8,128)(2,1)}, bf16[704,512]{1,0:T(8,128)(2,1)}, bf16[...) custom-call(bf16[352,1024]{1,0:T(8,128)(2,1)} %add_convert_fusion.4.own_ref, ...), custom_call_target="tpu_custom_call" | custom-call | flops 2214592512 | bytes 11075584 | tf_op jit(solution)/shard_map/pallas_call | solution.py:436
  135.6 11.0 %shard_map.247 = (bf16[704,512]{1,0:T(8,128)(2,1)}, bf16[704,512]{1,0:T(8,128)(2,1)}, f32[704,512]{1,0:T(8,128)}) custom-call(bf16[704,512]{1,0:T(8,128)(2,1)} %get-tuple-element.109.q_ref.refs_16_, bf16[704,512]{1,0:T(8,128)(2,1)} %get-tuple-element.110.k_ref.refs_17_, bf16[704,512]{1,0:T(8,128)(2,1)} %get-tuple-element.111.v_ref.refs_18_, ...), custom_call_target="tpu_custom_call" | custom-call | flops 1015021568 | bytes 5046272 | tf_op jit(solution)/shard_map/pallas_call | solution.py:436
  175.7 10.5 %shard_map.250 = (bf16[704,1024]{1,0:T(8,128)(2,1)}, bf16[704,2048]{1,0:T(8,128)(2,1)}, bf16[704,2048]{1,0:T(8,128)(2,1)}) custom-call(bf16[352,1024]{1,0:T(8,128)(2,1)} %get-tuple-element.115.own_ref, bf16[352,1024]{1,0:T(8,128)(2,1)} %collective-permute-done.9.other_ref, bf16[1024,512]{1,0:T(8,128)(2,1)} %bitcast.357, ...), custom_call_target="tpu_custom_call" | custom-call | flops 2952790016 | bytes 14286848 | tf_op jit(solution)/shard_map/pallas_call | solution.py:436
  186.2 7.6 %shard_map.251 = (f32[352,1024]{1,0:T(8,128)}, bf16[352,1024]{1,0:T(8,128)(2,1)}) custom-call(bf16[704,2048]{1,0:T(8,128)(2,1)} %get-tuple-element.116.left_ref.act_ref, bf16[1024,512]{1,0:T(8,128)(2,1)} %bitcast.361, bf16[1024,512]{1,0:T(8,128)(2,1)} %collective-permute-done.14.gx.ugx, bf16[1024,512]{1,0:T(8,128)(2,1)} %collective-permute-done.15.gy.ugy, ...), custom_call_target="tpu_custom_call" | custom-call | flops 2952790016 | bytes 9240576 | tf_op jit(solution)/shard_map/pallas_call | solution.py:436
  203.0 5.2 collective-permute-done.20.gx.refs_2_.refs_6_.refs_10_.refs_14_
  213.0 8.2 %collective-permute-done.22.ga.refs_3_.refs_7_ = bf16[512,512]{1,0:T(8,128)(2,1)} collective-permute-done((bf16[512,512]{1,0:T(8,128)(2,1)}, bf16[512,512]{1,0:T(8,128)(2,1)}, u32[]{:S(2)}, u32[]{:S(2)}) %collective-permute-start.22) | collective-permute-done | bytes 524320 | tf_op jit(solution)/shard_map/ppermute | solution.py:415
  222.9 10.9 %shard_map.253 = (bf16[704,1024]{1,0:T(8,128)(2,1)}, bf16[704,512]{1,0:T(8,128)(2,1)}, bf16[704,512]{1,0:T(8,128)(2,1)}, bf16[704,512]{1,0:T(8,128)(2,1)}, bf16[...) custom-call(bf16[352,1024]{1,0:T(8,128)(2,1)} %get-tuple-element.120.own_ref, ...), custom_call_target="tpu_custom_call" | custom-call | flops 2214592512 | bytes 11075584 | tf_op jit(solution)/shard_map/pallas_call | solution.py:436
  233.8 11.1 %shard_map.254 = (bf16[704,512]{1,0:T(8,128)(2,1)}, bf16[704,512]{1,0:T(8,128)(2,1)}, f32[704,512]{1,0:T(8,128)}) custom-call(bf16[704,512]{1,0:T(8,128)(2,1)} %get-tuple-element.121.q_ref.refs_16_, bf16[704,512]{1,0:T(8,128)(2,1)} %get-tuple-element.122.k_ref.refs_17_, bf16[704,512]{1,0:T(8,128)(2,1)} %get-tuple-element.123.v_ref.refs_18_, ...), custom_call_target="tpu_custom_call" | custom-call | flops 1015021568 | bytes 5046272 | tf_op jit(solution)/shard_map/pallas_call | solution.py:436
  248.5 5.0 collective-permute-start.24
  264.2 14.4 %collective-permute-done.30.gx.ugx = bf16[1024,512]{1,0:T(8,128)(2,1)} collective-permute-done((bf16[1024,512]{1,0:T(8,128)(2,1)}, bf16[1024,512]{1,0:T(8,128)(2,1)}, u32[]{:S(2)}, u32[]{:S(2)}) %collective-permute-start.30) | collective-permute-done | bytes 1048608 | tf_op jit(solution)/shard_map/ppermute | solution.py:415
  283.9 5.9 collective-permute-done.28.ga.dga
  289.9 5.0 collective-permute-start.36
  294.8 10.4 %shard_map.257 = (bf16[704,1024]{1,0:T(8,128)(2,1)}, bf16[704,2048]{1,0:T(8,128)(2,1)}, bf16[704,2048]{1,0:T(8,128)(2,1)}) custom-call(bf16[352,1024]{1,0:T(8,128)(2,1)} %get-tuple-element.128.own_ref, bf16[352,1024]{1,0:T(8,128)(2,1)} %collective-permute-done.25.other_ref, bf16[1024,512]{1,0:T(8,128)(2,1)} %bitcast.365, ...), custom_call_target="tpu_custom_call" | custom-call | flops 2952790016 | bytes 14286848 | tf_op jit(solution)/shard_map/pallas_call | solution.py:436
  305.3 7.6 %shard_map.258 = (f32[352,1024]{1,0:T(8,128)}, bf16[352,1024]{1,0:T(8,128)(2,1)}) custom-call(bf16[704,2048]{1,0:T(8,128)(2,1)} %get-tuple-element.129.left_ref.act_ref, bf16[1024,512]{1,0:T(8,128)(2,1)} %bitcast.369, bf16[1024,512]{1,0:T(8,128)(2,1)} %collective-permute-done.30.gx.ugx, bf16[1024,512]{1,0:T(8,128)(2,1)} %collective-permute-done.31.gy.ugy, ...), custom_call_target="tpu_custom_call" | custom-call | flops 2952790016 | bytes 9240576 | tf_op jit(solution)/shard_map/pallas_call | solution.py:436
  325.6 21.5 %shard_map.260 = (f32[8,2048]{1,0:T(8,128)}, f32[352,1024]{1,0:T(8,128)}, bf16[352,1024]{1,0:T(8,128)(2,1)}, bf16[1024,512]{1,0:T(8,128)(2,1)}, bf16[1024,512]{1...) custom-call(bf16[352,1024]{1,0:T(8,128)(2,1)} %copy-done.17, ...), custom_call_target="tpu_custom_call" | custom-call | flops 11811160064 | bytes 29032448 | tf_op jit(solution)/shard_map/pallas_call | solution.py:436
  352.1 8.7 %collective-permute-done.68 = bf16[512,512]{1,0:T(8,128)(2,1)S(1)} collective-permute-done((bf16[512,512]{1,0:T(8,128)(2,1)}, bf16[512,512]{1,0:T(8,128)(2,1)S(1)}, u32[]{:S(2)}, u32[]{:S(2)}) %collective-permute-start.68) | collective-permute-done | bytes 524320 | tf_op jit(solution)/shard_map/ppermute | solution.py:415
  365.1 7.0 collective-permute-done.64
  386.9 6.6 collective-permute-done.69
  397.4 48.0 %shard_map.262 = (f32[8,512]{1,0:T(8,128)}, f32[352,1024]{1,0:T(8,128)}, bf16[352,1024]{1,0:T(8,128)(2,1)}, bf16[4,2,128,512]{3,2,1,0:T(8,128)(2,1)}, bf16[4,2,1...) custom-call(bf16[352,1024]{1,0:T(8,128)(2,1)} %get-tuple-element.139, ...), custom_call_target="tpu_custom_call" | custom-call | flops 8443133952 | bytes 14417920 | tf_op jit(solution)/shard_map/pallas_call | solution.py:436
  471.4 21.8 %shard_map.264 = (f32[8,2048]{1,0:T(8,128)}, f32[352,1024]{1,0:T(8,128)}, bf16[352,1024]{1,0:T(8,128)(2,1)}, bf16[1024,512]{1,0:T(8,128)(2,1)}, bf16[1024,512]{1...) custom-call(bf16[352,1024]{1,0:T(8,128)(2,1)} %get-tuple-element.149, ...), custom_call_target="tpu_custom_call" | custom-call | flops 11811160064 | bytes 29032448 | tf_op jit(solution)/shard_map/pallas_call | solution.py:436
  497.7 8.0 %collective-permute-done.56 = bf16[512,512]{1,0:T(8,128)(2,1)} collective-permute-done((bf16[512,512]{1,0:T(8,128)(2,1)}, bf16[512,512]{1,0:T(8,128)(2,1)}, u32[]{:S(2)}, u32[]{:S(2)}) %collective-permute-start.56) | collective-permute-done | bytes 524320 | tf_op jit(solution)/shard_map/ppermute | solution.py:415
  516.0 14.6 %collective-permute-done.57 = bf16[1024,512]{1,0:T(8,128)(2,1)S(1)} collective-permute-done((bf16[1024,512]{1,0:T(8,128)(2,1)}, bf16[1024,512]{1,0:T(8,128)(2,1)S(1)}, u32[]{:S(2)}, u32[]{:S(2)}) %collective-permute-start.57) | collective-permute-done | bytes 1048608 | tf_op jit(solution)/shard_map/ppermute | solution.py:415
  535.2 9.9 %collective-permute-done.52 = bf16[512,512]{1,0:T(8,128)(2,1)} collective-permute-done((bf16[512,512]{1,0:T(8,128)(2,1)}, bf16[512,512]{1,0:T(8,128)(2,1)}, u32[]{:S(2)}, u32[]{:S(2)}) %collective-permute-start.52) | collective-permute-done | bytes 524320 | tf_op jit(solution)/shard_map/ppermute | solution.py:415
  560.1 47.5 %shard_map.266 = (f32[8,512]{1,0:T(8,128)}, f32[352,1024]{1,0:T(8,128)}, bf16[352,1024]{1,0:T(8,128)(2,1)}, bf16[4,2,128,512]{3,2,1,0:T(8,128)(2,1)}, bf16[4,2,1...) custom-call(bf16[352,1024]{1,0:T(8,128)(2,1)} %get-tuple-element.156, ...), custom_call_target="tpu_custom_call" | custom-call | flops 8443133952 | bytes 14417920 | tf_op jit(solution)/shard_map/pallas_call | solution.py:436
  614.9 6.3 collective-permute-done.48
  634.9 12.1 %collective-permute-done.49 = bf16[1024,512]{1,0:T(8,128)(2,1)S(1)} collective-permute-done((bf16[1024,512]{1,0:T(8,128)(2,1)}, bf16[1024,512]{1,0:T(8,128)(2,1)S(1)}, u32[]{:S(2)}, u32[]{:S(2)}) %collective-permute-start.49) | collective-permute-done | bytes 1048608 | tf_op jit(solution)/shard_map/ppermute | solution.py:415
  664.2 16.7 %all-to-all-done.1 = f32[32,1,2818]{2,1,0:T(1,128)S(1)} async-done(((f32[32,1,2818]{2,1,0:T(1,128)}), f32[32,1,2818]{2,1,0:T(1,128)S(1)}, u32[]{:S(2)}, u32[]{:S(2)}) %all-to-all-start.1) | async-done | bytes 360736 | tf_op jit(solution)/shard_map/all_to_all | solution.py:1255
  (604 shorter events, 261.1 us)
Async XLA Ops:
  23.8 39.1 %all-gather.8.cloned.1.call-start = ((), (), s32[]{:S(2)}) async-start(), calls=%async_computation.8 | async-start | bytes 1310720 | tf_op jit(solution)/shard_map/all_gather | solution.py:1101
  23.9 42.8 %collective-permute-start = (bf16[340,1024]{1,0:T(8,128)(2,1)}, bf16[340,1024]{1,0:T(8,128)(2,1)S(1)}, u32[]{:S(2)}, u32[]{:S(2)}) collective-permute-start(bf16[340,1024]{1,0:T(8,128)(2,1)} %param.15), channel_id=1, source_target_pairs={{0,0},{1,8},{8,1},{9,9},{2,2},{3,10},{10,3},{11,11},{4,4},{5,12},{... | collective-permute-start | bytes 2088968 | tf_op jit(solution)/shard_map/ppermute | solution.py:419
  35.4 58.2 %all-gather.10.cloned.1.call-start = ((), (), s32[]{:S(2)}) async-start(), calls=%async_computation.9 | async-start | bytes 1310720 | tf_op jit(solution)/shard_map/all_gather | solution.py:1101
  38.8 82.8 %all-gather.12.cloned.1.call-start = ((), (), s32[]{:S(2)}) async-start(), calls=%async_computation.10 | async-start | bytes 1310720 | tf_op jit(solution)/shard_map/all_gather | solution.py:1101
  41.5 127.3 %all-gather.14.cloned.1.call-start = ((), (), s32[]{:S(2)}) async-start(), calls=%async_computation.11 | async-start | bytes 1310720 | tf_op jit(solution)/shard_map/all_gather | solution.py:1101
  88.3 34.4 %collective-permute-start.5 = (bf16[512,512]{1,0:T(8,128)(2,1)S(1)}, bf16[512,512]{1,0:T(8,128)(2,1)}, u32[]{:S(2)}, u32[]{:S(2)}) collective-permute-start(bf16[512,512]{1,0:T(8,128)(2,1)S(1)} %slice.743), channel_id=1, source_target_pairs={{0,16},{16,0},{1,17},{17,1},{2,18},{18,2},{3,19},{19,3},{4,20},{20... | collective-permute-start | bytes 1572872 | tf_op jit(solution)/shard_map/ppermute | solution.py:415
  90.6 33.3 %collective-permute-start.6 = (bf16[512,512]{1,0:T(8,128)(2,1)S(1)}, bf16[512,512]{1,0:T(8,128)(2,1)S(1)}, u32[]{:S(2)}, u32[]{:S(2)}) collective-permute-start(bf16[512,512]{1,0:T(8,128)(2,1)S(1)} %slice.744), channel_id=1, source_target_pairs={{0,1},{1,0},{2,3},{3,2},{4,5},{5,4},{6,7},{7,6},{8,9},{9,8},{10,11... | collective-permute-start | bytes 1572872 | tf_op jit(solution)/shard_map/ppermute | solution.py:415
  91.9 119.7 %all-gather.16.cloned.1.call-start = ((), (), s32[]{:S(2)}) async-start(), calls=%async_computation.12 | async-start | bytes 1310720 | tf_op jit(solution)/shard_map/all_gather | solution.py:1101
  93.7 65.4 %collective-permute-start.10 = (bf16[1024,512]{1,0:T(8,128)(2,1)}, bf16[1024,512]{1,0:T(8,128)(2,1)}, u32[]{:S(2)}, u32[]{:S(2)}) collective-permute-start(bf16[1024,512]{1,0:T(8,128)(2,1)} %bitcast.355), channel_id=1, source_target_pairs={{0,1},{1,0},{2,3},{3,2},{4,5},{5,4},{6,7},{7,6},{8,9},{9,8},{10,11... | collective-permute-start | bytes 3145736 | tf_op jit(solution)/shard_map/ppermute | solution.py:415
  94.0 66.6 %collective-permute-start.11 = (bf16[1024,512]{1,0:T(8,128)(2,1)}, bf16[1024,512]{1,0:T(8,128)(2,1)}, u32[]{:S(2)}, u32[]{:S(2)}) collective-permute-start(bf16[1024,512]{1,0:T(8,128)(2,1)} %bitcast.356), channel_id=1, source_target_pairs={{0,16},{16,0},{1,17},{17,1},{2,18},{18,2},{3,19},{19,3},{4,20},{20... | collective-permute-start | bytes 3145736 | tf_op jit(solution)/shard_map/ppermute | solution.py:415
  121.6 40.4 %collective-permute-start.14 = (bf16[1024,512]{1,0:T(8,128)(2,1)}, bf16[1024,512]{1,0:T(8,128)(2,1)}, u32[]{:S(2)}, u32[]{:S(2)}) collective-permute-start(bf16[1024,512]{1,0:T(8,128)(2,1)} %bitcast.359), channel_id=1, source_target_pairs={{0,1},{1,0},{2,3},{3,2},{4,5},{5,4},{6,7},{7,6},{8,9},{9,8},{10,11... | collective-permute-start | bytes 3145736 | tf_op jit(solution)/shard_map/ppermute | solution.py:415
  122.7 42.3 %collective-permute-start.15 = (bf16[1024,512]{1,0:T(8,128)(2,1)}, bf16[1024,512]{1,0:T(8,128)(2,1)}, u32[]{:S(2)}, u32[]{:S(2)}) collective-permute-start(bf16[1024,512]{1,0:T(8,128)(2,1)} %bitcast.360), channel_id=1, source_target_pairs={{0,16},{16,0},{1,17},{17,1},{2,18},{18,2},{3,19},{19,3},{4,20},{20... | collective-permute-start | bytes 3145736 | tf_op jit(solution)/shard_map/ppermute | solution.py:415
  158.8 94.7 %all-gather.18.cloned.1.call-start = ((), (), s32[]{:S(2)}) async-start(), calls=%async_computation.13 | async-start | bytes 1310720 | tf_op jit(solution)/shard_map/all_gather | solution.py:1101
  173.4 34.8 %collective-permute-start.20 = (bf16[1024,512]{1,0:T(8,128)(2,1)S(1)}, bf16[1024,512]{1,0:T(8,128)(2,1)S(1)}, u32[]{:S(2)}, u32[]{:S(2)}) collective-permute-start(bf16[1024,512]{1,0:T(8,128)(2,1)S(1)} %bitcast.266), channel_id=1, source_target_pairs={{0,1},{1,0},{2,3},{3,2},{4,5},{5,4},{6,7},{7,6},{8,9},{9,8},{10,11... | collective-permute-start | bytes 3145736 | tf_op jit(solution)/shard_map/ppermute | solution.py:415
  174.5 35.8 %collective-permute-start.21 = (bf16[1024,512]{1,0:T(8,128)(2,1)S(1)}, bf16[1024,512]{1,0:T(8,128)(2,1)S(1)}, u32[]{:S(2)}, u32[]{:S(2)}) collective-permute-start(bf16[1024,512]{1,0:T(8,128)(2,1)S(1)} %bitcast.267), channel_id=1, source_target_pairs={{0,16},{16,0},{1,17},{17,1},{2,18},{18,2},{3,19},{19,3},{4,20},{20... | collective-permute-start | bytes 3145736 | tf_op jit(solution)/shard_map/ppermute | solution.py:415
  197.0 465.9 %reduce-scatter.17.cloned.1.call-start = ((), (), s32[]{:S(2)}) async-start(), calls=%async_computation.19 | async-start | bytes 1310720 | tf_op jit(solution)/shard_map/reduce_scatter | solution.py:1053
  211.6 48.6 %collective-permute-start.26 = (bf16[1024,512]{1,0:T(8,128)(2,1)}, bf16[1024,512]{1,0:T(8,128)(2,1)}, u32[]{:S(2)}, u32[]{:S(2)}) collective-permute-start(bf16[1024,512]{1,0:T(8,128)(2,1)} %bitcast.363), channel_id=1, source_target_pairs={{0,1},{1,0},{2,3},{3,2},{4,5},{5,4},{6,7},{7,6},{8,9},{9,8},{10,11... | collective-permute-start | bytes 3145736 | tf_op jit(solution)/shard_map/ppermute | solution.py:415
  212.8 49.1 %collective-permute-start.27 = (bf16[1024,512]{1,0:T(8,128)(2,1)}, bf16[1024,512]{1,0:T(8,128)(2,1)}, u32[]{:S(2)}, u32[]{:S(2)}) collective-permute-start(bf16[1024,512]{1,0:T(8,128)(2,1)} %bitcast.364), channel_id=1, source_target_pairs={{0,16},{16,0},{1,17},{17,1},{2,18},{18,2},{3,19},{19,3},{4,20},{20... | collective-permute-start | bytes 3145736 | tf_op jit(solution)/shard_map/ppermute | solution.py:415
  259.8 35.1 %collective-permute-start.25 = (bf16[352,1024]{1,0:T(8,128)(2,1)}, bf16[352,1024]{1,0:T(8,128)(2,1)}, u32[]{:S(2)}, u32[]{:S(2)}) collective-permute-start(bf16[352,1024]{1,0:T(8,128)(2,1)} %get-tuple-element.128.own_ref), channel_id=1, source_target_pairs={{0,8},{8,0},{1,9},{9,1},{2,10},{10,2},{3,11},{11,3},{4,12},{12,4},... | collective-permute-start | bytes 2162696 | tf_op jit(solution)/shard_map/ppermute | solution.py:411
  263.0 31.9 %collective-permute-start.29 = (bf16[512,512]{1,0:T(8,128)(2,1)S(1)}, bf16[512,512]{1,0:T(8,128)(2,1)}, u32[]{:S(2)}, u32[]{:S(2)}) collective-permute-start(bf16[512,512]{1,0:T(8,128)(2,1)S(1)} %slice.795), channel_id=1, source_target_pairs={{0,1},{1,0},{2,3},{3,2},{4,5},{5,4},{6,7},{7,6},{8,9},{9,8},{10,11... | collective-permute-start | bytes 1572872 | tf_op jit(solution)/shard_map/ppermute | solution.py:415
  374.1 80.6 %collective-permute-start.65 = (bf16[1024,512]{1,0:T(8,128)(2,1)}, bf16[1024,512]{1,0:T(8,128)(2,1)S(1)}, u32[]{:S(2)}, u32[]{:S(2)}) collective-permute-start(bf16[1024,512]{1,0:T(8,128)(2,1)} %fusion.14), channel_id=1, source_target_pairs={{0,16},{16,0},{1,17},{17,1},{2,18},{18,2},{3,19},{19,3},{4,20},{20... | collective-permute-start | bytes 3145736 | tf_op jit(solution)/shard_map/ppermute | solution.py:415
  376.3 78.4 %collective-permute-start.63 = (bf16[1024,512]{1,0:T(8,128)(2,1)}, bf16[1024,512]{1,0:T(8,128)(2,1)}, u32[]{:S(2)}, u32[]{:S(2)}) collective-permute-start(bf16[1024,512]{1,0:T(8,128)(2,1)} %fusion.13), channel_id=1, source_target_pairs={{0,1},{1,0},{2,3},{3,2},{4,5},{5,4},{6,7},{7,6},{8,9},{9,8},{10,11... | collective-permute-start | bytes 3145736 | tf_op jit(solution)/shard_map/ppermute | solution.py:415
  397.3 265.6 %reduce-scatter.15.cloned.1.call-start = ((), (), s32[]{:S(2)}) async-start(), calls=%async_computation.18 | async-start | bytes 1310720 | tf_op jit(solution)/shard_map/reduce_scatter | solution.py:1053
  457.4 205.6 %reduce-scatter.13.cloned.1.call-start = ((), (), s32[]{:S(2)}) async-start(), calls=%async_computation.17 | async-start | bytes 1310720 | tf_op jit(solution)/shard_map/reduce_scatter | solution.py:1053
  497.4 186.3 %reduce-scatter.11.cloned.1.call-start = ((), (), s32[]{:S(2)}) async-start(), calls=%async_computation.16 | async-start | bytes 1310720 | tf_op jit(solution)/shard_map/reduce_scatter | solution.py:1053
  512.4 34.8 %collective-permute-start.42 = (bf16[352,1024]{1,0:T(8,128)(2,1)}, bf16[352,1024]{1,0:T(8,128)(2,1)}, u32[]{:S(2)}, u32[]{:S(2)}) collective-permute-start(bf16[352,1024]{1,0:T(8,128)(2,1)} %get-tuple-element.153), channel_id=1, source_target_pairs={{0,8},{8,0},{1,9},{9,1},{2,10},{10,2},{3,11},{11,3},{4,12},{12,4},... | collective-permute-start | bytes 2162696 | tf_op jit(solution)/shard_map/ppermute | solution.py:411
  515.7 40.0 %collective-permute-start.50 = (bf16[512,512]{1,0:T(8,128)(2,1)}, bf16[512,512]{1,0:T(8,128)(2,1)}, u32[]{:S(2)}, u32[]{:S(2)}) collective-permute-start(bf16[512,512]{1,0:T(8,128)(2,1)} %get-tuple-element.182), channel_id=1, source_target_pairs={{0,16},{16,0},{1,17},{17,1},{2,18},{18,2},{3,19},{19,3},{4,20},{20... | collective-permute-start | bytes 1572872 | tf_op jit(solution)/shard_map/ppermute | solution.py:415
  535.1 148.6 %reduce-scatter.9.cloned.1.call-start = ((), (), s32[]{:S(2)}) async-start(), calls=%async_computation.15 | async-start | bytes 1310720 | tf_op jit(solution)/shard_map/reduce_scatter | solution.py:1053
  547.3 62.0 %collective-permute-start.53 = (bf16[1024,512]{1,0:T(8,128)(2,1)}, bf16[1024,512]{1,0:T(8,128)(2,1)S(1)}, u32[]{:S(2)}, u32[]{:S(2)}) collective-permute-start(bf16[1024,512]{1,0:T(8,128)(2,1)} %fusion.10), channel_id=1, source_target_pairs={{0,16},{16,0},{1,17},{17,1},{2,18},{18,2},{3,19},{19,3},{4,20},{20... | collective-permute-start | bytes 3145736 | tf_op jit(solution)/shard_map/ppermute | solution.py:415
  557.9 51.3 %collective-permute-start.51 = (bf16[1024,512]{1,0:T(8,128)(2,1)}, bf16[1024,512]{1,0:T(8,128)(2,1)S(1)}, u32[]{:S(2)}, u32[]{:S(2)}) collective-permute-start(bf16[1024,512]{1,0:T(8,128)(2,1)} %fusion.9), channel_id=1, source_target_pairs={{0,1},{1,0},{2,3},{3,2},{4,5},{5,4},{6,7},{7,6},{8,9},{9,8},{10,11... | collective-permute-start | bytes 3145736 | tf_op jit(solution)/shard_map/ppermute | solution.py:415
  610.7 73.9 %reduce-scatter.7.cloned.1.call-start = ((), (), s32[]{:S(2)}) async-start(), calls=%async_computation.14 | async-start | bytes 1310720 | tf_op jit(solution)/shard_map/reduce_scatter | solution.py:1053
  659.4 31.9 %collective-permute-start.45 = (f32[340,1024]{1,0:T(8,128)}, f32[340,1024]{1,0:T(8,128)}, u32[]{:S(2)}, u32[]{:S(2)}) collective-permute-start(f32[340,1024]{1,0:T(8,128)} %maximum_select_fusion), channel_id=1, source_target_pairs={{0,0},{1,8},{8,1},{9,9},{2,2},{3,10},{10,3},{11,11},{4,4},{5,12},{... | collective-permute-start | bytes 4177928 | tf_op jit(solution)/shard_map/ppermute | solution.py:419
  (122 other events, 1606.9 us)
Sparse Core Ops, SparseCore 0:
  35.6 27.3 all-gather.7
  65.1 27.4 all-gather.9
  94.1 27.4 all-gather.11
  123.0 27.7 all-gather.13
  158.9 25.3 all-gather.15
  197.2 25.1 all-gather.17
  397.4 28.3 reduce-scatter.16
  457.5 26.7 reduce-scatter.14
  497.5 25.9 reduce-scatter.12
  535.2 31.2 reduce-scatter.10
  610.8 25.7 reduce-scatter.8
  651.6 32.9 reduce-scatter.6

commit v3 on v2

--- a/solution.py
+++ b/solution.py
@@ -415,8 +415,8 @@
     return lax.ppermute(values, axis, [(0, 1), (1, 0)])
 
 
-def trade(values):
-    return lax.ppermute(values, ("core", "x"), [(0, 0), (1, 2), (2, 1), (3, 3)])
+def trade(values, moves):
+    return jnp.where(moves, lax.ppermute(values, ("core", "x"), [(1, 2), (2, 1)]), values)
 
 
 def turned(values, flag, axis):
@@ -443,7 +443,7 @@
         compiler_params=pltpu.CompilerParams(
             dimension_semantics=("arbitrary",) * len(grid), vmem_limit_bytes=VMEM_BYTES
         ),
-        cost_estimate=pl.CostEstimate(flops=flops, bytes_accessed=moved, transcendentals=0),
+        cost_estimate=pl.CostEstimate(flops=flops // 64, bytes_accessed=moved // 64, transcendentals=0),
     )(*args)
 
 
@@ -457,30 +457,41 @@
         body(pl.ds(pl.multiple_of(step * size, size), size))
 
 
-def weight_specs(low):
-    return [
-        pl.BlockSpec((low, low), lambda t: (jnp.minimum(t, 1), 0)),
-        pl.BlockSpec((low, low), lambda t: (jnp.maximum(t - 2, 0), 0)),
-        pl.BlockSpec((low, low), lambda t: (jnp.minimum(t, 1), 0)),
-        fixed((low, low)),
-        fixed((low, low)),
-    ]
+def early(dims, row=0):
+    return pl.BlockSpec(dims, lambda t: (row + jnp.minimum(t, 1), 0))
+
+
+def late(dims, row=0):
+    return pl.BlockSpec(dims, lambda t: (row + jnp.maximum(t - 2, 0), 0))
+
+
+def weight_specs(low, blocks=None):
+    if blocks is not None and blocks[0].ndim == 4:
+        shape = (2, None, low // 2, low)
+
+        def spec(block, first):
+            pick = (lambda t: jnp.minimum(t, 1)) if first else (lambda t: jnp.maximum(t - 2, 0))
+            return pl.BlockSpec(shape, lambda t: (pick(t), block, 0, 0))
+
+        return [spec(0, True), spec(2, False), spec(1, True), spec(3, False)]
+    return [early((low, low)), late((low, low)), early((low, low)), late((low, low))]
+
+
+def matrix(ref):
+    value = ref[...]
+    return value.reshape(-1, value.shape[-1])
 
 
 def with_tile(step, refs, body):
-    g, gx, gy, ga, gb = refs
+    g, gx, gy, gd = refs
 
     @pl.when(step < 2)
     def _():
-        body(g[...], gy[...])
-
-    @pl.when(step == 2)
+        body(g, gy)
+
+    @pl.when(step >= 2)
     def _():
-        body(gx[...], ga[...])
-
-    @pl.when(step == 3)
-    def _():
-        body(gx[...], gb[...])
+        body(gx, gd)
 
 
 def join_into(joined, own, other):
@@ -494,7 +505,7 @@
     low, both = width // 2, 2 * rows
     hid = 4 * low
 
-    def body(own_ref, other_ref, g, gx, gy, ga, gb, bias_ref, joined, act, slope):
+    def body(own_ref, other_ref, g, gx, gy, gd, bias_ref, joined, act, slope):
         step = pl.program_id(0)
 
         @pl.when(step == 0)
@@ -514,7 +525,7 @@
                     inner = pre * ((0.5 * root) + (1.5 * 0.044715 * root) * square)
                     slope[sl, lanes] = (half + (1.0 - tanh * tanh) * inner).astype(BF)
 
-        with_tile(step, (g, gx, gy, ga, gb), product)
+        with_tile(step, (g, gx, gy, gd), product)
 
     return call(
         body,
@@ -529,14 +540,14 @@
     )
 
 
-def fc_back(own, other, up_blocks, down_blocks, slope, act, hidden):
+def fc_back(own, other, up_blocks, down_blocks, slope, act, hidden, by_z):
     rows, width = own.shape
     low, both = width // 2, 2 * rows
     hid = 4 * low
 
-    def body(own_ref, other_ref, ug, ugx, ugy, uga, ugb, dg, dgx, dgy, dga, dgb, slope_ref, act_ref, hid_ref,
+    def body(own_ref, other_ref, ug, ugx, ugy, ugd, dg, dgx, dgy, dgd, slope_ref, act_ref, hid_ref,
              sums, out_own, out_other, *rest):
-        two_refs, one_refs, (joined, grad, acc) = rest[:5], rest[5:10], rest[10:]
+        two_refs, one_refs, (joined, grad, acc) = rest[: -7], rest[-7:-3], rest[-3:]
         step = pl.program_id(0)
 
         @pl.when(step == 0)
@@ -545,13 +556,13 @@
 
         def product(up_one, up_two, down_one, down_two, first, last, near, far):
             for i, sl in enumerate((slice(rows, both), slice(0, rows))):
-                value = dot(joined[sl, :low], up_one[...], NT) + dot(joined[sl, low:], up_two[...], NT)
+                value = dot(joined[sl, :low], matrix(up_one), NT) + dot(joined[sl, low:], matrix(up_two), NT)
                 value = (value * slope_ref[sl, :].astype(F32)).astype(BF)
                 grad[sl, :] = value
                 total = jnp.sum(value.astype(F32).reshape(rows // 8, 8, low), axis=0)
                 sums[...] = total if i == 0 else sums[...] + total
                 for lanes, down in ((slice(0, low), down_one), (slice(low, width), down_two)):
-                    part = dot(value, down[...])
+                    part = dot(value, matrix(down))
                     if not first:
                         part = part + acc[sl, lanes]
                     if not last:
@@ -561,8 +572,12 @@
                     else:
                         out_own[:, lanes] = part
             for refs, left, right in ((two_refs, act_ref, joined), (one_refs, grad, hid_ref)):
-                refs[near][...] = dot(left[...], right[:, :low], TN).astype(BF)
-                refs[far][...] = dot(left[...], right[:, low:], TN).astype(BF)
+                for j, lanes in ((near, slice(0, low)), (far, slice(low, width))):
+                    value = dot(left[...], right[:, lanes], TN).astype(BF)
+                    if len(refs) == 1:
+                        refs[0][:, j // 2] = value.reshape(2, low // 2, low)
+                    else:
+                        refs[j][...] = value
 
         @pl.when(step == 0)
         def _():
@@ -574,30 +589,29 @@
 
         @pl.when(step == 2)
         def _():
-            product(ugx, uga, dgx, dga, False, False, 1, 3)
+            product(ugx, ugd, dgx, dgd, False, False, 1, 3)
 
         @pl.when(step == 3)
         def _():
-            product(ugx, ugb, dgx, dgb, False, True, 1, 4)
+            product(ugx, ugd, dgx, dgd, False, True, 1, 3)
 
     tiles = pl.BlockSpec((both, low), lambda t: (0, t))
-    early = pl.BlockSpec((low, low), lambda t: (jnp.minimum(t, 1), 0))
-    late = pl.BlockSpec((low, low), lambda t: (jnp.maximum(t - 2, 0), 0))
-    whole, part = shape_of((2 * low, low), BF), shape_of((low, low), BF)
+    whole = shape_of((2 * low, low), BF)
+    z_specs = [pl.BlockSpec((2, 2, low // 2, low), lambda t: (t % 2, t // 2, 0, 0))]
     found = call(
         body,
         (4,),
-        [fixed((rows, width))] * 2 + weight_specs(low) + weight_specs(low) + [tiles, tiles, fixed((both, width))],
+        [fixed((rows, width))] * 2 + weight_specs(low, up_blocks) + weight_specs(low, down_blocks) + [tiles, tiles, fixed((both, width))],
         [pl.BlockSpec((8, low), lambda t: (0, t)), fixed((rows, width)), fixed((rows, width))]
-        + [early, late, early, fixed((low, low)), fixed((low, low))] * 2,
+        + (z_specs if by_z else weight_specs(low)) + weight_specs(low),
         [shape_of((8, hid), F32), shape_of((rows, width), F32), shape_of((rows, width), BF)]
-        + [whole, whole, whole, part, part] * 2,
+        + ([shape_of((4, 4, low // 2, low), BF)] if by_z else [whole] * 4) + [whole] * 4,
         [pltpu.VMEM((both, width), BF), pltpu.VMEM((both, low), BF), pltpu.VMEM((both, width), F32)],
         8 * both * width * hid,
         8 * hid * width + 6 * both * width + 4 * both * hid + 6 * rows * width,
         (own, other, *up_blocks, *down_blocks, slope, act, hidden),
     )
-    return found[:3], found[3:8], found[8:]
+    return found[:3], found[3:-4], found[-4:]
 
 
 def fc_down(left, blocks):
@@ -605,13 +619,13 @@
     rows, low = both // 2, hid // 4
     width = 2 * low
 
-    def body(left_ref, g, gx, gy, ga, gb, own, other, acc):
+    def body(left_ref, g, gx, gy, gd, own, other, acc):
         step = pl.program_id(0)
 
         def product(one, two, first, last):
             for i, sl in enumerate((slice(rows, both), slice(0, rows))):
                 for lanes, right in ((slice(0, low), one), (slice(low, width), two)):
-                    part = dot(left_ref[sl, :], right[...])
+                    part = dot(left_ref[sl, :], matrix(right))
                     if not first:
                         part = part + acc[sl, lanes]
                     if not last:
@@ -631,16 +645,16 @@
 
         @pl.when(step == 2)
         def _():
-            product(gx, ga, False, False)
+            product(gx, gd, False, False)
 
         @pl.when(step == 3)
         def _():
-            product(gx, gb, False, True)
+            product(gx, gd, False, True)
 
     return call(
         body,
         (4,),
-        [pl.BlockSpec((both, low), lambda t: (0, t))] + weight_specs(low),
+        [pl.BlockSpec((both, low), lambda t: (0, t))] + weight_specs(low, blocks),
         [fixed((rows, width))] * 2,
         [shape_of((rows, width), F32), shape_of((rows, width), BF)],
         [pltpu.VMEM((both, width), F32)],
@@ -661,7 +675,7 @@
     low, both = width // 2, 2 * rows
     tile = low // 2
 
-    def body(own_ref, other_ref, g, gx, gy, ga, gb, vec, ones_ref, joined, q_raw, k_raw, q_low, k_low, v_low, acc):
+    def body(own_ref, other_ref, g, gx, gy, gd, vec, ones_ref, joined, q_raw, k_raw, q_low, k_low, v_low, acc):
         step = pl.program_id(0)
         part = step % 3
 
@@ -676,13 +690,9 @@
         def _():
             product(g[...], gy[...])
 
-        @pl.when(jnp.logical_and(step >= 3, part < 2))
-        def _():
-            product(gx[...], ga[...])
-
-        @pl.when(step == 5)
-        def _():
-            product(gx[...], gb[...])
+        @pl.when(step >= 3)
+        def _():
+            product(gx[...], gd[...])
 
         def unit(value):
             square = dot((value * value).astype(BF), ones_ref[...])
@@ -721,8 +731,7 @@
             pl.BlockSpec((tile, low), lambda t: (jnp.minimum(t, 2), 0)),
             pl.BlockSpec((tile, low), lambda t: (jnp.maximum(t - 3, 0), 0)),
             pl.BlockSpec((tile, low), lambda t: (jnp.minimum(t, 2), 0)),
-            pl.BlockSpec((tile, low), lambda t: (jnp.clip(t - 3, 0, 1), 0)),
-            fixed((tile, low)),
+            pl.BlockSpec((tile, low), lambda t: (jnp.maximum(t - 3, 0), 0)),
             pl.BlockSpec((8, tile), lambda t: (0, half(t))),
             fixed((tile, tile)),
         ],
@@ -742,21 +751,27 @@
 
     def body(q_ref, k_ref, v_ref, end_ref, place_ref, out_ref, rest_ref, log_ref):
         place = place_ref[0:1, :]
-        ones = jnp.ones((both, head_width), BF)
-        for h in range(2):
-            lanes = slice(h * head_width, (h + 1) * head_width)
-            keys = k_ref[:, lanes]
-            values = jnp.concatenate((v_ref[:, lanes], ones), axis=1)
-            for c in range(4):
-                sl = slice(c * chunk, (c + 1) * chunk)
-                scores = dot(q_ref[sl, lanes], keys, NT)
+        lane = lax.broadcasted_iota(jnp.int32, (both, pair), 1)
+        value = v_ref[...]
+        ones = jnp.ones_like(value)
+        wide = [
+            jnp.concatenate((jnp.where(lane // head_width == h, value, ones), ones), axis=1) for h in range(2)
+        ]
+        first = lane[:chunk] < head_width
+        for c in range(4):
+            sl = slice(c * chunk, (c + 1) * chunk)
+            queries = q_ref[sl, :]
+            found = []
+            for h in range(2):
+                own = jnp.where(first if h == 0 else ~first, queries, jnp.zeros_like(queries))
+                scores = dot(own, k_ref[...], NT)
                 expo = jnp.where(place < end_ref[sl, :], jnp.exp(scores), 0.0).astype(BF)
-                mixed = dot(expo, values)
-                total = mixed[:, head_width:]
-                value = mixed[:, :head_width] / total
-                out_ref[sl, lanes] = value.astype(BF)
-                rest_ref[sl, lanes] = (value - value.astype(BF).astype(F32)).astype(BF)
-                log_ref[sl, lanes] = jnp.log(total)
+                found.append(dot(expo, wide[h]))
+            out = jnp.where(first, found[0][:, :pair] / found[0][:, pair:], found[1][:, :pair] / found[1][:, pair:])
+            low_out = out.astype(BF)
+            out_ref[sl, :] = low_out
+            rest_ref[sl, :] = (out - low_out.astype(F32)).astype(BF)
+            log_ref[sl, :] = jnp.log(jnp.where(first, found[1][:, pair:], found[0][:, pair:]))
 
     block = pl.BlockSpec((both, pair), lambda t: (0, t))
     return call(
@@ -783,7 +798,7 @@
     def body(own_ref, other_ref, *refs):
         w_refs, refs = refs[:16], refs[16:]
         (q_ref, k_ref, v_ref, attn_ref, rest_ref, log_ref, qr_ref, kr_ref, hid_ref, scale_ref, place_ref, end_ref,
-         sums, out_own, out_other, keep, by_x, by_y, far_a, far_b, joined, weights, ds_ref, three_ref, acc) = refs
+         sums, out_own, out_other, keep, by_x, by_y, far, joined, weights, ds_ref, three_ref, acc) = refs
         step = pl.program_id(0)
 
         @pl.when(step == 0)
@@ -798,55 +813,64 @@
                     weights[rows_i, :low] = w_refs[4 * i + 2 * side][...]
                     weights[rows_i, low:] = w_refs[4 * i + 2 * side + 1][...]
 
-        grad_pair = dot(joined[...], weights[3 * pair :, :], NT).astype(BF)
+        grad = dot(joined[...], weights[3 * pair :, :], NT).astype(BF)
         ends = end_ref[0:1, :]
-        lane = lax.broadcasted_iota(jnp.int32, (both, head_width), 1)
-        ones = jnp.ones((both, head_width), BF)
+        lane = lax.broadcasted_iota(jnp.int32, (both, pair), 1)
+        inner = lane % head_width
+        row_head = lax.broadcasted_iota(jnp.int32, (pair, pair), 0) // head_width
+        lane_head = lax.broadcasted_iota(jnp.int32, (pair, pair), 1) // head_width
+        same = (row_head == lane_head).astype(BF)
+        swap = (row_head != lane_head).astype(BF)
+        swap_twice = jnp.concatenate((swap, swap), axis=0)
 
         def spread(value):
             high = value.astype(BF)
-            rest = value - high.astype(F32)
-            mid = rest.astype(BF)
-            small = (rest - mid.astype(F32)).astype(BF)
+            left = value - high.astype(F32)
+            mid = left.astype(BF)
+            small = (left - mid.astype(F32)).astype(BF)
             zero = jnp.zeros_like(high)
-            return jnp.where(lane == 0, high, jnp.where(lane == 1, mid, jnp.where(lane == 2, small, zero)))
+            return jnp.where(inner == 0, high, jnp.where(inner == 1, mid, jnp.where(inner == 2, small, zero)))
 
         def unit_back(raw, grad_unit):
             raw = raw.astype(F32)
-            rate = lax.rsqrt(jnp.sum(raw * raw, axis=1, keepdims=True) + EPS_UNIT)
+            rate = lax.rsqrt(dot((raw * raw).astype(BF), same) + EPS_UNIT)
             unit = raw * rate
-            cross = jnp.sum(grad_unit * unit, axis=1, keepdims=True)
+            cross = dot((grad_unit * unit).astype(BF), same)
             return rate * (grad_unit - unit * cross), unit
 
+        product = grad.astype(F32) * (attn_ref[...].astype(F32) + rest_ref[...].astype(F32))
+        high = product.astype(BF)
+        small = (product - high.astype(F32)).astype(BF)
+        delta = dot(jnp.concatenate((high, small), axis=1), swap_twice)
+        log_terms, delta_terms = spread(-log_ref[...]), spread(-delta)
+        queries, keys, values = q_ref[...], k_ref[...], v_ref[...]
+        zero, one = jnp.zeros_like(keys), jnp.ones_like(keys)
+        dk_parts, dv_parts = [None] * 4, [None] * 4
+        d_qt = None
         for h in range(2):
-            lanes = slice(h * head_width, (h + 1) * head_width)
-            queries, keys, values, grads = q_ref[:, lanes], k_ref[:, lanes], v_ref[:, lanes], grad_pair[:, lanes]
-            mixed = attn_ref[:, lanes].astype(F32) + rest_ref[:, lanes].astype(F32)
-            delta = jnp.sum(grads.astype(F32) * mixed, axis=1, keepdims=True)
-            q_wide = jnp.concatenate((queries, spread(-log_ref[:, lanes])), axis=1)
-            g_wide = jnp.concatenate((grads, spread(jnp.broadcast_to(-delta, (both, head_width)))), axis=1)
-            k_wide = jnp.concatenate((keys, ones), axis=1)
-            v_wide = jnp.concatenate((values, ones), axis=1)
-            dk_parts, dv_parts = [], []
+            mine = lane // head_width == h
+            q_own, g_own, k_own = [jnp.where(mine, v, zero) for v in (queries, grad, keys)]
+            q_wide, g_wide = jnp.where(mine, queries, log_terms), jnp.where(mine, grad, delta_terms)
+            k_wide, v_wide = jnp.where(mine, keys, one), jnp.where(mine, values, one)
             for c in range(4):
                 sl = slice(c * chunk, (c + 1) * chunk)
                 scores = dot(k_wide[sl], q_wide, NT)
                 probs = jnp.where(place_ref[sl, :] < ends, jnp.exp(scores), 0.0)
-                d_probs = dot(v_wide[sl], g_wide, NT)
-                d_scores = (probs * d_probs).astype(BF)
+                d_scores = (probs * dot(v_wide[sl], g_wide, NT)).astype(BF)
                 ds_ref[sl, :] = d_scores
-                dv_parts.append(dot(probs.astype(BF), grads))
-                dk_parts.append(dot(d_scores, queries))
-            d_qn = dot(keys, ds_ref[...], TN).T
-            d_kn = jnp.concatenate(dk_parts, axis=0)
-            d_v = jnp.concatenate(dv_parts, axis=0).astype(BF)
-            d_q, unit_q = unit_back(qr_ref[:, lanes], d_qn * scale_ref[0:1, lanes])
-            d_k, _ = unit_back(kr_ref[:, lanes], d_kn)
-            d_q, d_k = d_q.astype(BF), d_k.astype(BF)
-            for i, value in enumerate((d_q, d_k, d_v)):
-                three_ref[:, i * pair + h * head_width : i * pair + (h + 1) * head_width] = value
-            for i, value in enumerate((d_q.astype(F32), d_v.astype(F32), d_qn * unit_q)):
-                sums[i : i + 1, lanes] = jnp.sum(value, axis=0, keepdims=True)
+                d_v, d_k = dot(probs.astype(BF), g_own), dot(d_scores, q_own)
+                dv_parts[c] = d_v if h == 0 else dv_parts[c] + d_v
+                dk_parts[c] = d_k if h == 0 else dk_parts[c] + d_k
+            part = dot(k_own, ds_ref[...], TN)
+            d_qt = part if h == 0 else d_qt + part
+        d_qn = d_qt.T
+        d_q, unit_q = unit_back(qr_ref[...], d_qn * scale_ref[0:1, :])
+        d_k, _ = unit_back(kr_ref[...], jnp.concatenate(dk_parts, axis=0))
+        d_q, d_k, d_v = d_q.astype(BF), d_k.astype(BF), jnp.concatenate(dv_parts, axis=0).astype(BF)
+        for i, value in enumerate((d_q, d_k, d_v)):
+            three_ref[:, i * pair : (i + 1) * pair] = value
+        for i, value in enumerate((d_q.astype(F32), d_v.astype(F32), d_qn * unit_q)):
+            sums[i : i + 1, :] = jnp.sum(value, axis=0, keepdims=True)
 
         for lanes in (slice(0, low), slice(low, width)):
             part = dot(three_ref[...], weights[: 3 * pair, lanes])
@@ -872,43 +896,31 @@
 
             @pl.when(step < 2)
             def _():
-                target = keep if i == 0 else by_y
                 for j in range(4):
-                    target[j, 0] = grads[j]
+                    (keep, by_y)[i][j, 0] = grads[j]
 
             @pl.when(step >= 2)
             def _():
                 for j in range(4):
-                    if i == 0:
-                        by_x[j, 0] = grads[j]
-                    else:
-                        (far_a if j < 2 else far_b)[j % 2, 0] = grads[j]
-
-    def early(row):
-        return pl.BlockSpec((pair, low), lambda t: (row + jnp.minimum(t, 1), 0))
-
-    def late(row):
-        return pl.BlockSpec((pair, low), lambda t: (row + jnp.maximum(t - 2, 0), 0))
-
-    g, gx, gy, ga, gb = blocks
+                    (by_x, far)[i][j, 0] = grads[j]
+
+    g, gx, gy, gd = blocks
     w_specs, w_args = [], []
     for i in range(4):
-        w_specs += [early(2 * i), early(2 * i), late(2 * i), late(2 * (i % 2))]
-        w_args += [g, gy, gx, ga if i < 2 else gb]
+        w_specs += [f((pair, low), 2 * i) for f in (early, early, late, late)]
+        w_args += [g, gy, gx, gd]
     block = pl.BlockSpec((both, pair), lambda t: (0, t))
     row = pl.BlockSpec((8, pair), lambda t: (0, t))
     first = pl.BlockSpec((4, 1, pair, low), lambda t: (0, jnp.minimum(t, 1), 0, 0))
     second = pl.BlockSpec((4, 1, pair, low), lambda t: (0, jnp.maximum(t - 2, 0), 0, 0))
-    halves = pl.BlockSpec((2, 1, pair, low), lambda t: (0, jnp.maximum(t - 2, 0), 0, 0))
-    whole, half = shape_of((4, 2, pair, low), BF), shape_of((2, 2, pair, low), BF)
     found = call(
         body,
         (steps,),
         [fixed((rows, width))] * 2 + w_specs + [block] * 8
         + [fixed((both, width)), row, fixed((both, 1)), fixed((8, both))],
-        [row, fixed((rows, width)), fixed((rows, width)), first, second, first, halves, halves],
+        [row, fixed((rows, width)), fixed((rows, width)), first, second, first, second],
         [shape_of((8, low), F32), shape_of((rows, width), F32), shape_of((rows, width), BF)]
-        + [whole, whole, whole, half, half],
+        + [shape_of((4, 2, pair, low), BF)] * 4,
         [
             pltpu.VMEM((both, width), BF), pltpu.VMEM((4 * pair, width), BF), pltpu.VMEM((both, both), BF),
             pltpu.VMEM((both, 3 * pair), BF), pltpu.VMEM((both, width), F32),
@@ -925,24 +937,23 @@
     both, low = attn.shape
     rows, width, tile = both // 2, 2 * low, low // 2
 
-    def body(attn_ref, g, gx, gy, gb, own, other):
-        for lanes, first, second in ((slice(0, low), g, gx), (slice(low, width), gy, gb)):
+    def body(attn_ref, g, gx, gy, gd, own, other):
+        for lanes, first, second in ((slice(0, low), g, gx), (slice(low, width), gy, gd)):
             value = dot(attn_ref[:, :tile], first[...]) + dot(attn_ref[:, tile:], second[...])
             own[:, lanes] = value[:rows]
             other[:, lanes] = value[rows:].astype(BF)
 
     last = pl.BlockSpec((tile, low), lambda t: (3, 0))
-    g, gx, gy, _, gb = blocks
     return call(
         body,
         (1,),
-        [fixed((both, low)), last, last, last, pl.BlockSpec((tile, low), lambda t: (1, 0))],
+        [fixed((both, low))] + [last] * 4,
         [fixed((rows, width))] * 2,
         [shape_of((rows, width), F32), shape_of((rows, width), BF)],
         [],
         2 * both * width * low,
         2 * low * width + 2 * both * low + 6 * rows * width,
-        (attn, g, gx, gy, gb),
+        (attn, *blocks),
     )
 
 
@@ -1027,28 +1038,43 @@
     )
 
 
-def gather_blocks(rows):
-    half = rows.shape[0] // 2
-    by_x = across(rows, "x")
-    by_y = across(rows, "y")
-    first = across(by_x[:half], "y")
-    second = across(by_y[half:], "x")
-    return rows, by_x, by_y, first, second
-
-
-def scatter_blocks(blocks, parts, z_size):
-    keep, by_x, by_y, far_a, far_b = [v.reshape(-1, v.shape[-1]) for v in blocks]
-    half = far_a.shape[0]
-    got_a, got_b = across(far_a, "y"), across(far_b, "x")
-
-    def added(block, got, start):
-        part = block[start : start + half].astype(F32) + got.astype(F32)
-        return lax.dynamic_update_slice_in_dim(block, part.astype(BF), start, 0)
-
-    got_x = across(added(by_x, got_a, 0), "x")
-    got_y = across(added(by_y, got_b, half), "y")
-    total = keep.astype(F32) + got_x.astype(F32) + got_y.astype(F32)
-    total = jnp.swapaxes(total.astype(BF).reshape(parts, z_size, -1, keep.shape[1]), 0, 1)
+def tie(value, *others):
+    return lax.optimization_barrier((value,) + others)[0]
+
+
+def add_low(*values):
+    return sum(v.astype(F32) for v in values).astype(BF)
+
+
+def flat(blocks):
+    return [v.reshape(-1, v.shape[-1]) for v in blocks]
+
+
+def near_parts(blocks, got_a, got_b):
+    _, near_x, near_y, _ = blocks
+    half, low = got_a.shape
+
+    def body(x_ref, y_ref, a_ref, b_ref, x_out, y_out):
+        x_out[...] = (x_ref[...].astype(F32) + a_ref[...].astype(F32)).astype(BF)
+        y_out[...] = (y_ref[...].astype(F32) + b_ref[...].astype(F32)).astype(BF)
+
+    front = pl.BlockSpec((half, low), lambda t: (0, 0))
+    back = pl.BlockSpec((half, low), lambda t: (1, 0))
+    return pl.pallas_call(
+        body,
+        grid=(1,),
+        in_specs=[front, back, front, front],
+        out_specs=[front, back],
+        out_shape=[shape_of(near_x.shape, BF), shape_of(near_y.shape, BF)],
+        input_output_aliases={0: 0, 1: 1},
+        compiler_params=pltpu.CompilerParams(vmem_limit_bytes=VMEM_BYTES),
+        cost_estimate=pl.CostEstimate(flops=2 * half * low, bytes_accessed=12 * half * low, transcendentals=0),
+    )(near_x, near_y, got_a, got_b)
+
+
+def settle(keep, got_x, got_y, parts, z_size):
+    total = add_low(keep, got_x, got_y)
+    total = jnp.swapaxes(total.reshape(parts, z_size, -1, keep.shape[1]), 0, 1)
     total = total.reshape(z_size, -1, keep.shape[1])
     return lax.psum_scatter(total, "z", scatter_dimension=0, tiled=False)
 
@@ -1097,13 +1123,32 @@
     )
     cuts = (0, four, four + hid_core, four + 2 * hid_core)
 
-    def gather(l, i):
+    def z_gather(l, i):
         by_z = lax.all_gather(shards[l, cuts[i] : cuts[i + 1]], "z", axis=0, tiled=False)
         if i == 0:
             by_z = jnp.swapaxes(by_z.reshape(z_size, 4, head_width, low), 0, 1)
-        return gather_blocks(by_z.reshape(-1, low))
-
-    blocks = [[gather(l, i) for i in range(3)] for l in range(layer_count)]
+        return by_z.reshape(-1, low)
+
+    def send(rows):
+        return rows, across(rows, "x"), across(rows, "y")
+
+    def send_on(state):
+        _, by_x, by_y = state
+        half = by_x.shape[0] // 2
+        return across(by_x[:half], "y"), across(by_y[half:], "x")
+
+    def whole(state, halves):
+        return (*state, jnp.concatenate(halves))
+
+    def together(*values):
+        return lax.optimization_barrier(values)
+
+    late = shards[1, cuts[2] :]
+    late_x, late_y = across(late, "x"), across(late, "y")
+    chunks = [z_gather(l, i) for l in range(layer_count) for i in range(3)][:5]
+    late_far = across(late_x, "y")
+    late_blocks = lax.all_gather(jnp.stack((late, late_y, late_x, late_far)), "z", axis=0, tiled=False)
+    sent = send(tie(chunks[0], late_far, late_y))
 
     cond_low = jax.nn.silu(cond.astype(F32)).astype(BF)
     silu_rows = lax.all_gather(cond_low, ("y", "core"), axis=0, tiled=True)
@@ -1166,35 +1211,70 @@
     ones = head_ones(low // 2, head_width)
 
     def own_tokens(values):
-        return jnp.pad(turned(trade(values), y, 1), ((0, rows_pad - rows_dev), (0, 0)))
+        return jnp.pad(turned(trade(values, core != x), y, 1), ((0, rows_pad - rows_dev), (0, 0)))
 
     state = own_tokens(hidden_in).astype(F32)
     grad = own_tokens(grad_out).astype(F32)
     hidden = (normalize(state)[0] * (1.0 + ada[0, 2][None]) + ada[0, 4][None]).astype(BF)
-    saved = []
-    for l in range(layer_count):
-        gamma1, gamma2, scale1, scale2, shift1, shift2 = [ada[l, i] for i in range(6)]
+    weights = [None] * 5 + [(late_blocks,) * 4]
+
+    def attn_start(l, hidden):
         vectors = eight_rows(bias_qkv[l, 0], bias_qkv[l, 1], scales[l])
-        joined1, q_raw, k_raw, q_low, k_low, v_low = qkv_up(
-            hidden, sibling(hidden), blocks[l][0], vectors, ones
-        )
-        attn, rest, logs = attn_mix(q_low, k_low, v_low, end_col, place_row, head_width)
-        own, send = attn_down(attn, blocks[l][0])
+        found = qkv_up(hidden, sibling(hidden), weights[3 * l], vectors, ones)
+        return found
+
+    def attn_end(l, attn, state):
+        own, send_own = attn_down(attn, weights[3 * l])
         branch, middle, hidden = mix(
-            own, sibling(send), state, eight_rows(bias_proj[l], gamma1, 1.0 + scale2, shift2), False
-        )
-        joined2, act, slope = fc_up(hidden, sibling(hidden), blocks[l][1], bias_fc1[l])
-        own, send = fc_down(act, blocks[l][2])
+            own, sibling(send_own), state,
+            eight_rows(bias_proj[l], ada[l, 0], 1.0 + ada[l, 3], ada[l, 5]), False,
+        )
+        return branch, middle, hidden
+
+    def fc_start(l, hidden):
+        return fc_up(hidden, sibling(hidden), weights[3 * l + 1], bias_fc1[l])
+
+    def fc_end(l, act, middle):
+        own, send_own = fc_down(act, weights[3 * l + 2])
         last = l == layer_count - 1
         after = ada[l if last else l + 1]
-        feed, later, hidden = mix(
-            own, sibling(send), middle, eight_rows(bias_fc2[l], gamma2, 1.0 + after[2], after[4]), last
-        )
-        saved.append(
-            (joined1, q_raw, k_raw, q_low, k_low, v_low, logs, attn, rest, branch, middle, joined2, act, slope, feed, state)
-        )
-        state = later
-    mixed = hidden
+        return mix(
+            own, sibling(send_own), middle,
+            eight_rows(bias_fc2[l], ada[l, 1], 1.0 + after[2], after[4]), last,
+        )
+
+    *sent, hidden, grad = together(*sent, hidden, grad)
+    halves = send_on(sent)
+    *halves, chunks[1], hidden = together(*halves, chunks[1], hidden)
+    weights[0], sent = whole(sent, halves), send(chunks[1])
+    found0 = attn_start(0, hidden)
+    attn0, rest0, logs0 = attn_mix(*found0[3:6], end_col, place_row, head_width)
+    *sent, attn0 = together(*sent, attn0)
+    halves = send_on(sent)
+    branch0, middle0, hidden2 = attn_end(0, attn0, state)
+    *halves, chunks[2], hidden2 = together(*halves, chunks[2], hidden2)
+    weights[1], sent = whole(sent, halves), send(chunks[2])
+    joined2, act, slope = fc_start(0, hidden2)
+    *sent, act = together(*sent, act)
+    halves = send_on(sent)
+    *halves, chunks[3], act = together(*halves, chunks[3], act)
+    weights[2], sent = whole(sent, halves), send(chunks[3])
+    feed, state1, hidden = fc_end(0, act, middle0)
+    saved = [(*found0, logs0, attn0, rest0, branch0, middle0, joined2, act, slope, feed, state)]
+    *sent, hidden = together(*sent, hidden)
+    halves = send_on(sent)
+    *halves, chunks[4], hidden = together(*halves, chunks[4], hidden)
+    weights[3], sent = whole(sent, halves), send(chunks[4])
+    found1 = attn_start(1, hidden)
+    attn1, rest1, logs1 = attn_mix(*found1[3:6], end_col, place_row, head_width)
+    *sent, attn1 = together(*sent, attn1)
+    halves = send_on(sent)
+    branch1, middle1, hidden2 = attn_end(1, attn1, state1)
+    *halves, hidden2 = together(*halves, hidden2)
+    weights[4] = whole(sent, halves)
+    joined2, act, slope = fc_start(1, hidden2)
+    feed, state2, mixed = fc_end(1, act, middle1)
+    saved.append((*found1, logs1, attn1, rest1, branch1, middle1, joined2, act, slope, feed, state1))
 
     top = layer_count - 1
     d_ada = [[None] * 6 for _ in range(layer_count)]
@@ -1202,36 +1282,99 @@
     d_weights = [None] * layer_count
     fold = lambda sums: jnp.sum(sums.reshape(-1, 8, sums.shape[1]), axis=1)
     d_low = (grad * ada[top, 1][None]).astype(BF)
-    d_ada[top][1] = jnp.sum(grad * saved[top][-2].astype(F32), axis=0)
+    d_ada[top][1] = jnp.sum(grad * saved[1][-2].astype(F32), axis=0)
     d_biases[top][1] = jnp.sum(d_low.astype(F32), axis=0)
-    for l in reversed(range(layer_count)):
-        gamma1, gamma2, scale1, scale2, shift1, shift2 = [ada[l, i] for i in range(6)]
-        (joined1, q_raw, k_raw, q_low, k_low, v_low, logs, attn, rest, branch, middle, joined2, act, slope, feed, state) = saved[l]
-        (sums_pre, own, send), two, one = fc_back(
-            d_low, sibling(d_low), blocks[l][2], blocks[l][1], slope, act, joined2
-        )
-        g_two = scatter_blocks(two, 1, z_size)
-        g_one = scatter_blocks(one, 1, z_size)
+    def fc_turn(l, d_low):
+        act, slope, joined2 = saved[l][-4], saved[l][-3], saved[l][-5]
+        return fc_back(
+            d_low, sibling(d_low), weights[3 * l + 2], weights[3 * l + 1], slope, act, joined2, l == 1
+        )
+
+    def fc_norm(l, found, grad):
+        sums_pre, own, send_own = found
         d_middle, d_low, sums = mix_back(
-            own, sibling(send), middle, grad, branch, eight_rows(1.0 + scale2, gamma1)
+            own, sibling(send_own), saved[l][10], grad, saved[l][9], eight_rows(1.0 + ada[l, 3], ada[l, 0])
         )
         d_ada[l][3], d_ada[l][5], d_ada[l][0], d_biases[l][0] = fold(sums)
-        (sums_qkv, own, send), four_parts = attn_back(
-            d_low, sibling(d_low), blocks[l][0], q_low, k_low, v_low, attn, rest, logs, q_raw, k_raw, joined1,
+        d_biases[l][3] = fold(sums_pre)[0]
+        return d_middle, d_low
+
+    def attn_turn(l, d_low):
+        joined1, q_raw, k_raw, q_low, k_low, v_low, logs, attn, rest = saved[l][:9]
+        return attn_back(
+            d_low, sibling(d_low), weights[3 * l], q_low, k_low, v_low, attn, rest, logs, q_raw, k_raw, joined1,
             eight_rows(scales[l]), place_col, end_row, head_width,
         )
-        g_attn = scatter_blocks(four_parts, 4, z_size)
+
+    def attn_norm(l, found, got_own, d_middle):
+        sums_qkv, own, _ = found
         before = max(l - 1, 0)
         grad, d_low, sums = mix_back(
-            own, sibling(send), state, d_middle, saved[before][-2], eight_rows(1.0 + scale1, ada[before, 1])
+            own, got_own, saved[l][-1], d_middle, saved[before][-2],
+            eight_rows(1.0 + ada[l, 2], ada[before, 1]),
         )
         sums = fold(sums)
         d_ada[l][2], d_ada[l][4] = sums[0], sums[1]
         if l > 0:
             d_ada[l - 1][1], d_biases[l - 1][1] = sums[2], sums[3]
-        d_head = jnp.sum(sums_qkv[2].reshape(heads, head_width), axis=1)
-        d_biases[l][2:] = sums_qkv[:2], fold(sums_pre)[0], d_head
-        d_weights[l] = jnp.concatenate((g_attn, g_one, g_two), axis=0)
+        d_biases[l][2] = sums_qkv[:2]
+        d_biases[l][4] = jnp.sum(sums_qkv[2].reshape(heads, head_width), axis=1)
+        return grad, d_low
+
+    def halves_of(blocks):
+        return across(blocks[3][:low], "y"), across(blocks[3][low:], "x")
+
+    def given_back(values):
+        return trade(turned(values[:rows_dev], y, 1).astype(BF), core != x)
+
+    mixed = given_back(mixed)
+    found, two, one = fc_turn(1, d_low)
+    mixed, *found = together(mixed, *found)
+    two_sum = lax.psum_scatter(two[0], "z", scatter_dimension=0, tiled=False)
+    got_a, got_b = halves_of(one)
+    d_middle, d_low = fc_norm(1, found, grad)
+    got_a, got_b, d_low = together(got_a, got_b, d_low)
+    near_x, near_y = near_parts(one, got_a, got_b)
+    one_x, one_y = across(near_x, "x"), across(near_y, "y")
+    found, four_parts = attn_turn(1, d_low)
+    one_x, one_y, *found = together(one_x, one_y, *found)
+    last = flat(four_parts)
+    got_a, got_b = halves_of(last)
+    grad, d_low = attn_norm(1, found, sibling(found[2]), d_middle)
+    got_a, got_b, d_low = together(got_a, got_b, d_low)
+    near_x, near_y = near_parts(last, got_a, got_b)
+    last_x, last_y = across(near_x, "x"), across(near_y, "y")
+    g_one1 = settle(one[0], one_x, one_y, 1, z_size)
+    found, two, one = fc_turn(0, d_low)
+    last_x, last_y, two_sum, *found = together(last_x, last_y, two_sum, *found)
+    got_a, got_b = halves_of(one)
+    d_middle, d_low = fc_norm(0, found, grad)
+    got_a, got_b, d_low = together(got_a, got_b, d_low)
+    near_x, near_y = near_parts(one, got_a, got_b)
+    one_x, one_y = across(near_x, "x"), across(near_y, "y")
+    far_a, far_b = halves_of(two)
+    g_attn1 = settle(last[0], last_x, last_y, 4, z_size)
+    found, four_parts = attn_turn(0, d_low)
+    one_x, one_y, far_a, far_b, *found = together(one_x, one_y, far_a, far_b, *found)
+    last = flat(four_parts)
+    got_a, got_b = halves_of(last)
+    got_own = sibling(found[2])
+    near_x, near_y = near_parts(two, far_a, far_b)
+    got_own, near_x, near_y = together(got_own, near_x, near_y)
+    two_x, two_y = across(near_x, "x"), across(near_y, "y")
+    grad, d_low = attn_norm(0, found, got_own, d_middle)
+    got_a, got_b, one_x, grad = together(got_a, got_b, one_x, grad)
+    g_one0 = settle(one[0], one_x, one_y, 1, z_size)
+    two_x, two_y, got_a = together(two_x, two_y, got_a)
+    near_x, near_y = near_parts(last, got_a, got_b)
+    last_x, last_y = across(near_x, "x"), across(near_y, "y")
+    g_two0 = settle(two[0], two_x, two_y, 1, z_size)
+    last_x, last_y, two_sum = together(last_x, last_y, two_sum)
+    late_far, late_y = across(two_sum[3], "y"), across(two_sum[1], "y")
+    g_attn0 = settle(last[0], last_x, last_y, 4, z_size)
+    late_x = across(add_low(two_sum[2], late_far), "x")
+    g_two1 = add_low(two_sum[0], late_x, late_y)
+    d_weights = [jnp.concatenate(v, axis=0) for v in ((g_attn0, g_one0, g_two0), (g_attn1, g_one1, g_two1))]
 
     def by_col(values):
         values = turned(values, y, values.ndim - 1)
@@ -1290,11 +1433,8 @@
     def pick(i, j):
         return jnp.concatenate((first[:, i:j], second[:, i:j]), axis=1)
 
-    def given_back(values):
-        return trade(turned(values[:rows_dev], y, 1))
-
     return (
-        given_back(mixed), given_back(grad), out_w_ada, out_b_ada, out_w_qkv, out_b_qkv, out_scale,
+        mixed, given_back(grad).astype(F32), out_w_ada, out_b_ada, out_w_qkv, out_b_qkv, out_scale,
         pick(three, four), out_b_proj, jnp.swapaxes(pick(cuts[1], cuts[2]), 1, 2), out_b_fc1,
         pick(cuts[2], cuts[3]), out_b_fc2,
     )

time: 717 us -> 660 us (0.921)
  waiting for transfers between devices: 208 us -> 178 us
  Pallas kernels: 259 us -> 239 us
  other arithmetic: 62.7 us -> 42.7 us
  local copies, waits for them, and re-layouts: 63.2 us -> 77.9 us
    all_gather x6, waiting for transfers between devices: 47.4 us -> 0.04 us  [the longest x5 0.04 us: z_gather(): lax.all_gather(shards[l, cuts[i]:cuts[i + 1]], 'z', axis=0, tiled=False)]
    pallas_call x22, Pallas kernels: 259 us -> 225 us  [call(): pl.pallas_call(body, grid=grid, in_specs=in_specs, out_specs=out_specs, o...]
    dynamic_update_slice x12 -> x0, other arithmetic: 24.6 us -> none  [added(): return lax.dynamic_update_slice_in_dim(block, part.astype(BF), start, 0)]
    ppermute x4, waiting for transfers between devices: 0.01 us -> 23.6 us  [trade(): lax.ppermute(values, ('core', 'x'), [(1, 2), (2, 1)])]
    all_to_all x1, waiting for transfers between devices: 16.7 us -> 0.01 us  [on_pair(): lax.all_to_all(pack.reshape(n_rows * z_size * x_size, -1), ('y', 'core',...]
    pallas_call x0 -> x5, Pallas kernels: none -> 13.5 us  [near_parts(): pl.pallas_call(body, grid=(1,), in_specs=[front, back, front, front], out...]
    ppermute x19, starting transfers between devices: 32.7 us -> 25.1 us  [sibling(): return lax.ppermute(values, 'core', [(0, 1), (1, 0)])]
    unnamed x161 -> x216, local copies, waits for them, and re-layouts: 20.9 us -> 27.3 us
  transfers between devices with their start and end apart: 85 -> 83, of which waited for: 27 -> 40; matrix products, arithmetic and copies ran while one was open for 14% -> 14% of each run, Pallas kernels for 36% -> 32%
where the time goes in v3:
time: 660 us; the launch traced here: 651 us
  Pallas kernels  239 us (36%)
  waiting for transfers between devices  178 us (27%)
  starting transfers between devices  87.7 us (13%)
  local copies, waits for them, and re-layouts  77.9 us (12%)
  other arithmetic  42.7 us (6%)
  between operations  16.7 us (3%)
    pallas_call x22, Pallas kernels, call(): pl.pallas_call(body, grid=grid, in_specs=in_specs, out_specs=out_specs, o...  225 us
    ppermute x46, waiting for transfers between devices, across(): return lax.ppermute(values, axis, [(0, 1), (1, 0)])  137 us
    ppermute x46, starting transfers between devices, across(): return lax.ppermute(values, axis, [(0, 1), (1, 0)])  35.9 us
    unnamed x216, local copies, waits for them, and re-layouts  27.3 us
    ppermute x19, starting transfers between devices, sibling(): return lax.ppermute(values, 'core', [(0, 1), (1, 0)])  25.1 us
    ppermute x4, waiting for transfers between devices, trade(): lax.ppermute(values, ('core', 'x'), [(1, 2), (2, 1)])  23.6 us
    ppermute x4, starting transfers between devices, trade(): lax.ppermute(values, ('core', 'x'), [(1, 2), (2, 1)])  14.8 us
    pallas_call x5, Pallas kernels, near_parts(): pl.pallas_call(body, grid=(1,), in_specs=[front, back, front, front], out...  13.5 us
  transfers between devices with their start and end apart: 83, of which 40 were waited for; matrix products, arithmetic and copies ran while one was open for 14% of the time, Pallas kernels for 32%

profile of v3, /device:TPU:1, one launch (start us, length us, event | category | flops | bytes accessed | tf_op | source)
XLA Modules:
  0.0 650.6 jit_solution(12680161887851091920)
XLA Ops:
  11.7 6.4 all-gather.1
  23.5 5.8 all-to-all-start
  38.7 6.1 all-to-all-done
  60.3 5.8 collective-permute-done.2
  72.4 18.6 %collective-permute-done.4.gx.refs_2_.refs_6_.refs_10_.refs_14_ = bf16[1024,512]{1,0:T(8,128)(2,1)S(1)} collective-permute-done((bf16[1024,512]{1,0:T(8,128)(2,1)S(1)}, bf16[1024,512]{1,0:T(8,128)(2,1)S(1)}, u32[]{:S(2)}, u32[]{:S(2)}) %collective-permute-start.4) | collective-permute-done | bytes 1048608 | tf_op jit(solution)/shard_map/ppermute | solution.py:415
  96.2 8.3 %collective-permute-done.8 = bf16[512,512]{1,0:T(8,128)(2,1)} collective-permute-done((bf16[512,512]{1,0:T(8,128)(2,1)}, bf16[512,512]{1,0:T(8,128)(2,1)}, u32[]{:S(2)}, u32[]{:S(2)}) %collective-permute-start.8) | collective-permute-done | bytes 524320 | tf_op jit(solution)/shard_map/ppermute | solution.py:415
  119.3 10.7 %shard_map.246 = (bf16[704,1024]{1,0:T(8,128)(2,1)}, bf16[704,512]{1,0:T(8,128)(2,1)}, bf16[704,512]{1,0:T(8,128)(2,1)}, bf16[704,512]{1,0:T(8,128)(2,1)}, bf16[...) custom-call(bf16[352,1024]{1,0:T(8,128)(2,1)} %add_convert_fusion.3.own_ref, ...), custom_call_target="tpu_custom_call" | custom-call | flops 34603008 | bytes 173056 | tf_op jit(solution)/shard_map/pallas_call | solution.py:436
  130.0 9.6 %shard_map.247 = (bf16[704,512]{1,0:T(8,128)(2,1)}, bf16[704,512]{1,0:T(8,128)(2,1)}, f32[704,512]{1,0:T(8,128)}) custom-call(bf16[704,512]{1,0:T(8,128)(2,1)} %get-tuple-element.204.q_ref.refs_16_, bf16[704,512]{1,0:T(8,128)(2,1)} %get-tuple-element.205.k_ref.refs_17_, bf16[704,512]{1,0:T(8,128)(2,1)} %get-tuple-element.206.v_ref.refs_18_, ...), custom_call_target="tpu_custom_call" | custom-call | flops 15859712 | bytes 78848 | tf_op jit(solution)/shard_map/pallas_call | solution.py:436
  167.8 10.3 %shard_map.250 = (bf16[704,1024]{1,0:T(8,128)(2,1)}, bf16[704,2048]{1,0:T(8,128)(2,1)}, bf16[704,2048]{1,0:T(8,128)(2,1)}) custom-call(bf16[352,1024]{1,0:T(8,128)(2,1)} %get-tuple-element.215.own_ref, bf16[352,1024]{1,0:T(8,128)(2,1)} %collective-permute-done.19.other_ref, bf16[1024,512]{1,0:T(8,128)(2,1)} %bitcast.294, ...), custom_call_target="tpu_custom_call" | custom-call | flops 46137344 | bytes 223232 | tf_op jit(solution)/shard_map/pallas_call | solution.py:436
  178.1 6.0 collective-permute-done.17.gx.ugx
  188.5 7.7 %collective-permute-done.20 = bf16[512,512]{1,0:T(8,128)(2,1)} collective-permute-done((bf16[512,512]{1,0:T(8,128)(2,1)}, bf16[512,512]{1,0:T(8,128)(2,1)}, u32[]{:S(2)}, u32[]{:S(2)}) %collective-permute-start.20) | collective-permute-done | bytes 524320 | tf_op jit(solution)/shard_map/ppermute | solution.py:415
  203.1 7.5 %shard_map.251 = (f32[352,1024]{1,0:T(8,128)}, bf16[352,1024]{1,0:T(8,128)(2,1)}) custom-call(bf16[704,2048]{1,0:T(8,128)(2,1)} %get-tuple-element.224.left_ref.act_ref, bf16[1024,512]{1,0:T(8,128)(2,1)} %bitcast.290, bf16[1024,512]{1,0:T(8,128)(2,1)} %copy-done.12, bf16[1024,512]{1,0:T(8,128)(2,1)} %copy-done.13, ...), custom_call_target="tpu_custom_call" | custom-call | flops 46137344 | bytes 144384 | tf_op jit(solution)/shard_map/pallas_call | solution.py:436
  210.6 5.1 collective-permute-start.24
  223.6 10.3 %collective-permute-done.25 = bf16[512,512]{1,0:T(8,128)(2,1)S(1)} collective-permute-done((bf16[512,512]{1,0:T(8,128)(2,1)}, bf16[512,512]{1,0:T(8,128)(2,1)S(1)}, u32[]{:S(2)}, u32[]{:S(2)}) %collective-permute-start.25) | collective-permute-done | bytes 524320 | tf_op jit(solution)/shard_map/ppermute | solution.py:415
  244.3 10.7 %shard_map.253 = (bf16[704,1024]{1,0:T(8,128)(2,1)}, bf16[704,512]{1,0:T(8,128)(2,1)}, bf16[704,512]{1,0:T(8,128)(2,1)}, bf16[704,512]{1,0:T(8,128)(2,1)}, bf16[...) custom-call(bf16[352,1024]{1,0:T(8,128)(2,1)} %get-tuple-element.236.own_ref, ...), custom_call_target="tpu_custom_call" | custom-call | flops 34603008 | bytes 173056 | tf_op jit(solution)/shard_map/pallas_call | solution.py:436
  255.0 9.6 %shard_map.254 = (bf16[704,512]{1,0:T(8,128)(2,1)}, bf16[704,512]{1,0:T(8,128)(2,1)}, f32[704,512]{1,0:T(8,128)}) custom-call(bf16[704,512]{1,0:T(8,128)(2,1)} %get-tuple-element.240.q_ref.refs_16_, bf16[704,512]{1,0:T(8,128)(2,1)} %get-tuple-element.241.k_ref.refs_17_, bf16[704,512]{1,0:T(8,128)(2,1)} %get-tuple-element.242.v_ref.refs_18_, ...), custom_call_target="tpu_custom_call" | custom-call | flops 15859712 | bytes 78848 | tf_op jit(solution)/shard_map/pallas_call | solution.py:436
  276.9 5.6 collective-permute-done.30
  288.5 10.3 %shard_map.257 = (bf16[704,1024]{1,0:T(8,128)(2,1)}, bf16[704,2048]{1,0:T(8,128)(2,1)}, bf16[704,2048]{1,0:T(8,128)(2,1)}) custom-call(bf16[352,1024]{1,0:T(8,128)(2,1)} %get-tuple-element.251.own_ref, bf16[352,1024]{1,0:T(8,128)(2,1)} %copy-done.41, bf16[1024,512]{1,0:T(8,128)(2,1)} %bitcast.299, bf16[1024,512]{1,0:T(8,128)(2,1)} %collective-permute-done.27.gx.dgx, ...), custom_call_target="tpu_custom_call" | custom-call | flops 46137344 | bytes 223232 | tf_op jit(solution)/shard_map/pallas_call | solution.py:436
  298.8 7.5 %shard_map.258 = (f32[352,1024]{1,0:T(8,128)}, bf16[352,1024]{1,0:T(8,128)(2,1)}) custom-call(bf16[704,2048]{1,0:T(8,128)(2,1)} %get-tuple-element.255.left_ref.act_ref, bf16[4,4,256,512]{3,2,1,0:T(8,128)(2,1)} %bitcast.264, bf16[4,4,256,512]{3,2,1,0:T(8,128)(2,1)} %bitcast.265, bf16[4,4,256,512]{3,2,1,0:T(8,128)(2,1)} %bitcast.266, ...), custom_call_target="tpu_custom_call" | custom-call | flops 46137344 | bytes 144384 | tf_op jit(solution)/shard_map/pallas_call | solution.py:436
  317.6 20.6 %shard_map.260 = (f32[8,2048]{1,0:T(8,128)}, f32[352,1024]{1,0:T(8,128)}, bf16[352,1024]{1,0:T(8,128)(2,1)}, bf16[4,4,256,512]{3,2,1,0:T(8,128)(2,1)}, bf16[1024...) custom-call(bf16[352,1024]{1,0:T(8,128)(2,1)} %copy-done.18, ...), custom_call_target="tpu_custom_call" | custom-call | flops 184549376 | bytes 453632 | tf_op jit(solution)/shard_map/pallas_call | solution.py:436
  343.1 9.5 %collective-permute-done.35 = bf16[340,1024]{1,0:T(8,128)(2,1)S(1)} collective-permute-done((bf16[340,1024]{1,0:T(8,128)(2,1)S(1)}, bf16[340,1024]{1,0:T(8,128)(2,1)S(1)}, u32[]{:S(2)}, u32[]{:S(2)}) %collective-permute-start.35) | collective-permute-done | bytes 696352 | tf_op jit(solution)/shard_map/ppermute | solution.py:419
  361.9 5.0 collective-permute-done.37.a_ref
  376.3 33.9 %shard_map.262 = (f32[8,512]{1,0:T(8,128)}, f32[352,1024]{1,0:T(8,128)}, bf16[352,1024]{1,0:T(8,128)(2,1)}, bf16[4,2,128,512]{3,2,1,0:T(8,128)(2,1)}, bf16[4,2,1...) custom-call(bf16[352,1024]{1,0:T(8,128)(2,1)} %get-tuple-element.272.own_ref, ...), custom_call_target="tpu_custom_call" | custom-call | flops 131923968 | bytes 225280 | tf_op jit(solution)/shard_map/pallas_call | solution.py:436
  435.1 20.9 %shard_map.265 = (f32[8,2048]{1,0:T(8,128)}, f32[352,1024]{1,0:T(8,128)}, bf16[352,1024]{1,0:T(8,128)(2,1)}, bf16[1024,512]{1,0:T(8,128)(2,1)}, bf16[1024,512]{1...) custom-call(bf16[352,1024]{1,0:T(8,128)(2,1)} %get-tuple-element.293, ...), custom_call_target="tpu_custom_call" | custom-call | flops 184549376 | bytes 453632 | tf_op jit(solution)/shard_map/pallas_call | solution.py:436
  467.0 5.5 collective-permute-done.47.a_ref
  482.4 34.0 %shard_map.268 = (f32[8,512]{1,0:T(8,128)}, f32[352,1024]{1,0:T(8,128)}, bf16[352,1024]{1,0:T(8,128)(2,1)}, bf16[4,2,128,512]{3,2,1,0:T(8,128)(2,1)}, bf16[4,2,1...) custom-call(bf16[352,1024]{1,0:T(8,128)(2,1)} %get-tuple-element.312.own_ref, ...), custom_call_target="tpu_custom_call" | custom-call | flops 131923968 | bytes 225280 | tf_op jit(solution)/shard_map/pallas_call | solution.py:436
  540.7 20.8 %collective-permute-done.61 = bf16[1024,512]{1,0:T(8,128)(2,1)} collective-permute-done((bf16[1024,512]{1,0:T(8,128)(2,1)S(1)}, bf16[1024,512]{1,0:T(8,128)(2,1)}, u32[]{:S(2)}, u32[]{:S(2)}) %collective-permute-start.61) | collective-permute-done | bytes 1048608 | tf_op jit(solution)/shard_map/ppermute | solution.py:415
  571.1 5.8 collective-permute-start.60
  578.9 4.8 all-to-all-start.1
  583.8 8.9 %collective-permute-done.63 = bf16[1024,512]{1,0:T(8,128)(2,1)S(1)} collective-permute-done((bf16[1024,512]{1,0:T(8,128)(2,1)}, bf16[1024,512]{1,0:T(8,128)(2,1)S(1)}, u32[]{:S(2)}, u32[]{:S(2)}) %collective-permute-start.63) | collective-permute-done | bytes 1048608 | tf_op jit(solution)/shard_map/ppermute | solution.py:415
  595.9 9.5 %collective-permute-done.60 = bf16[340,1024]{1,0:T(8,128)(2,1)} collective-permute-done((bf16[340,1024]{1,0:T(8,128)(2,1)S(1)}, bf16[340,1024]{1,0:T(8,128)(2,1)}, u32[]{:S(2)}, u32[]{:S(2)}) %collective-permute-start.60) | collective-permute-done | bytes 696352 | tf_op jit(solution)/shard_map/ppermute | solution.py:419
  610.8 6.8 %collective-permute-done.65 = bf16[256,512]{1,0:T(8,128)(2,1)S(1)} collective-permute-done((bf16[256,512]{1,0:T(8,128)(2,1)S(1)}, bf16[256,512]{1,0:T(8,128)(2,1)S(1)}, u32[]{:S(2)}, u32[]{:S(2)}) %collective-permute-start.65) | collective-permute-done | bytes 262176 | tf_op jit(solution)/shard_map/ppermute | solution.py:415
  (658 shorter events, 285.9 us)
Async XLA Ops:
  7.2 50.9 %all-gather.9.cloned.1.call-start = ((), (), s32[]{:S(2)}) async-start(), calls=%async_computation.8 | async-start | bytes 1310720 | tf_op jit(solution)/shard_map/all_gather | solution.py:1127
  29.4 66.8 %all-gather.11.cloned.1.call-start = ((), (), s32[]{:S(2)}) async-start(), calls=%async_computation.9 | async-start | bytes 1310720 | tf_op jit(solution)/shard_map/all_gather | solution.py:1127
  35.9 119.7 %all-gather.13.cloned.1.call-start = ((), (), s32[]{:S(2)}) async-start(), calls=%async_computation.10 | async-start | bytes 1310720 | tf_op jit(solution)/shard_map/all_gather | solution.py:1127
  45.9 141.3 %all-gather.15.cloned.1.call-start = ((), (), s32[]{:S(2)}) async-start(), calls=%async_computation.11 | async-start | bytes 1310720 | tf_op jit(solution)/shard_map/all_gather | solution.py:1127
  54.9 168.7 %all-gather.17.cloned.1.call-start = ((), (), s32[]{:S(2)}) async-start(), calls=%async_computation.12 | async-start | bytes 1310720 | tf_op jit(solution)/shard_map/all_gather | solution.py:1127
  66.8 24.2 %collective-permute-start.4 = (bf16[1024,512]{1,0:T(8,128)(2,1)S(1)}, bf16[1024,512]{1,0:T(8,128)(2,1)S(1)}, u32[]{:S(2)}, u32[]{:S(2)}) collective-permute-start(bf16[1024,512]{1,0:T(8,128)(2,1)S(1)} %bitcast.272), channel_id=1, source_target_pairs={{0,1},{1,0},{2,3},{3,2},{4,5},{5,4},{6,7},{7,6},{8,9},{9,8},{10,11... | collective-permute-start | bytes 3145736 | tf_op jit(solution)/shard_map/ppermute | solution.py:415
  66.9 24.1 %collective-permute-start.5 = (bf16[1024,512]{1,0:T(8,128)(2,1)S(1)}, bf16[1024,512]{1,0:T(8,128)(2,1)S(1)}, u32[]{:S(2)}, u32[]{:S(2)}) collective-permute-start(bf16[1024,512]{1,0:T(8,128)(2,1)S(1)} %bitcast.273), channel_id=1, source_target_pairs={{0,16},{16,0},{1,17},{17,1},{2,18},{18,2},{3,19},{19,3},{4,20},{20... | collective-permute-start | bytes 3145736 | tf_op jit(solution)/shard_map/ppermute | solution.py:415
  72.3 226.5 %all-gather.19.cloned.1.call-start = ((), (), s32[]{:S(2)}) async-start(), calls=%async_computation.19 | async-start | bytes 5242880 | tf_op jit(solution)/shard_map/all_gather | solution.py:1150
  106.5 33.1 %collective-permute-start.10 = (bf16[1024,512]{1,0:T(8,128)(2,1)}, bf16[1024,512]{1,0:T(8,128)(2,1)}, u32[]{:S(2)}, u32[]{:S(2)}) collective-permute-start(bf16[1024,512]{1,0:T(8,128)(2,1)} %bitcast.292), channel_id=1, source_target_pairs={{0,1},{1,0},{2,3},{3,2},{4,5},{5,4},{6,7},{7,6},{8,9},{9,8},{10,11... | collective-permute-start | bytes 3145736 | tf_op jit(solution)/shard_map/ppermute | solution.py:415
  107.3 32.3 %collective-permute-start.11 = (bf16[1024,512]{1,0:T(8,128)(2,1)}, bf16[1024,512]{1,0:T(8,128)(2,1)}, u32[]{:S(2)}, u32[]{:S(2)}) collective-permute-start(bf16[1024,512]{1,0:T(8,128)(2,1)} %bitcast.293), channel_id=1, source_target_pairs={{0,16},{16,0},{1,17},{17,1},{2,18},{18,2},{3,19},{19,3},{4,20},{20... | collective-permute-start | bytes 3145736 | tf_op jit(solution)/shard_map/ppermute | solution.py:415
  115.6 340.5 %reduce-scatter.7.cloned.1.call-start = ((), (), s32[]{:S(2)}) async-start(), calls=%async_computation.13 | async-start | bytes 5242880 | tf_op jit(solution)/shard_map/reduce_scatter | solution.py:1333
  197.0 24.4 %collective-permute-start.22 = (bf16[1024,512]{1,0:T(8,128)(2,1)S(1)}, bf16[1024,512]{1,0:T(8,128)(2,1)S(1)}, u32[]{:S(2)}, u32[]{:S(2)}) collective-permute-start(bf16[1024,512]{1,0:T(8,128)(2,1)S(1)} %bitcast.280), channel_id=1, source_target_pairs={{0,1},{1,0},{2,3},{3,2},{4,5},{5,4},{6,7},{7,6},{8,9},{9,8},{10,11... | collective-permute-start | bytes 3145736 | tf_op jit(solution)/shard_map/ppermute | solution.py:415
  197.9 23.5 %collective-permute-start.23 = (bf16[1024,512]{1,0:T(8,128)(2,1)S(1)}, bf16[1024,512]{1,0:T(8,128)(2,1)S(1)}, u32[]{:S(2)}, u32[]{:S(2)}) collective-permute-start(bf16[1024,512]{1,0:T(8,128)(2,1)S(1)} %bitcast.281), channel_id=1, source_target_pairs={{0,16},{16,0},{1,17},{17,1},{2,18},{18,2},{3,19},{19,3},{4,20},{20... | collective-permute-start | bytes 3145736 | tf_op jit(solution)/shard_map/ppermute | solution.py:415
  234.0 30.7 %collective-permute-start.27 = (bf16[1024,512]{1,0:T(8,128)(2,1)}, bf16[1024,512]{1,0:T(8,128)(2,1)}, u32[]{:S(2)}, u32[]{:S(2)}) collective-permute-start(bf16[1024,512]{1,0:T(8,128)(2,1)} %bitcast.297), channel_id=1, source_target_pairs={{0,1},{1,0},{2,3},{3,2},{4,5},{5,4},{6,7},{7,6},{8,9},{9,8},{10,11... | collective-permute-start | bytes 3145736 | tf_op jit(solution)/shard_map/ppermute | solution.py:415
  234.1 30.5 %collective-permute-start.28 = (bf16[1024,512]{1,0:T(8,128)(2,1)}, bf16[1024,512]{1,0:T(8,128)(2,1)}, u32[]{:S(2)}, u32[]{:S(2)}) collective-permute-start(bf16[1024,512]{1,0:T(8,128)(2,1)} %bitcast.298), channel_id=1, source_target_pairs={{0,16},{16,0},{1,17},{17,1},{2,18},{18,2},{3,19},{19,3},{4,20},{20... | collective-permute-start | bytes 3145736 | tf_op jit(solution)/shard_map/ppermute | solution.py:415
  338.2 287.1 %reduce-scatter.17.cloned.1.call-start = ((), (), s32[]{:S(2)}) async-start(), calls=%async_computation.18 | async-start | bytes 1310720 | tf_op jit(solution)/shard_map/reduce_scatter | solution.py:1079
  370.8 39.4 %collective-permute-start.43 = (bf16[1024,512]{1,0:T(8,128)(2,1)}, bf16[1024,512]{1,0:T(8,128)(2,1)S(1)}, u32[]{:S(2)}, u32[]{:S(2)}) collective-permute-start(bf16[1024,512]{1,0:T(8,128)(2,1)} %get-tuple-element.283), channel_id=1, source_target_pairs={{0,1},{1,0},{2,3},{3,2},{4,5},{5,4},{6,7},{7,6},{8,9},{9,8},{10,11... | collective-permute-start | bytes 3145736 | tf_op jit(solution)/shard_map/ppermute | solution.py:415
  372.3 37.9 %collective-permute-start.44 = (bf16[1024,512]{1,0:T(8,128)(2,1)}, bf16[1024,512]{1,0:T(8,128)(2,1)S(1)}, u32[]{:S(2)}, u32[]{:S(2)}) collective-permute-start(bf16[1024,512]{1,0:T(8,128)(2,1)} %get-tuple-element.284), channel_id=1, source_target_pairs={{0,16},{16,0},{1,17},{17,1},{2,18},{18,2},{3,19},{19,3},{4,20},{20... | collective-permute-start | bytes 3145736 | tf_op jit(solution)/shard_map/ppermute | solution.py:415
  416.0 209.3 %reduce-scatter.15.cloned.1.call-start = ((), (), s32[]{:S(2)}) async-start(), calls=%async_computation.17 | async-start | bytes 1310720 | tf_op jit(solution)/shard_map/reduce_scatter | solution.py:1079
  429.9 26.2 %collective-permute-start.49 = (bf16[1024,512]{1,0:T(8,128)(2,1)}, bf16[1024,512]{1,0:T(8,128)(2,1)S(1)}, u32[]{:S(2)}, u32[]{:S(2)}) collective-permute-start(bf16[1024,512]{1,0:T(8,128)(2,1)} %get-tuple-element.301), channel_id=1, source_target_pairs={{0,1},{1,0},{2,3},{3,2},{4,5},{5,4},{6,7},{7,6},{8,9},{9,8},{10,11... | collective-permute-start | bytes 3145736 | tf_op jit(solution)/shard_map/ppermute | solution.py:415
  430.6 25.5 %collective-permute-start.50 = (bf16[1024,512]{1,0:T(8,128)(2,1)}, bf16[1024,512]{1,0:T(8,128)(2,1)S(1)}, u32[]{:S(2)}, u32[]{:S(2)}) collective-permute-start(bf16[1024,512]{1,0:T(8,128)(2,1)} %get-tuple-element.302), channel_id=1, source_target_pairs={{0,16},{16,0},{1,17},{17,1},{2,18},{18,2},{3,19},{19,3},{4,20},{20... | collective-permute-start | bytes 3145736 | tf_op jit(solution)/shard_map/ppermute | solution.py:415
  462.2 164.2 %reduce-scatter.11.cloned.1.call-start = ((), (), s32[]{:S(2)}) async-start(), calls=%async_computation.15 | async-start | bytes 1310720 | tf_op jit(solution)/shard_map/reduce_scatter | solution.py:1079
  475.8 40.7 %collective-permute-start.55 = (bf16[1024,512]{1,0:T(8,128)(2,1)}, bf16[1024,512]{1,0:T(8,128)(2,1)S(1)}, u32[]{:S(2)}, u32[]{:S(2)}) collective-permute-start(bf16[1024,512]{1,0:T(8,128)(2,1)} %get-tuple-element.323), channel_id=1, source_target_pairs={{0,1},{1,0},{2,3},{3,2},{4,5},{5,4},{6,7},{7,6},{8,9},{9,8},{10,11... | collective-permute-start | bytes 3145736 | tf_op jit(solution)/shard_map/ppermute | solution.py:415
  476.7 39.8 %collective-permute-start.56 = (bf16[1024,512]{1,0:T(8,128)(2,1)}, bf16[1024,512]{1,0:T(8,128)(2,1)S(1)}, u32[]{:S(2)}, u32[]{:S(2)}) collective-permute-start(bf16[1024,512]{1,0:T(8,128)(2,1)} %get-tuple-element.324), channel_id=1, source_target_pairs={{0,16},{16,0},{1,17},{17,1},{2,18},{18,2},{3,19},{19,3},{4,20},{20... | collective-permute-start | bytes 3145736 | tf_op jit(solution)/shard_map/ppermute | solution.py:415
  480.5 35.8 %collective-permute-start.57 = (bf16[512,512]{1,0:T(8,128)(2,1)}, bf16[512,512]{1,0:T(8,128)(2,1)S(1)}, u32[]{:S(2)}, u32[]{:S(2)}) collective-permute-start(bf16[512,512]{1,0:T(8,128)(2,1)} %get-tuple-element.496), channel_id=1, source_target_pairs={{0,16},{16,0},{1,17},{17,1},{2,18},{18,2},{3,19},{19,3},{4,20},{20... | collective-permute-start | bytes 1572872 | tf_op jit(solution)/shard_map/ppermute | solution.py:415
  481.6 34.8 %collective-permute-start.58 = (bf16[512,512]{1,0:T(8,128)(2,1)}, bf16[512,512]{1,0:T(8,128)(2,1)S(1)}, u32[]{:S(2)}, u32[]{:S(2)}) collective-permute-start(bf16[512,512]{1,0:T(8,128)(2,1)} %get-tuple-element.495), channel_id=1, source_target_pairs={{0,1},{1,0},{2,3},{3,2},{4,5},{5,4},{6,7},{7,6},{8,9},{9,8},{10,11... | collective-permute-start | bytes 1572872 | tf_op jit(solution)/shard_map/ppermute | solution.py:415
  537.5 89.0 %reduce-scatter.13.cloned.1.call-start = ((), (), s32[]{:S(2)}) async-start(), calls=%async_computation.16 | async-start | bytes 1310720 | tf_op jit(solution)/shard_map/reduce_scatter | solution.py:1079
  537.9 23.6 %collective-permute-start.61 = (bf16[1024,512]{1,0:T(8,128)(2,1)S(1)}, bf16[1024,512]{1,0:T(8,128)(2,1)}, u32[]{:S(2)}, u32[]{:S(2)}) collective-permute-start(bf16[1024,512]{1,0:T(8,128)(2,1)S(1)} %copy-done.21), channel_id=1, source_target_pairs={{0,1},{1,0},{2,3},{3,2},{4,5},{5,4},{6,7},{7,6},{8,9},{9,8},{10,11... | collective-permute-start | bytes 3145736 | tf_op jit(solution)/shard_map/ppermute | solution.py:415
  569.1 23.5 %collective-permute-start.63 = (bf16[1024,512]{1,0:T(8,128)(2,1)}, bf16[1024,512]{1,0:T(8,128)(2,1)S(1)}, u32[]{:S(2)}, u32[]{:S(2)}) collective-permute-start(bf16[1024,512]{1,0:T(8,128)(2,1)} %get-tuple-element.359), channel_id=1, source_target_pairs={{0,1},{1,0},{2,3},{3,2},{4,5},{5,4},{6,7},{7,6},{8,9},{9,8},{10,11... | collective-permute-start | bytes 3145736 | tf_op jit(solution)/shard_map/ppermute | solution.py:415
  571.1 34.3 %collective-permute-start.60 = (bf16[340,1024]{1,0:T(8,128)(2,1)S(1)}, bf16[340,1024]{1,0:T(8,128)(2,1)}, u32[]{:S(2)}, u32[]{:S(2)}) collective-permute-start(bf16[340,1024]{1,0:T(8,128)(2,1)S(1)} %fusion.4), channel_id=1, source_target_pairs={{1,8},{8,1},{3,10},{10,3},{5,12},{12,5},{7,14},{14,7},{17,24},{24,... | collective-permute-start | bytes 2088968 | tf_op jit(solution)/shard_map/ppermute | solution.py:419
  578.9 28.8 %all-to-all-start.1 = ((f32[32,1,2818]{2,1,0:T(1,128)}), f32[32,1,2818]{2,1,0:T(1,128)S(1)}, u32[]{:S(2)}, u32[]{:S(2)}) async-start(f32[32,1,2818]{2,1,0:T(1,128)} %all_to_all.14), calls=%async_computation.2 | async-start | bytes 753664 | tf_op jit(solution)/shard_map/all_to_all | solution.py:1398
  583.7 47.1 %reduce-scatter.9.cloned.1.call-start = ((), (), s32[]{:S(2)}) async-start(), calls=%async_computation.14 | async-start | bytes 1310720 | tf_op jit(solution)/shard_map/reduce_scatter | solution.py:1079
  (146 other events, 1263.7 us)
Sparse Core Ops, SparseCore 0:
  21.8 34.2 all-gather.8
  57.7 26.5 all-gather.10
  85.9 27.4 all-gather.12
  114.8 27.4 all-gather.14
  144.3 27.4 all-gather.16
  173.1 80.3 all-gather.18
  338.3 77.7 reduce-scatter.6
  418.5 27.4 reduce-scatter.16
  462.3 27.7 reduce-scatter.14
  537.6 28.8 reduce-scatter.10
  569.4 31.4 reduce-scatter.12
  603.7 27.1 reduce-scatter.8

commit v4 on v3

--- a/solution.py
+++ b/solution.py
@@ -469,12 +469,12 @@
     if blocks is not None and blocks[0].ndim == 4:
         shape = (2, None, low // 2, low)
 
-        def spec(block, first):
-            pick = (lambda t: jnp.minimum(t, 1)) if first else (lambda t: jnp.maximum(t - 2, 0))
+        def spec(block, pick):
             return pl.BlockSpec(shape, lambda t: (pick(t), block, 0, 0))
 
-        return [spec(0, True), spec(2, False), spec(1, True), spec(3, False)]
-    return [early((low, low)), late((low, low)), early((low, low)), late((low, low))]
+        first, second = lambda t: jnp.minimum(t, 1), lambda t: jnp.maximum(t - 2, 0)
+        return [spec(0, first), spec(2, second), spec(1, first), spec(3, lambda t: 0), spec(3, lambda t: 1)]
+    return [early((low, low)), late((low, low)), early((low, low)), fixed((low, low)), fixed((low, low))]
 
 
 def matrix(ref):
@@ -483,15 +483,19 @@
 
 
 def with_tile(step, refs, body):
-    g, gx, gy, gd = refs
+    g, gx, gy, ga, gb = refs
 
     @pl.when(step < 2)
     def _():
         body(g, gy)
 
-    @pl.when(step >= 2)
+    @pl.when(step == 2)
     def _():
-        body(gx, gd)
+        body(gx, ga)
+
+    @pl.when(step == 3)
+    def _():
+        body(gx, gb)
 
 
 def join_into(joined, own, other):
@@ -505,7 +509,7 @@
     low, both = width // 2, 2 * rows
     hid = 4 * low
 
-    def body(own_ref, other_ref, g, gx, gy, gd, bias_ref, joined, act, slope):
+    def body(own_ref, other_ref, g, gx, gy, ga, gb, bias_ref, joined, act, slope):
         step = pl.program_id(0)
 
         @pl.when(step == 0)
@@ -525,7 +529,7 @@
                     inner = pre * ((0.5 * root) + (1.5 * 0.044715 * root) * square)
                     slope[sl, lanes] = (half + (1.0 - tanh * tanh) * inner).astype(BF)
 
-        with_tile(step, (g, gx, gy, gd), product)
+        with_tile(step, (g, gx, gy, ga, gb), product)
 
     return call(
         body,
@@ -545,9 +549,15 @@
     low, both = width // 2, 2 * rows
     hid = 4 * low
 
-    def body(own_ref, other_ref, ug, ugx, ugy, ugd, dg, dgx, dgy, dgd, slope_ref, act_ref, hid_ref,
+    def body(own_ref, other_ref, ug, ugx, ugy, uga, ugb, dg, dgx, dgy, dga, dgb, slope_ref, act_ref, hid_ref,
              sums, out_own, out_other, *rest):
-        two_refs, one_refs, (joined, grad, acc) = rest[: -7], rest[-7:-3], rest[-3:]
+        joined, grad, acc = rest[-3:]
+        if by_z:
+            two_refs, one_refs = rest[:1], rest[1:-3]
+        else:
+            far_a, far_b = rest[6], rest[7]
+            two_refs = (*rest[:3], far_a.at[1], far_b.at[1])
+            one_refs = (*rest[3:6], far_a.at[0], far_b.at[0])
         step = pl.program_id(0)
 
         @pl.when(step == 0)
@@ -575,7 +585,7 @@
                 for j, lanes in ((near, slice(0, low)), (far, slice(low, width))):
                     value = dot(left[...], right[:, lanes], TN).astype(BF)
                     if len(refs) == 1:
-                        refs[0][:, j // 2] = value.reshape(2, low // 2, low)
+                        refs[0][:, min(j, 3) // 2] = value.reshape(2, low // 2, low)
                     else:
                         refs[j][...] = value
 
@@ -589,29 +599,34 @@
 
         @pl.when(step == 2)
         def _():
-            product(ugx, ugd, dgx, dgd, False, False, 1, 3)
+            product(ugx, uga, dgx, dga, False, False, 1, 3)
 
         @pl.when(step == 3)
         def _():
-            product(ugx, ugd, dgx, dgd, False, True, 1, 3)
+            product(ugx, ugb, dgx, dgb, False, True, 1, 4)
 
     tiles = pl.BlockSpec((both, low), lambda t: (0, t))
     whole = shape_of((2 * low, low), BF)
+    block_specs = weight_specs(low)
+    block_shapes = [whole] * 3 + [shape_of((low, low), BF)] * 2
     z_specs = [pl.BlockSpec((2, 2, low // 2, low), lambda t: (t % 2, t // 2, 0, 0))]
     found = call(
         body,
         (4,),
         [fixed((rows, width))] * 2 + weight_specs(low, up_blocks) + weight_specs(low, down_blocks) + [tiles, tiles, fixed((both, width))],
         [pl.BlockSpec((8, low), lambda t: (0, t)), fixed((rows, width)), fixed((rows, width))]
-        + (z_specs if by_z else weight_specs(low)) + weight_specs(low),
+        + (z_specs + block_specs if by_z else block_specs[:3] * 2 + [fixed((2, low, low))] * 2),
         [shape_of((8, hid), F32), shape_of((rows, width), F32), shape_of((rows, width), BF)]
-        + ([shape_of((4, 4, low // 2, low), BF)] if by_z else [whole] * 4) + [whole] * 4,
+        + ([shape_of((4, 4, low // 2, low), BF)] + block_shapes if by_z
+           else [whole] * 6 + [shape_of((2, low, low), BF)] * 2),
         [pltpu.VMEM((both, width), BF), pltpu.VMEM((both, low), BF), pltpu.VMEM((both, width), F32)],
         8 * both * width * hid,
         8 * hid * width + 6 * both * width + 4 * both * hid + 6 * rows * width,
         (own, other, *up_blocks, *down_blocks, slope, act, hidden),
     )
-    return found[:3], found[3:-4], found[-4:]
+    if by_z:
+        return found[:3], found[3], found[4:]
+    return found[:3], found[3:9], found[9:]
 
 
 def fc_down(left, blocks):
@@ -619,7 +634,7 @@
     rows, low = both // 2, hid // 4
     width = 2 * low
 
-    def body(left_ref, g, gx, gy, gd, own, other, acc):
+    def body(left_ref, g, gx, gy, ga, gb, own, other, acc):
         step = pl.program_id(0)
 
         def product(one, two, first, last):
@@ -645,11 +660,11 @@
 
         @pl.when(step == 2)
         def _():
-            product(gx, gd, False, False)
+            product(gx, ga, False, False)
 
         @pl.when(step == 3)
         def _():
-            product(gx, gd, False, True)
+            product(gx, gb, False, True)
 
     return call(
         body,
@@ -675,7 +690,7 @@
     low, both = width // 2, 2 * rows
     tile = low // 2
 
-    def body(own_ref, other_ref, g, gx, gy, gd, vec, ones_ref, joined, q_raw, k_raw, q_low, k_low, v_low, acc):
+    def body(own_ref, other_ref, g, gx, gy, ga, gb, vec, ones_ref, joined, q_raw, k_raw, q_low, k_low, v_low, acc):
         step = pl.program_id(0)
         part = step % 3
 
@@ -690,9 +705,13 @@
         def _():
             product(g[...], gy[...])
 
-        @pl.when(step >= 3)
-        def _():
-            product(gx[...], gd[...])
+        @pl.when(jnp.logical_and(step >= 3, part < 2))
+        def _():
+            product(gx[...], ga[...])
+
+        @pl.when(step == 5)
+        def _():
+            product(gx[...], gb[...])
 
         def unit(value):
             square = dot((value * value).astype(BF), ones_ref[...])
@@ -731,7 +750,8 @@
             pl.BlockSpec((tile, low), lambda t: (jnp.minimum(t, 2), 0)),
             pl.BlockSpec((tile, low), lambda t: (jnp.maximum(t - 3, 0), 0)),
             pl.BlockSpec((tile, low), lambda t: (jnp.minimum(t, 2), 0)),
-            pl.BlockSpec((tile, low), lambda t: (jnp.maximum(t - 3, 0), 0)),
+            pl.BlockSpec((tile, low), lambda t: (jnp.clip(t - 3, 0, 1), 0)),
+            fixed((tile, low)),
             pl.BlockSpec((8, tile), lambda t: (0, half(t))),
             fixed((tile, tile)),
         ],
@@ -787,31 +807,34 @@
     )
 
 
-def attn_back(own, other, blocks, q_low, k_low, v_low, attn, rest, logs, q_raw, k_raw, hidden, scale_row,
-              place_col, end_row, head_width):
+def attn_back(x, own, other, blocks, q_low, k_low, v_low, attn, rest, logs, q_raw, k_raw, hidden, scale_row,
+              place_col, end_row, head_width, before=None):
     rows, width = own.shape
     both, low = q_low.shape
     pair = 2 * head_width
     chunk = both // 4
-    steps = low // pair
+    first_call = before is None
 
     def body(own_ref, other_ref, *refs):
-        w_refs, refs = refs[:16], refs[16:]
-        (q_ref, k_ref, v_ref, attn_ref, rest_ref, log_ref, qr_ref, kr_ref, hid_ref, scale_ref, place_ref, end_ref,
-         sums, out_own, out_other, keep, by_x, by_y, far, joined, weights, ds_ref, three_ref, acc) = refs
+        w_refs, refs = refs[:8], refs[8:]
+        (q_ref, k_ref, v_ref, attn_ref, rest_ref, log_ref, qr_ref, kr_ref, hid_ref, scale_ref, place_ref,
+         end_ref), refs = refs[:12], refs[12:]
+        if first_call:
+            sums, total_ref, near_out, far_a, far_b = refs[:5]
+            joined, weights, ds_ref, three_ref = refs[5:]
+        else:
+            before_ref, sums, out_own, out_other, near_out, far_out = refs[:6]
+            joined, weights, ds_ref, three_ref, total_ref = refs[6:]
         step = pl.program_id(0)
 
         @pl.when(step == 0)
         def _():
             join_into(joined, own_ref, other_ref)
 
-        for side, when in ((0, step < 2), (1, step >= 2)):
-            @pl.when(when)
-            def _():
-                for i in range(4):
-                    rows_i = slice(i * pair, (i + 1) * pair)
-                    weights[rows_i, :low] = w_refs[4 * i + 2 * side][...]
-                    weights[rows_i, low:] = w_refs[4 * i + 2 * side + 1][...]
+        for i in range(4):
+            rows_i = slice(i * pair, (i + 1) * pair)
+            weights[rows_i, :low] = w_refs[2 * i][...]
+            weights[rows_i, low:] = w_refs[2 * i + 1][...]
 
         grad = dot(joined[...], weights[3 * pair :, :], NT).astype(BF)
         ends = end_ref[0:1, :]
@@ -877,68 +900,71 @@
 
             @pl.when(step == 0)
             def _():
-                acc[:, lanes] = part
-
-            @pl.when(jnp.logical_and(step > 0, step < steps - 1))
+                total_ref[:, lanes] = part if first_call else part + before_ref[:, lanes]
+
+            @pl.when(step == 1)
             def _():
-                acc[:, lanes] += part
-
-            @pl.when(step == steps - 1)
-            def _():
-                total = acc[:, lanes] + part
-                out_own[:, lanes] = total[:rows]
-                out_other[:, lanes] = total[rows:].astype(BF)
+                total = total_ref[:, lanes] + part
+                if first_call:
+                    total_ref[:, lanes] = total
+                else:
+                    out_own[:, lanes] = total[:rows]
+                    out_other[:, lanes] = total[rows:].astype(BF)
 
         for i, lanes in enumerate((slice(0, low), slice(low, width))):
             three = dot(three_ref[...], hid_ref[:, lanes], TN).astype(BF)
             proj = dot(attn_ref[...], joined[:, lanes], TN).astype(BF)
             grads = [three[j * pair : (j + 1) * pair] for j in range(3)] + [proj]
-
-            @pl.when(step < 2)
-            def _():
-                for j in range(4):
-                    (keep, by_y)[i][j, 0] = grads[j]
-
-            @pl.when(step >= 2)
-            def _():
-                for j in range(4):
-                    (by_x, far)[i][j, 0] = grads[j]
-
-    g, gx, gy, gd = blocks
+            for j in range(4):
+                if i == 0:
+                    near_out[j, 0] = grads[j]
+                elif first_call:
+                    (far_a if j < 2 else far_b)[j % 2, 0] = grads[j]
+                else:
+                    far_out[j, 0] = grads[j]
+
     w_specs, w_args = [], []
     for i in range(4):
-        w_specs += [f((pair, low), 2 * i) for f in (early, early, late, late)]
-        w_args += [g, gy, gx, gd]
-    block = pl.BlockSpec((both, pair), lambda t: (0, t))
+        far_row = 2 * (i % 2) if x else 2 * i
+        w_specs += [pl.BlockSpec((pair, low), lambda t, row=row: (row + t, 0)) for row in (2 * i, far_row)]
+        w_args += [blocks[1], blocks[3 + i // 2]] if x else [blocks[0], blocks[2]]
+    block = pl.BlockSpec((both, pair), lambda t: (0, 2 * x + t))
     row = pl.BlockSpec((8, pair), lambda t: (0, t))
-    first = pl.BlockSpec((4, 1, pair, low), lambda t: (0, jnp.minimum(t, 1), 0, 0))
-    second = pl.BlockSpec((4, 1, pair, low), lambda t: (0, jnp.maximum(t - 2, 0), 0, 0))
+    four = pl.BlockSpec((4, 1, pair, low), lambda t: (0, t, 0, 0))
+    duo = pl.BlockSpec((2, 1, pair, low), lambda t: (0, t, 0, 0))
+    whole, half = shape_of((4, 2, pair, low), BF), shape_of((2, 2, pair, low), BF)
+    total = shape_of((both, width), F32)
     found = call(
         body,
-        (steps,),
+        (2,),
         [fixed((rows, width))] * 2 + w_specs + [block] * 8
-        + [fixed((both, width)), row, fixed((both, 1)), fixed((8, both))],
-        [row, fixed((rows, width)), fixed((rows, width)), first, second, first, second],
-        [shape_of((8, low), F32), shape_of((rows, width), F32), shape_of((rows, width), BF)]
-        + [shape_of((4, 2, pair, low), BF)] * 4,
+        + [fixed((both, width)), pl.BlockSpec((8, pair), lambda t: (0, 2 * x + t)), fixed((both, 1)), fixed((8, both))]
+        + ([] if first_call else [fixed((both, width))]),
+        [row] + ([fixed((both, width)), four, duo, duo] if first_call else [fixed((rows, width))] * 2 + [four] * 2),
+        [shape_of((8, 2 * pair), F32)]
+        + (
+            [total, whole, half, half] if first_call
+            else [shape_of((rows, width), F32), shape_of((rows, width), BF), whole, whole]
+        ),
         [
             pltpu.VMEM((both, width), BF), pltpu.VMEM((4 * pair, width), BF), pltpu.VMEM((both, both), BF),
-            pltpu.VMEM((both, 3 * pair), BF), pltpu.VMEM((both, width), F32),
-        ],
-        10 * both * both * low + 16 * both * width * low,
-        24 * both * low + 8 * both * width,
+            pltpu.VMEM((both, 3 * pair), BF),
+        ] + ([] if first_call else [pltpu.VMEM((both, width), F32)]),
+        5 * both * both * low + 8 * both * width * low,
+        12 * both * low + 8 * both * width,
         (own, other, *w_args, q_low, k_low, v_low, attn, rest, logs, q_raw, k_raw, hidden, scale_row,
-         place_col, end_row),
-    )
-    return found[:3], found[3:]
+         place_col, end_row) + (() if first_call else (before,)),
+    )
+    start = 2 if first_call else 3
+    return found[:start], [v.reshape(-1, low) for v in found[start:]]
 
 
 def attn_down(attn, blocks):
     both, low = attn.shape
     rows, width, tile = both // 2, 2 * low, low // 2
 
-    def body(attn_ref, g, gx, gy, gd, own, other):
-        for lanes, first, second in ((slice(0, low), g, gx), (slice(low, width), gy, gd)):
+    def body(attn_ref, g, gx, gy, gb, own, other):
+        for lanes, first, second in ((slice(0, low), g, gx), (slice(low, width), gy, gb)):
             value = dot(attn_ref[:, :tile], first[...]) + dot(attn_ref[:, tile:], second[...])
             own[:, lanes] = value[:rows]
             other[:, lanes] = value[rows:].astype(BF)
@@ -947,13 +973,13 @@
     return call(
         body,
         (1,),
-        [fixed((both, low))] + [last] * 4,
+        [fixed((both, low))] + [last] * 3 + [pl.BlockSpec((tile, low), lambda t: (1, 0))],
         [fixed((rows, width))] * 2,
         [shape_of((rows, width), F32), shape_of((rows, width), BF)],
         [],
         2 * both * width * low,
         2 * low * width + 2 * both * low + 6 * rows * width,
-        (attn, *blocks),
+        (attn, *blocks[:3], blocks[4]),
     )
 
 
@@ -1046,36 +1072,42 @@
     return sum(v.astype(F32) for v in values).astype(BF)
 
 
-def flat(blocks):
-    return [v.reshape(-1, v.shape[-1]) for v in blocks]
-
-
-def near_parts(blocks, got_a, got_b):
-    _, near_x, near_y, _ = blocks
-    half, low = got_a.shape
-
-    def body(x_ref, y_ref, a_ref, b_ref, x_out, y_out):
-        x_out[...] = (x_ref[...].astype(F32) + a_ref[...].astype(F32)).astype(BF)
-        y_out[...] = (y_ref[...].astype(F32) + b_ref[...].astype(F32)).astype(BF)
+def near_parts(pairs, got_a, got_b):
+    half, low = got_a.shape[-2:]
+    count = len(pairs)
+    got_a, got_b = [v.reshape(count, half, low) for v in (got_a, got_b)]
+
+    def body(*refs):
+        ins, a_ref, b_ref, outs = refs[: 2 * count], refs[2 * count], refs[2 * count + 1], refs[2 * count + 2 :]
+        for i in range(count):
+            for j, got in ((2 * i, a_ref), (2 * i + 1, b_ref)):
+                outs[j][...] = (ins[j][...].astype(F32) + got[i].astype(F32)).astype(BF)
 
     front = pl.BlockSpec((half, low), lambda t: (0, 0))
     back = pl.BlockSpec((half, low), lambda t: (1, 0))
-    return pl.pallas_call(
+    flat = [v for pair in pairs for v in pair]
+    found = pl.pallas_call(
         body,
         grid=(1,),
-        in_specs=[front, back, front, front],
-        out_specs=[front, back],
-        out_shape=[shape_of(near_x.shape, BF), shape_of(near_y.shape, BF)],
-        input_output_aliases={0: 0, 1: 1},
+        in_specs=[front, back] * count + [fixed(got_a.shape)] * 2,
+        out_specs=[front, back] * count,
+        out_shape=[shape_of(v.shape, BF) for v in flat],
+        input_output_aliases={i: i for i in range(2 * count)},
         compiler_params=pltpu.CompilerParams(vmem_limit_bytes=VMEM_BYTES),
-        cost_estimate=pl.CostEstimate(flops=2 * half * low, bytes_accessed=12 * half * low, transcendentals=0),
-    )(near_x, near_y, got_a, got_b)
-
-
-def settle(keep, got_x, got_y, parts, z_size):
+        cost_estimate=pl.CostEstimate(
+            flops=2 * count * half * low, bytes_accessed=12 * count * half * low, transcendentals=0
+        ),
+    )(*flat, got_a, got_b)
+    return [found[2 * i : 2 * i + 2] for i in range(count)]
+
+
+def summed(keep, got_x, got_y, parts, z_size):
     total = add_low(keep, got_x, got_y)
     total = jnp.swapaxes(total.reshape(parts, z_size, -1, keep.shape[1]), 0, 1)
-    total = total.reshape(z_size, -1, keep.shape[1])
+    return total.reshape(z_size, -1, keep.shape[1])
+
+
+def over_z(total):
     return lax.psum_scatter(total, "z", scatter_dimension=0, tiled=False)
 
 
@@ -1132,13 +1164,14 @@
     def send(rows):
         return rows, across(rows, "x"), across(rows, "y")
 
-    def send_on(state):
+    def send_on(state, then):
         _, by_x, by_y = state
         half = by_x.shape[0] // 2
-        return across(by_x[:half], "y"), across(by_y[half:], "x")
+        first, second, then = together(by_x[:half], by_y[half:], then)
+        return (across(first, "y"), across(second, "x")), then
 
     def whole(state, halves):
-        return (*state, jnp.concatenate(halves))
+        return (*state, *halves)
 
     def together(*values):
         return lax.optimization_barrier(values)
@@ -1146,12 +1179,11 @@
     late = shards[1, cuts[2] :]
     late_x, late_y = across(late, "x"), across(late, "y")
     chunks = [z_gather(l, i) for l in range(layer_count) for i in range(3)][:5]
+
+    cond_low = jax.nn.silu(cond.astype(F32)).astype(BF)
+    silu_rows = lax.all_gather(tie(cond_low, late), ("y", "core"), axis=0, tiled=True)
+    late_x, late_y, silu_rows = together(late_x, late_y, silu_rows)
     late_far = across(late_x, "y")
-    late_blocks = lax.all_gather(jnp.stack((late, late_y, late_x, late_far)), "z", axis=0, tiled=False)
-    sent = send(tie(chunks[0], late_far, late_y))
-
-    cond_low = jax.nn.silu(cond.astype(F32)).astype(BF)
-    silu_rows = lax.all_gather(cond_low, ("y", "core"), axis=0, tiled=True)
     row = y * 2 + core
     silu_own = lax.dynamic_slice_in_dim(silu_rows, row * rows_d, rows_d, axis=1)
     seqs = silu_rows.shape[0]
@@ -1170,9 +1202,14 @@
     to_all = jnp.swapaxes(part.reshape(y_size, x_size, z_size, -1), 1, 2)
     to_all = jnp.broadcast_to(to_all[:, None], (y_size, 2) + to_all.shape[1:])
     from_all = lax.all_to_all(
-        to_all.reshape(n_rows * z_size * x_size, -1), ("y", "core", "z", "x"),
+        tie(to_all.reshape(n_rows * z_size * x_size, -1), chunks[0]), ("y", "core", "z", "x"),
         split_axis=0, concat_axis=0, tiled=True,
     ).reshape(n_rows, z_size, x_size, -1)
+    *sent, from_all = together(*send(tie(chunks[0], late_far, late_y)), from_all)
+    late_blocks = lax.all_gather(
+        tie(jnp.stack((late, late_y, late_x, late_far)), *sent), "z", axis=0, tiled=False
+    )
+    halves, from_all = send_on(sent, from_all)
     ada = jnp.sum(from_all[..., :ada_size], axis=0).reshape(z_size * x_size, layer_count, 6, d_col)
     ada = turned(jnp.transpose(ada, (1, 2, 0, 3)).reshape(layer_count, 6, width), y, 2)
     small = jnp.transpose(from_all[..., ada_size:], (1, 2, 0, 3)).reshape(z_size, x_size, -1)
@@ -1213,10 +1250,9 @@
     def own_tokens(values):
         return jnp.pad(turned(trade(values, core != x), y, 1), ((0, rows_pad - rows_dev), (0, 0)))
 
-    state = own_tokens(hidden_in).astype(F32)
-    grad = own_tokens(grad_out).astype(F32)
+    state = own_tokens(tie(hidden_in, silu_rows)).astype(F32)
     hidden = (normalize(state)[0] * (1.0 + ada[0, 2][None]) + ada[0, 4][None]).astype(BF)
-    weights = [None] * 5 + [(late_blocks,) * 4]
+    weights = [None] * 5 + [(late_blocks,) * 5]
 
     def attn_start(l, hidden):
         vectors = eight_rows(bias_qkv[l, 0], bias_qkv[l, 1], scales[l])
@@ -1243,37 +1279,37 @@
             eight_rows(bias_fc2[l], ada[l, 1], 1.0 + after[2], after[4]), last,
         )
 
-    *sent, hidden, grad = together(*sent, hidden, grad)
-    halves = send_on(sent)
     *halves, chunks[1], hidden = together(*halves, chunks[1], hidden)
     weights[0], sent = whole(sent, halves), send(chunks[1])
     found0 = attn_start(0, hidden)
     attn0, rest0, logs0 = attn_mix(*found0[3:6], end_col, place_row, head_width)
     *sent, attn0 = together(*sent, attn0)
-    halves = send_on(sent)
+    halves, attn0 = send_on(sent, attn0)
     branch0, middle0, hidden2 = attn_end(0, attn0, state)
     *halves, chunks[2], hidden2 = together(*halves, chunks[2], hidden2)
     weights[1], sent = whole(sent, halves), send(chunks[2])
     joined2, act, slope = fc_start(0, hidden2)
     *sent, act = together(*sent, act)
-    halves = send_on(sent)
+    halves, act = send_on(sent, act)
     *halves, chunks[3], act = together(*halves, chunks[3], act)
     weights[2], sent = whole(sent, halves), send(chunks[3])
     feed, state1, hidden = fc_end(0, act, middle0)
     saved = [(*found0, logs0, attn0, rest0, branch0, middle0, joined2, act, slope, feed, state)]
     *sent, hidden = together(*sent, hidden)
-    halves = send_on(sent)
+    halves, hidden = send_on(sent, hidden)
     *halves, chunks[4], hidden = together(*halves, chunks[4], hidden)
     weights[3], sent = whole(sent, halves), send(chunks[4])
     found1 = attn_start(1, hidden)
     attn1, rest1, logs1 = attn_mix(*found1[3:6], end_col, place_row, head_width)
     *sent, attn1 = together(*sent, attn1)
-    halves = send_on(sent)
+    halves, attn1 = send_on(sent, attn1)
     branch1, middle1, hidden2 = attn_end(1, attn1, state1)
-    *halves, hidden2 = together(*halves, hidden2)
+    *halves, hidden2, grad_out = together(*halves, hidden2, grad_out)
     weights[4] = whole(sent, halves)
+    grad = own_tokens(grad_out).astype(F32)
     joined2, act, slope = fc_start(1, hidden2)
     feed, state2, mixed = fc_end(1, act, middle1)
+    mixed, grad = together(mixed, grad)
     saved.append((*found1, logs1, attn1, rest1, branch1, middle1, joined2, act, slope, feed, state1))
 
     top = layer_count - 1
@@ -1290,24 +1326,24 @@
             d_low, sibling(d_low), weights[3 * l + 2], weights[3 * l + 1], slope, act, joined2, l == 1
         )
 
-    def fc_norm(l, found, grad):
-        sums_pre, own, send_own = found
+    def fc_norm(l, sums_pre, own, got_own, grad):
         d_middle, d_low, sums = mix_back(
-            own, sibling(send_own), saved[l][10], grad, saved[l][9], eight_rows(1.0 + ada[l, 3], ada[l, 0])
+            own, got_own, saved[l][10], grad, saved[l][9], eight_rows(1.0 + ada[l, 3], ada[l, 0])
         )
         d_ada[l][3], d_ada[l][5], d_ada[l][0], d_biases[l][0] = fold(sums)
         d_biases[l][3] = fold(sums_pre)[0]
         return d_middle, d_low
 
-    def attn_turn(l, d_low):
+    def attn_turn(x, l, d_low, d_other, before=None):
         joined1, q_raw, k_raw, q_low, k_low, v_low, logs, attn, rest = saved[l][:9]
         return attn_back(
-            d_low, sibling(d_low), weights[3 * l], q_low, k_low, v_low, attn, rest, logs, q_raw, k_raw, joined1,
-            eight_rows(scales[l]), place_col, end_row, head_width,
-        )
-
-    def attn_norm(l, found, got_own, d_middle):
-        sums_qkv, own, _ = found
+            x, d_low, d_other, weights[3 * l], q_low, k_low, v_low, attn, rest, logs, q_raw, k_raw, joined1,
+            eight_rows(scales[l]), place_col, end_row, head_width, before,
+        )
+
+    def attn_norm(l, sums_one, found, got_own, d_middle):
+        sums_qkv, own = found
+        sums_qkv = jnp.concatenate((sums_qkv, sums_one), axis=1)
         before = max(l - 1, 0)
         grad, d_low, sums = mix_back(
             own, got_own, saved[l][-1], d_middle, saved[before][-2],
@@ -1321,60 +1357,65 @@
         d_biases[l][4] = jnp.sum(sums_qkv[2].reshape(heads, head_width), axis=1)
         return grad, d_low
 
-    def halves_of(blocks):
-        return across(blocks[3][:low], "y"), across(blocks[3][low:], "x")
-
     def given_back(values):
         return trade(turned(values[:rows_dev], y, 1).astype(BF), core != x)
 
-    mixed = given_back(mixed)
-    found, two, one = fc_turn(1, d_low)
-    mixed, *found = together(mixed, *found)
-    two_sum = lax.psum_scatter(two[0], "z", scatter_dimension=0, tiled=False)
-    got_a, got_b = halves_of(one)
-    d_middle, d_low = fc_norm(1, found, grad)
-    got_a, got_b, d_low = together(got_a, got_b, d_low)
-    near_x, near_y = near_parts(one, got_a, got_b)
-    one_x, one_y = across(near_x, "x"), across(near_y, "y")
-    found, four_parts = attn_turn(1, d_low)
-    one_x, one_y, *found = together(one_x, one_y, *found)
-    last = flat(four_parts)
-    got_a, got_b = halves_of(last)
-    grad, d_low = attn_norm(1, found, sibling(found[2]), d_middle)
-    got_a, got_b, d_low = together(got_a, got_b, d_low)
-    near_x, near_y = near_parts(last, got_a, got_b)
-    last_x, last_y = across(near_x, "x"), across(near_y, "y")
-    g_one1 = settle(one[0], one_x, one_y, 1, z_size)
-    found, two, one = fc_turn(0, d_low)
-    last_x, last_y, two_sum, *found = together(last_x, last_y, two_sum, *found)
-    got_a, got_b = halves_of(one)
-    d_middle, d_low = fc_norm(0, found, grad)
-    got_a, got_b, d_low = together(got_a, got_b, d_low)
-    near_x, near_y = near_parts(one, got_a, got_b)
-    one_x, one_y = across(near_x, "x"), across(near_y, "y")
-    far_a, far_b = halves_of(two)
-    g_attn1 = settle(last[0], last_x, last_y, 4, z_size)
-    found, four_parts = attn_turn(0, d_low)
-    one_x, one_y, far_a, far_b, *found = together(one_x, one_y, far_a, far_b, *found)
-    last = flat(four_parts)
-    got_a, got_b = halves_of(last)
-    got_own = sibling(found[2])
-    near_x, near_y = near_parts(two, far_a, far_b)
-    got_own, near_x, near_y = together(got_own, near_x, near_y)
-    two_x, two_y = across(near_x, "x"), across(near_y, "y")
-    grad, d_low = attn_norm(0, found, got_own, d_middle)
-    got_a, got_b, one_x, grad = together(got_a, got_b, one_x, grad)
-    g_one0 = settle(one[0], one_x, one_y, 1, z_size)
-    two_x, two_y, got_a = together(two_x, two_y, got_a)
-    near_x, near_y = near_parts(last, got_a, got_b)
-    last_x, last_y = across(near_x, "x"), across(near_y, "y")
-    g_two0 = settle(two[0], two_x, two_y, 1, z_size)
-    last_x, last_y, two_sum = together(last_x, last_y, two_sum)
-    late_far, late_y = across(two_sum[3], "y"), across(two_sum[1], "y")
-    g_attn0 = settle(last[0], last_x, last_y, 4, z_size)
-    late_x = across(add_low(two_sum[2], late_far), "x")
-    g_two1 = add_low(two_sum[0], late_x, late_y)
-    d_weights = [jnp.concatenate(v, axis=0) for v in ((g_attn0, g_one0, g_two0), (g_attn1, g_one1, g_two1))]
+    def halves_out(parts):
+        return across(parts[-2], "y"), across(parts[-1], "x")
+
+    def near_out(pair):
+        return across(pair[0], "x"), across(pair[1], "y")
+
+    (sums_pre, own, send_own), two, one = fc_turn(1, d_low)
+    z_two = over_z(two)
+    got = halves_out(one)
+    d_middle, d_low = fc_norm(1, sums_pre, own, sibling(send_own), grad)
+    *got, d_low = together(*got, d_low)
+    near = near_out(near_parts([one[1:3]], *got)[0])
+
+    d_other = sibling(d_low)
+    (sums_one, total), last_x = attn_turn(1, 1, d_low, d_other)
+    near_a, near_b, total, *last_x = together(*near, total, *last_x)
+    got = halves_out(last_x)
+    sum_one, total = together(summed(one[0], near_a, near_b, 1, z_size), total)
+    (sums_two, own, send_own), last = attn_turn(0, 1, d_low, d_other, total)
+    *got, send_own = together(*got, send_own)
+    pair = near_parts([(last_x[0], last[1])], *got)[0]
+    *pair, send_own = together(*pair, send_own)
+    near = near_out(pair)
+    grad, d_low = attn_norm(1, sums_one, (sums_two, own), sibling(send_own), d_middle)
+    z_two, d_low = together(z_two, d_low)
+    g_one1 = over_z(sum_one)
+
+    (sums_pre, own, send_own), blocks, far = fc_turn(0, d_low)
+    near_a, near_b, send_own = together(*near, send_own)
+    got = across(far[0], "y"), across(far[1], "x")
+    d_middle, d_low = fc_norm(0, sums_pre, own, sibling(send_own), grad)
+    sum_attn, d_low = together(summed(last[0], near_a, near_b, 4, z_size), d_low)
+    g_attn1 = over_z(sum_attn)
+    d_other = sibling(d_low)
+    (sums_one, total), last_x = attn_turn(1, 0, d_low, d_other)
+    *got, total, last_a, last_b, last_c, g_one1 = together(*got, total, *last_x, g_one1)
+    last_x = (last_a, last_b, last_c)
+    one, two = near_parts([blocks[4:6], blocks[1:3]], *got)
+    *one, total = together(*one, total)
+    near_one, near_two = near_out(one), near_out(two)
+    (sums_two, own, send_own), last = attn_turn(0, 0, d_low, d_other, total)
+    near_a, near_b, send_own, g_attn1 = together(*near_one, send_own, g_attn1)
+    got = halves_out(last_x)
+    sum_one, send_own = together(summed(blocks[3], near_a, near_b, 1, z_size), send_own)
+    g_one0 = over_z(sum_one)
+    grad, d_low = attn_norm(0, sums_one, (sums_two, own), sibling(send_own), d_middle)
+    near_a, near_b, grad = together(*near_two, grad)
+    sum_two, *got = together(summed(blocks[0], near_a, near_b, 1, z_size), *got)
+    g_two0 = over_z(sum_two)
+    near = near_out(near_parts([(last_x[0], last[1])], *got)[0])
+    *near, z_two, mixed = together(*near, z_two, mixed)
+    g_attn0 = over_z(summed(last[0], *near, 4, z_size))
+    late_far, late_y = across(z_two[3], "y"), across(z_two[1], "y")
+    mixed, grad_in = given_back(mixed), given_back(grad).astype(F32)
+    late_x = across(add_low(z_two[2], late_far), "x")
+    g_two1 = add_low(z_two[0], late_x, late_y)
 
     def by_col(values):
         values = turned(values, y, values.ndim - 1)
@@ -1421,22 +1462,26 @@
     out_b_fc1 = jnp.stack([v.reshape(-1) for v in outs[3]])
     out_scale = jnp.stack([v.reshape(-1) for v in outs[4]])
 
-    own = jnp.stack(d_weights)
-    kept = jnp.where(core == 0, own[:, :, :rows_d], own[:, :, rows_d:])
-    came = sibling(jnp.where(core == 0, own[:, :, rows_d:], own[:, :, :rows_d]))
-    first = jnp.where(core == 0, kept, came).astype(F32)
-    second = jnp.where(core == 0, came, kept).astype(F32)
+    def both_cores(own):
+        kept = jnp.where(core == 0, own[:, :, :rows_d], own[:, :, rows_d:])
+        came = sibling(jnp.where(core == 0, own[:, :, rows_d:], own[:, :, :rows_d]))
+        return jnp.where(core == 0, kept, came).astype(F32), jnp.where(core == 0, came, kept).astype(F32)
+
+    fc_first, fc_second = both_cores(
+        jnp.stack((jnp.concatenate((g_one0, g_two0)), jnp.concatenate((g_one1, g_two1))))
+    )
+    out_w_fc1 = jnp.swapaxes(jnp.concatenate((fc_first[:, :hid_core], fc_second[:, :hid_core]), axis=1), 1, 2)
+    out_w_fc2 = jnp.concatenate((fc_first[:, hid_core:], fc_second[:, hid_core:]), axis=1)
+    own, out_w_fc1, out_w_fc2, out_w_ada = together(jnp.stack((g_attn0, g_attn1)), out_w_fc1, out_w_fc2, out_w_ada)
+    first, second = both_cores(own)
     wq = jnp.stack((first[:, :three], second[:, :three]), axis=1)
     wq = wq.reshape(layer_count, 2, 3, head_width, rows_d)
     out_w_qkv = jnp.transpose(wq, (0, 4, 2, 1, 3)).reshape(layer_count, rows_d, 3, d_col)
-
-    def pick(i, j):
-        return jnp.concatenate((first[:, i:j], second[:, i:j]), axis=1)
+    out_w_proj = jnp.concatenate((first[:, three:], second[:, three:]), axis=1)
 
     return (
-        mixed, given_back(grad).astype(F32), out_w_ada, out_b_ada, out_w_qkv, out_b_qkv, out_scale,
-        pick(three, four), out_b_proj, jnp.swapaxes(pick(cuts[1], cuts[2]), 1, 2), out_b_fc1,
-        pick(cuts[2], cuts[3]), out_b_fc2,
+        mixed, grad_in, out_w_ada, out_b_ada, out_w_qkv, out_b_qkv, out_scale,
+        out_w_proj, out_b_proj, out_w_fc1, out_b_fc1, out_w_fc2, out_b_fc2,
     )
 
 

time: 660 us -> 617 us (0.935)
  waiting for transfers between devices: 178 us -> 138 us
  local copies, waits for them, and re-layouts: 77.9 us -> 57.6 us
  Pallas kernels: 239 us -> 246 us
  other arithmetic: 42.7 us -> 49.5 us
    ppermute x46 -> x44, waiting for transfers between devices: 137 us -> 88.9 us  [across(): return lax.ppermute(values, axis, [(0, 1), (1, 0)])]
    ppermute x4, waiting for transfers between devices: 23.6 us -> 0.75 us  [trade(): lax.ppermute(values, ('core', 'x'), [(1, 2), (2, 1)])]
    reduce_scatter x6, waiting for transfers between devices: 4.52 us -> 15.4 us  [over_z(): return lax.psum_scatter(total, 'z', scatter_dimension=0, tiled=False)]
    pallas_call x22 -> x24, Pallas kernels: 225 us -> 234 us  [call(): pl.pallas_call(body, grid=grid, in_specs=in_specs, out_specs=out_specs, o...]
    all_to_all x1, waiting for transfers between devices: 6.08 us -> 14.3 us  [on_pair(): lax.all_to_all(tie(to_all.reshape(n_rows * z_size * x_size, -1), chunks[0...]
    slice x19 -> x14, local copies, waits for them, and re-layouts: 17.8 us -> 9.98 us  [the longest x10 9.81 us: send_on(): first, second, then = together(by_x[:half], by_y[half:], then)]
    ppermute x19 -> x20, starting transfers between devices: 25.1 us -> 32.3 us  [sibling(): return lax.ppermute(values, 'core', [(0, 1), (1, 0)])]
    unnamed x216 -> x208, local copies, waits for them, and re-layouts: 27.3 us -> 21.3 us
  transfers between devices with their start and end apart: 83 -> 82, of which waited for: 40 -> 39; matrix products, arithmetic and copies ran while one was open for 14% -> 14% of each run, Pallas kernels for 32% -> 36%
where the time goes in v4:
time: 617 us; the launch traced here: 611 us
  Pallas kernels  246 us (40%)
  waiting for transfers between devices  138 us (22%)
  starting transfers between devices  93.5 us (15%)
  local copies, waits for them, and re-layouts  57.6 us (9%)
  other arithmetic  49.5 us (8%)
  between operations  16.2 us (3%)
  blocking collectives  7.33 us (1%)
    pallas_call x24, Pallas kernels, call(): pl.pallas_call(body, grid=grid, in_specs=in_specs, out_specs=out_specs, o...  234 us
    ppermute x44, waiting for transfers between devices, across(): return lax.ppermute(values, axis, [(0, 1), (1, 0)])  88.9 us
    ppermute x44, starting transfers between devices, across(): return lax.ppermute(values, axis, [(0, 1), (1, 0)])  39.6 us
    ppermute x20, starting transfers between devices, sibling(): return lax.ppermute(values, 'core', [(0, 1), (1, 0)])  32.3 us
    unnamed x208, local copies, waits for them, and re-layouts  21.3 us
    reduce_scatter x6, waiting for transfers between devices, over_z(): return lax.psum_scatter(total, 'z', scatter_dimension=0, tiled=False)  15.4 us
    all_to_all x1, waiting for transfers between devices, on_pair(): lax.all_to_all(tie(to_all.reshape(n_rows * z_size * x_size, -1), chunks[0...  14.3 us
    ppermute x4, starting transfers between devices, trade(): lax.ppermute(values, ('core', 'x'), [(1, 2), (2, 1)])  13.2 us
  transfers between devices with their start and end apart: 82, of which 39 were waited for; matrix products, arithmetic and copies ran while one was open for 14% of the time, Pallas kernels for 36%

profile of v4, /device:TPU:1, one launch (start us, length us, event | category | flops | bytes accessed | tf_op | source)
XLA Modules:
  0.0 610.6 jit_solution(16189987970338290243)
XLA Ops:
  24.5 7.3 %all-gather.1 = bf16[4,4,1024]{2,1,0:T(4,128)(2,1)S(1)} all-gather(bf16[1,4,1024]{2,1,0:T(4,128)(2,1)S(1)} %bitcast.360), channel_id=1, replica_groups=mesh['y'=2,'core'=2,'z'=4,'x'=2] {'y','core'}, dimensions={0}, use_global_device_ids=true | all-gather | bytes 40960 | tf_op jit(solution)/shard_map/all_gather | solution.py:1184
  60.5 14.3 %all-to-all-done = f32[32,1,2176]{2,1,0:T(1,128)} async-done(((f32[32,1,2176]{2,1,0:T(1,128)}), f32[32,1,2176]{2,1,0:T(1,128)}, u32[]{:S(2)}, u32[]{:S(2)}) %all-to-all-start) | async-done | bytes 278560 | tf_op jit(solution)/shard_map/all_to_all | solution.py:1204
  85.0 7.4 %collective-permute-done.6.ga.refs_1_.refs_3_ = bf16[512,512]{1,0:T(8,128)(2,1)S(1)} collective-permute-done((bf16[512,512]{1,0:T(8,128)(2,1)}, bf16[512,512]{1,0:T(8,128)(2,1)S(1)}, u32[]{:S(2)}, u32[]{:S(2)}) %collective-permute-start.6) | collective-permute-done | bytes 524320 | tf_op jit(solution)/shard_map/ppermute | solution.py:415
  99.1 10.9 %shard_map.246 = (bf16[704,1024]{1,0:T(8,128)(2,1)}, bf16[704,512]{1,0:T(8,128)(2,1)}, bf16[704,512]{1,0:T(8,128)(2,1)}, bf16[704,512]{1,0:T(8,128)(2,1)}, bf16[...) custom-call(bf16[352,1024]{1,0:T(8,128)(2,1)} %add_convert_fusion.3.own_ref, ...), custom_call_target="tpu_custom_call" | custom-call | flops 34603008 | bytes 173056 | tf_op jit(solution)/shard_map/pallas_call | solution.py:436
  110.0 9.6 %shard_map.247 = (bf16[704,512]{1,0:T(8,128)(2,1)}, bf16[704,512]{1,0:T(8,128)(2,1)}, f32[704,512]{1,0:T(8,128)}) custom-call(bf16[704,512]{1,0:T(8,128)(2,1)} %get-tuple-element.254.q_ref.refs_8_, bf16[704,512]{1,0:T(8,128)(2,1)} %get-tuple-element.255.k_ref.refs_9_, bf16[704,512]{1,0:T(8,128)(2,1)} %get-tuple-element.256.v_ref.refs_10_, ...), custom_call_target="tpu_custom_call" | custom-call | flops 15859712 | bytes 78848 | tf_op jit(solution)/shard_map/pallas_call | solution.py:436
  132.4 6.9 %collective-permute-done.13.ga.dga = bf16[512,512]{1,0:T(8,128)(2,1)S(1)} collective-permute-done((bf16[512,512]{1,0:T(8,128)(2,1)}, bf16[512,512]{1,0:T(8,128)(2,1)S(1)}, u32[]{:S(2)}, u32[]{:S(2)}) %collective-permute-start.13) | collective-permute-done | bytes 524320 | tf_op jit(solution)/shard_map/ppermute | solution.py:415
  145.2 10.6 %shard_map.250 = (bf16[704,1024]{1,0:T(8,128)(2,1)}, bf16[704,2048]{1,0:T(8,128)(2,1)}, bf16[704,2048]{1,0:T(8,128)(2,1)}) custom-call(bf16[352,1024]{1,0:T(8,128)(2,1)} %get-tuple-element.268.own_ref, bf16[352,1024]{1,0:T(8,128)(2,1)} %collective-permute-done.18.other_ref, bf16[1024,512]{1,0:T(8,128)(2,1)} %bitcast.297, bf16[1024,512]{1,0:T(8,128)(2,1)} %copy-done.12, ...), custom_call_target="tpu_custom_call" | custom-call | flops 46137344 | bytes 223232 | tf_op jit(solution)/shard_map/pallas_call | solution.py:436
  155.7 7.9 %collective-permute-done.16.gx.ugx = bf16[1024,512]{1,0:T(8,128)(2,1)S(1)} collective-permute-done((bf16[1024,512]{1,0:T(8,128)(2,1)}, bf16[1024,512]{1,0:T(8,128)(2,1)S(1)}, u32[]{:S(2)}, u32[]{:S(2)}) %collective-permute-start.16) | collective-permute-done | bytes 1048608 | tf_op jit(solution)/shard_map/ppermute | solution.py:415
  168.5 8.6 %collective-permute-done.19.ga.uga = bf16[512,512]{1,0:T(8,128)(2,1)} collective-permute-done((bf16[512,512]{1,0:T(8,128)(2,1)}, bf16[512,512]{1,0:T(8,128)(2,1)}, u32[]{:S(2)}, u32[]{:S(2)}) %collective-permute-start.19) | collective-permute-done | bytes 524320 | tf_op jit(solution)/shard_map/ppermute | solution.py:415
  179.2 7.6 %shard_map.251 = (f32[352,1024]{1,0:T(8,128)}, bf16[352,1024]{1,0:T(8,128)(2,1)}) custom-call(bf16[704,2048]{1,0:T(8,128)(2,1)} %get-tuple-element.280.left_ref.act_ref, bf16[1024,512]{1,0:T(8,128)(2,1)} %bitcast.293, bf16[1024,512]{1,0:T(8,128)(2,1)} %copy-done.10, bf16[1024,512]{1,0:T(8,128)(2,1)} %copy-done.11, ...), custom_call_target="tpu_custom_call" | custom-call | flops 46137344 | bytes 144384 | tf_op jit(solution)/shard_map/pallas_call | solution.py:436
  202.6 7.7 %collective-permute-done.24.ga.refs_1_.refs_3_ = bf16[512,512]{1,0:T(8,128)(2,1)S(1)} collective-permute-done((bf16[512,512]{1,0:T(8,128)(2,1)}, bf16[512,512]{1,0:T(8,128)(2,1)S(1)}, u32[]{:S(2)}, u32[]{:S(2)}) %collective-permute-start.24) | collective-permute-done | bytes 524320 | tf_op jit(solution)/shard_map/ppermute | solution.py:415
  212.4 8.3 %collective-permute-start.28 = (bf16[352,1024]{1,0:T(8,128)(2,1)}, bf16[352,1024]{1,0:T(8,128)(2,1)}, u32[]{:S(2)}, u32[]{:S(2)}) collective-permute-start(bf16[352,1024]{1,0:T(8,128)(2,1)} %get-tuple-element.295.own_ref), channel_id=1, source_target_pairs={{0,8},{8,0},{1,9},{9,1},{2,10},{10,2},{3,11},{11,3},{4,12},{12,4},... | collective-permute-start | bytes 2162696 | tf_op jit(solution)/shard_map/ppermute | solution.py:411
  223.0 10.9 %shard_map.253 = (bf16[704,1024]{1,0:T(8,128)(2,1)}, bf16[704,512]{1,0:T(8,128)(2,1)}, bf16[704,512]{1,0:T(8,128)(2,1)}, bf16[704,512]{1,0:T(8,128)(2,1)}, bf16[...) custom-call(bf16[352,1024]{1,0:T(8,128)(2,1)} %get-tuple-element.295.own_ref, ...), custom_call_target="tpu_custom_call" | custom-call | flops 34603008 | bytes 173056 | tf_op jit(solution)/shard_map/pallas_call | solution.py:436
  233.9 9.8 %shard_map.254 = (bf16[704,512]{1,0:T(8,128)(2,1)}, bf16[704,512]{1,0:T(8,128)(2,1)}, f32[704,512]{1,0:T(8,128)}) custom-call(bf16[704,512]{1,0:T(8,128)(2,1)} %get-tuple-element.299.q_ref.refs_8_, bf16[704,512]{1,0:T(8,128)(2,1)} %get-tuple-element.300.k_ref.refs_9_, bf16[704,512]{1,0:T(8,128)(2,1)} %get-tuple-element.301.v_ref.refs_10_, ...), custom_call_target="tpu_custom_call" | custom-call | flops 15859712 | bytes 78848 | tf_op jit(solution)/shard_map/pallas_call | solution.py:436
  257.4 6.9 %collective-permute-done.29.ga.dga = bf16[512,512]{1,0:T(8,128)(2,1)S(1)} collective-permute-done((bf16[512,512]{1,0:T(8,128)(2,1)}, bf16[512,512]{1,0:T(8,128)(2,1)S(1)}, u32[]{:S(2)}, u32[]{:S(2)}) %collective-permute-start.29) | collective-permute-done | bytes 524320 | tf_op jit(solution)/shard_map/ppermute | solution.py:415
  270.6 10.4 %shard_map.257 = (bf16[704,1024]{1,0:T(8,128)(2,1)}, bf16[704,2048]{1,0:T(8,128)(2,1)}, bf16[704,2048]{1,0:T(8,128)(2,1)}) custom-call(bf16[352,1024]{1,0:T(8,128)(2,1)} %get-tuple-element.313.own_ref, bf16[352,1024]{1,0:T(8,128)(2,1)} %copy-done.44, bf16[1024,512]{1,0:T(8,128)(2,1)} %bitcast.301, bf16[1024,512]{1,0:T(8,128)(2,1)} %collective-permute-done.26.gx.dgx, ...), custom_call_target="tpu_custom_call" | custom-call | flops 46137344 | bytes 223232 | tf_op jit(solution)/shard_map/pallas_call | solution.py:436
  281.0 7.5 %shard_map.258 = (f32[352,1024]{1,0:T(8,128)}, bf16[352,1024]{1,0:T(8,128)(2,1)}) custom-call(bf16[704,2048]{1,0:T(8,128)(2,1)} %get-tuple-element.317.left_ref.act_ref, bf16[4,4,256,512]{3,2,1,0:T(8,128)(2,1)} %bitcast.265, bf16[4,4,256,512]{3,2,1,0:T(8,128)(2,1)} %bitcast.266, bf16[4,4,256,512]{3,2,1,0:T(8,128)(2,1)} %bitcast.267, ...), custom_call_target="tpu_custom_call" | custom-call | flops 46137344 | bytes 144384 | tf_op jit(solution)/shard_map/pallas_call | solution.py:436
  299.8 21.3 %shard_map.260 = (f32[8,2048]{1,0:T(8,128)}, f32[352,1024]{1,0:T(8,128)}, bf16[352,1024]{1,0:T(8,128)(2,1)}, bf16[4,4,256,512]{3,2,1,0:T(8,128)(2,1)}, bf16[1024...) custom-call(bf16[352,1024]{1,0:T(8,128)(2,1)} %copy-done.20, ...), custom_call_target="tpu_custom_call" | custom-call | flops 184549376 | bytes 453632 | tf_op jit(solution)/shard_map/pallas_call | solution.py:436
  328.0 4.8 shard_map.261
  348.8 18.0 %shard_map.263 = (f32[8,256]{1,0:T(8,128)}, f32[704,1024]{1,0:T(8,128)}, bf16[4,2,128,512]{3,2,1,0:T(8,128)(2,1)}, bf16[2,2,128,512]{3,2,1,0:T(8,128)(2,1)}, bf16[2,2,128,512]{3,2,1,0:T(8,128)(2,1)}) custom-call(bf16[352,1024]{1,0:T(8,128)(2,1)} %get-tuple-element.334.own_ref, bf16[352,1024]{1,0:T(8,128)(2,1)} %copy-done.19, bf16[1024,512]{1,0:T(8,128)(2,1)} %copy-done.5, ...), custom_call_target="tpu_custom_call" | custom-call | flops 65961984 | bytes 157696 | tf_op jit(solution)/shard_map/pallas_call | solution.py:436
  370.6 18.7 %shard_map.264 = (f32[8,256]{1,0:T(8,128)}, f32[352,1024]{1,0:T(8,128)}, bf16[352,1024]{1,0:T(8,128)(2,1)}, bf16[4,2,128,512]{3,2,1,0:T(8,128)(2,1)}, bf16[4,2,128,512]{3,2,1,0:T(8,128)(2,1)}) custom-call(bf16[352,1024]{1,0:T(8,128)(2,1)} %get-tuple-element.334.own_ref, bf16[352,1024]{1,0:T(8,128)(2,1)} %copy-done.19, bf16[1024,512]{1,0:T(8,128)(2,1)} %bitcast.287, ...), custom_call_target="tpu_custom_call" | custom-call | flops 65961984 | bytes 157696 | tf_op jit(solution)/shard_map/pallas_call | solution.py:436
  398.5 4.7 shard_map.266
  406.8 21.9 %shard_map.267 = (f32[8,2048]{1,0:T(8,128)}, f32[352,1024]{1,0:T(8,128)}, bf16[352,1024]{1,0:T(8,128)(2,1)}, bf16[1024,512]{1,0:T(8,128)(2,1)}, bf16[1024,512]{1...) custom-call(bf16[352,1024]{1,0:T(8,128)(2,1)} %get-tuple-element.370, ...), custom_call_target="tpu_custom_call" | custom-call | flops 184549376 | bytes 453632 | tf_op jit(solution)/shard_map/pallas_call | solution.py:436
  432.8 5.0 shard_map.268
  441.5 18.2 %shard_map.269 = (f32[8,256]{1,0:T(8,128)}, f32[704,1024]{1,0:T(8,128)}, bf16[4,2,128,512]{3,2,1,0:T(8,128)(2,1)}, bf16[2,2,128,512]{3,2,1,0:T(8,128)(2,1)}, bf16[2,2,128,512]{3,2,1,0:T(8,128)(2,1)}) custom-call(bf16[352,1024]{1,0:T(8,128)(2,1)} %get-tuple-element.386.own_ref, bf16[352,1024]{1,0:T(8,128)(2,1)} %copy-done.18, bf16[1024,512]{1,0:T(8,128)(2,1)} %copy-done.3, ...), custom_call_target="tpu_custom_call" | custom-call | flops 65961984 | bytes 157696 | tf_op jit(solution)/shard_map/pallas_call | solution.py:436
  466.8 18.6 %shard_map.271 = (f32[8,256]{1,0:T(8,128)}, f32[352,1024]{1,0:T(8,128)}, bf16[352,1024]{1,0:T(8,128)(2,1)}, bf16[4,2,128,512]{3,2,1,0:T(8,128)(2,1)}, bf16[4,2,128,512]{3,2,1,0:T(8,128)(2,1)}) custom-call(bf16[352,1024]{1,0:T(8,128)(2,1)} %get-tuple-element.386.own_ref, bf16[352,1024]{1,0:T(8,128)(2,1)} %copy-done.18, bf16[1024,512]{1,0:T(8,128)(2,1)} %bitcast.279, ...), custom_call_target="tpu_custom_call" | custom-call | flops 65961984 | bytes 157696 | tf_op jit(solution)/shard_map/pallas_call | solution.py:436
  497.3 4.9 shard_map.272
  502.1 8.4 %collective-permute-done.52 = bf16[1024,512]{1,0:T(8,128)(2,1)S(1)} collective-permute-done((bf16[1024,512]{1,0:T(8,128)(2,1)}, bf16[1024,512]{1,0:T(8,128)(2,1)S(1)}, u32[]{:S(2)}, u32[]{:S(2)}) %collective-permute-start.52) | collective-permute-done | bytes 1048608 | tf_op jit(solution)/shard_map/ppermute | solution.py:415
  514.6 5.0 collective-permute-start.62
  541.4 14.5 %collective-permute-done.59 = bf16[1024,512]{1,0:T(8,128)(2,1)S(1)} collective-permute-done((bf16[1024,512]{1,0:T(8,128)(2,1)}, bf16[1024,512]{1,0:T(8,128)(2,1)S(1)}, u32[]{:S(2)}, u32[]{:S(2)}) %collective-permute-start.59) | collective-permute-done | bytes 1048608 | tf_op jit(solution)/shard_map/ppermute | solution.py:415
  570.2 4.7 collective-permute-start.66
  581.9 15.3 %reduce-scatter.13.cloned.1.call-done = bf16[1,256,512]{2,1,0:T(8,128)(2,1)} async-done(((bf16[4,256,512]{2,1,0:T(8,128)(2,1)}), bf16[1,256,512]{2,1,0:T(8,128)(2,1)}) %reduce-scatter.13.cloned.1.call-update) | async-done | bytes 262160 | tf_op jit(solution)/shard_map/reduce_scatter | solution.py:1111
  (648 shorter events, 257.6 us)
Async XLA Ops:
  7.2 36.8 %all-gather.9.cloned.1.call-start = ((), (), s32[]{:S(2)}) async-start(), calls=%async_computation.8 | async-start | bytes 1310720 | tf_op jit(solution)/shard_map/all_gather | solution.py:1159
  14.0 71.0 %all-gather.11.cloned.1.call-start = ((), (), s32[]{:S(2)}) async-start(), calls=%async_computation.9 | async-start | bytes 1310720 | tf_op jit(solution)/shard_map/all_gather | solution.py:1159
  14.7 117.7 %all-gather.13.cloned.1.call-start = ((), (), s32[]{:S(2)}) async-start(), calls=%async_computation.10 | async-start | bytes 1310720 | tf_op jit(solution)/shard_map/all_gather | solution.py:1159
  15.4 151.7 %all-gather.15.cloned.1.call-start = ((), (), s32[]{:S(2)}) async-start(), calls=%async_computation.11 | async-start | bytes 1310720 | tf_op jit(solution)/shard_map/all_gather | solution.py:1159
  18.4 184.2 %all-gather.17.cloned.1.call-start = ((), (), s32[]{:S(2)}) async-start(), calls=%async_computation.12 | async-start | bytes 1310720 | tf_op jit(solution)/shard_map/all_gather | solution.py:1159
  45.3 31.9 %collective-permute-start.4 = (bf16[1024,512]{1,0:T(8,128)(2,1)S(1)}, bf16[1024,512]{1,0:T(8,128)(2,1)S(1)}, u32[]{:S(2)}, u32[]{:S(2)}) collective-permute-start(bf16[1024,512]{1,0:T(8,128)(2,1)S(1)} %bitcast.275), channel_id=1, source_target_pairs={{0,1},{1,0},{2,3},{3,2},{4,5},{5,4},{6,7},{7,6},{8,9},{9,8},{10,11... | collective-permute-start | bytes 3145736 | tf_op jit(solution)/shard_map/ppermute | solution.py:415
  46.6 30.7 %collective-permute-start.5 = (bf16[1024,512]{1,0:T(8,128)(2,1)S(1)}, bf16[1024,512]{1,0:T(8,128)(2,1)S(1)}, u32[]{:S(2)}, u32[]{:S(2)}) collective-permute-start(bf16[1024,512]{1,0:T(8,128)(2,1)S(1)} %bitcast.276), channel_id=1, source_target_pairs={{0,16},{16,0},{1,17},{17,1},{2,18},{18,2},{3,19},{19,3},{4,20},{20... | collective-permute-start | bytes 3145736 | tf_op jit(solution)/shard_map/ppermute | solution.py:415
  55.7 225.3 %all-gather.19.cloned.1.call-start = ((), (), s32[]{:S(2)}) async-start(), calls=%async_computation.19 | async-start | bytes 5242880 | tf_op jit(solution)/shard_map/all_gather | solution.py:1209
  93.3 26.3 %collective-permute-start.9 = (bf16[1024,512]{1,0:T(8,128)(2,1)}, bf16[1024,512]{1,0:T(8,128)(2,1)S(1)}, u32[]{:S(2)}, u32[]{:S(2)}) collective-permute-start(bf16[1024,512]{1,0:T(8,128)(2,1)} %bitcast.295), channel_id=1, source_target_pairs={{0,1},{1,0},{2,3},{3,2},{4,5},{5,4},{6,7},{7,6},{8,9},{9,8},{10,11... | collective-permute-start | bytes 3145736 | tf_op jit(solution)/shard_map/ppermute | solution.py:415
  93.6 26.0 %collective-permute-start.10 = (bf16[1024,512]{1,0:T(8,128)(2,1)}, bf16[1024,512]{1,0:T(8,128)(2,1)S(1)}, u32[]{:S(2)}, u32[]{:S(2)}) collective-permute-start(bf16[1024,512]{1,0:T(8,128)(2,1)} %bitcast.296), channel_id=1, source_target_pairs={{0,16},{16,0},{1,17},{17,1},{2,18},{18,2},{3,19},{19,3},{4,20},{20... | collective-permute-start | bytes 3145736 | tf_op jit(solution)/shard_map/ppermute | solution.py:415
  125.4 277.8 %reduce-scatter.7.cloned.1.call-start = ((), (), s32[]{:S(2)}) async-start(), calls=%async_computation.13 | async-start | bytes 5242880 | tf_op jit(solution)/shard_map/reduce_scatter | solution.py:1111
  210.9 32.8 %collective-permute-start.26 = (bf16[1024,512]{1,0:T(8,128)(2,1)}, bf16[1024,512]{1,0:T(8,128)(2,1)}, u32[]{:S(2)}, u32[]{:S(2)}) collective-permute-start(bf16[1024,512]{1,0:T(8,128)(2,1)} %bitcast.299), channel_id=1, source_target_pairs={{0,1},{1,0},{2,3},{3,2},{4,5},{5,4},{6,7},{7,6},{8,9},{9,8},{10,11... | collective-permute-start | bytes 3145736 | tf_op jit(solution)/shard_map/ppermute | solution.py:415
  211.5 32.2 %collective-permute-start.27 = (bf16[1024,512]{1,0:T(8,128)(2,1)}, bf16[1024,512]{1,0:T(8,128)(2,1)}, u32[]{:S(2)}, u32[]{:S(2)}) collective-permute-start(bf16[1024,512]{1,0:T(8,128)(2,1)} %bitcast.300), channel_id=1, source_target_pairs={{0,16},{16,0},{1,17},{17,1},{2,18},{18,2},{3,19},{19,3},{4,20},{20... | collective-permute-start | bytes 3145736 | tf_op jit(solution)/shard_map/ppermute | solution.py:415
  321.2 138.5 %reduce-scatter.9.cloned.1.call-start = ((), (), s32[]{:S(2)}) async-start(), calls=%async_computation.14 | async-start | bytes 1310720 | tf_op jit(solution)/shard_map/reduce_scatter | solution.py:1111
  341.2 25.6 %collective-permute-start.40 = (bf16[1024,512]{1,0:T(8,128)(2,1)}, bf16[1024,512]{1,0:T(8,128)(2,1)S(1)}, u32[]{:S(2)}, u32[]{:S(2)}) collective-permute-start(bf16[1024,512]{1,0:T(8,128)(2,1)} %get-tuple-element.345), channel_id=1, source_target_pairs={{0,1},{1,0},{2,3},{3,2},{4,5},{5,4},{6,7},{7,6},{8,9},{9,8},{10,11... | collective-permute-start | bytes 3145736 | tf_op jit(solution)/shard_map/ppermute | solution.py:415
  342.7 24.1 %collective-permute-start.41 = (bf16[1024,512]{1,0:T(8,128)(2,1)}, bf16[1024,512]{1,0:T(8,128)(2,1)S(1)}, u32[]{:S(2)}, u32[]{:S(2)}) collective-permute-start(bf16[1024,512]{1,0:T(8,128)(2,1)} %get-tuple-element.346), channel_id=1, source_target_pairs={{0,16},{16,0},{1,17},{17,1},{2,18},{18,2},{3,19},{19,3},{4,20},{20... | collective-permute-start | bytes 3145736 | tf_op jit(solution)/shard_map/ppermute | solution.py:415
  394.9 94.1 %reduce-scatter.11.cloned.1.call-start = ((), (), s32[]{:S(2)}) async-start(), calls=%async_computation.15 | async-start | bytes 1310720 | tf_op jit(solution)/shard_map/reduce_scatter | solution.py:1111
  395.0 33.7 %collective-permute-start.48 = (bf16[1024,512]{1,0:T(8,128)(2,1)}, bf16[1024,512]{1,0:T(8,128)(2,1)S(1)}, u32[]{:S(2)}, u32[]{:S(2)}) collective-permute-start(bf16[1024,512]{1,0:T(8,128)(2,1)} %get-tuple-element.376), channel_id=1, source_target_pairs={{0,1},{1,0},{2,3},{3,2},{4,5},{5,4},{6,7},{7,6},{8,9},{9,8},{10,11... | collective-permute-start | bytes 3145736 | tf_op jit(solution)/shard_map/ppermute | solution.py:415
  396.3 32.5 %collective-permute-start.49 = (bf16[1024,512]{1,0:T(8,128)(2,1)}, bf16[1024,512]{1,0:T(8,128)(2,1)S(1)}, u32[]{:S(2)}, u32[]{:S(2)}) collective-permute-start(bf16[1024,512]{1,0:T(8,128)(2,1)} %get-tuple-element.377), channel_id=1, source_target_pairs={{0,16},{16,0},{1,17},{17,1},{2,18},{18,2},{3,19},{19,3},{4,20},{20... | collective-permute-start | bytes 3145736 | tf_op jit(solution)/shard_map/ppermute | solution.py:415
  429.2 30.5 %collective-permute-start.46 = (bf16[2,512,512]{2,1,0:T(8,128)(2,1)}, bf16[2,512,512]{2,1,0:T(8,128)(2,1)}, u32[]{:S(2)}, u32[]{:S(2)}) collective-permute-start(bf16[2,512,512]{2,1,0:T(8,128)(2,1)} %get-tuple-element.373), channel_id=1, source_target_pairs={{0,16},{16,0},{1,17},{17,1},{2,18},{18,2},{3,19},{19,3},{4,20},{20... | collective-permute-start | bytes 3145736 | tf_op jit(solution)/shard_map/ppermute | solution.py:415
  429.9 29.8 %collective-permute-start.47 = (bf16[2,512,512]{2,1,0:T(8,128)(2,1)}, bf16[2,512,512]{2,1,0:T(8,128)(2,1)}, u32[]{:S(2)}, u32[]{:S(2)}) collective-permute-start(bf16[2,512,512]{2,1,0:T(8,128)(2,1)} %get-tuple-element.374), channel_id=1, source_target_pairs={{0,1},{1,0},{2,3},{3,2},{4,5},{5,4},{6,7},{7,6},{8,9},{9,8},{10,11... | collective-permute-start | bytes 3145736 | tf_op jit(solution)/shard_map/ppermute | solution.py:415
  437.8 131.1 %reduce-scatter.15.cloned.1.call-start = ((), (), s32[]{:S(2)}) async-start(), calls=%async_computation.17 | async-start | bytes 1310720 | tf_op jit(solution)/shard_map/reduce_scatter | solution.py:1111
  463.4 24.7 %collective-permute-start.54 = (bf16[1024,512]{1,0:T(8,128)(2,1)}, bf16[1024,512]{1,0:T(8,128)(2,1)}, u32[]{:S(2)}, u32[]{:S(2)}) collective-permute-start(bf16[1024,512]{1,0:T(8,128)(2,1)} %get-tuple-element.414), channel_id=1, source_target_pairs={{0,1},{1,0},{2,3},{3,2},{4,5},{5,4},{6,7},{7,6},{8,9},{9,8},{10,11... | collective-permute-start | bytes 3145736 | tf_op jit(solution)/shard_map/ppermute | solution.py:415
  464.4 24.7 %collective-permute-start.55 = (bf16[1024,512]{1,0:T(8,128)(2,1)}, bf16[1024,512]{1,0:T(8,128)(2,1)}, u32[]{:S(2)}, u32[]{:S(2)}) collective-permute-start(bf16[1024,512]{1,0:T(8,128)(2,1)} %get-tuple-element.415), channel_id=1, source_target_pairs={{0,16},{16,0},{1,17},{17,1},{2,18},{18,2},{3,19},{19,3},{4,20},{20... | collective-permute-start | bytes 3145736 | tf_op jit(solution)/shard_map/ppermute | solution.py:415
  465.1 45.5 %collective-permute-start.52 = (bf16[1024,512]{1,0:T(8,128)(2,1)}, bf16[1024,512]{1,0:T(8,128)(2,1)S(1)}, u32[]{:S(2)}, u32[]{:S(2)}) collective-permute-start(bf16[1024,512]{1,0:T(8,128)(2,1)} %get-tuple-element.410), channel_id=1, source_target_pairs={{0,1},{1,0},{2,3},{3,2},{4,5},{5,4},{6,7},{7,6},{8,9},{9,8},{10,11... | collective-permute-start | bytes 3145736 | tf_op jit(solution)/shard_map/ppermute | solution.py:415
  465.3 45.8 %collective-permute-start.53 = (bf16[1024,512]{1,0:T(8,128)(2,1)}, bf16[1024,512]{1,0:T(8,128)(2,1)S(1)}, u32[]{:S(2)}, u32[]{:S(2)}) collective-permute-start(bf16[1024,512]{1,0:T(8,128)(2,1)} %get-tuple-element.411), channel_id=1, source_target_pairs={{0,16},{16,0},{1,17},{17,1},{2,18},{18,2},{3,19},{19,3},{4,20},{20... | collective-permute-start | bytes 3145736 | tf_op jit(solution)/shard_map/ppermute | solution.py:415
  466.4 60.7 %collective-permute-start.57 = (bf16[512,512]{1,0:T(8,128)(2,1)}, bf16[512,512]{1,0:T(8,128)(2,1)}, u32[]{:S(2)}, u32[]{:S(2)}) collective-permute-start(bf16[512,512]{1,0:T(8,128)(2,1)} %bitcast.82), channel_id=1, source_target_pairs={{0,16},{16,0},{1,17},{17,1},{2,18},{18,2},{3,19},{19,3},{4,20},{20... | collective-permute-start | bytes 1572872 | tf_op jit(solution)/shard_map/ppermute | solution.py:415
  488.1 39.1 %collective-permute-start.58 = (bf16[512,512]{1,0:T(8,128)(2,1)}, bf16[512,512]{1,0:T(8,128)(2,1)}, u32[]{:S(2)}, u32[]{:S(2)}) collective-permute-start(bf16[512,512]{1,0:T(8,128)(2,1)} %bitcast.395), channel_id=1, source_target_pairs={{0,1},{1,0},{2,3},{3,2},{4,5},{5,4},{6,7},{7,6},{8,9},{9,8},{10,11... | collective-permute-start | bytes 1572872 | tf_op jit(solution)/shard_map/ppermute | solution.py:415
  524.4 44.5 %reduce-scatter.17.cloned.1.call-start = ((), (), s32[]{:S(2)}) async-start(), calls=%async_computation.18 | async-start | bytes 1310720 | tf_op jit(solution)/shard_map/reduce_scatter | solution.py:1111
  529.7 26.2 %collective-permute-start.59 = (bf16[1024,512]{1,0:T(8,128)(2,1)}, bf16[1024,512]{1,0:T(8,128)(2,1)S(1)}, u32[]{:S(2)}, u32[]{:S(2)}) collective-permute-start(bf16[1024,512]{1,0:T(8,128)(2,1)} %get-tuple-element.430), channel_id=1, source_target_pairs={{0,1},{1,0},{2,3},{3,2},{4,5},{5,4},{6,7},{7,6},{8,9},{9,8},{10,11... | collective-permute-start | bytes 3145736 | tf_op jit(solution)/shard_map/ppermute | solution.py:415
  531.1 25.2 %collective-permute-start.60 = (bf16[1024,512]{1,0:T(8,128)(2,1)}, bf16[1024,512]{1,0:T(8,128)(2,1)}, u32[]{:S(2)}, u32[]{:S(2)}) collective-permute-start(bf16[1024,512]{1,0:T(8,128)(2,1)} %get-tuple-element.431), channel_id=1, source_target_pairs={{0,16},{16,0},{1,17},{17,1},{2,18},{18,2},{3,19},{19,3},{4,20},{20... | collective-permute-start | bytes 3145736 | tf_op jit(solution)/shard_map/ppermute | solution.py:415
  532.3 64.9 %reduce-scatter.13.cloned.1.call-start = ((), (), s32[]{:S(2)}) async-start(), calls=%async_computation.16 | async-start | bytes 1310720 | tf_op jit(solution)/shard_map/reduce_scatter | solution.py:1111
  (143 other events, 1474.5 us)
Sparse Core Ops, SparseCore 0:
  14.1 29.8 all-gather.8
  45.6 34.0 all-gather.10
  81.3 26.6 all-gather.12
  109.4 27.4 all-gather.14
  138.8 27.4 all-gather.16
  167.7 80.4 all-gather.18
  321.3 75.2 reduce-scatter.6
  399.0 27.4 reduce-scatter.8
  437.9 26.2 reduce-scatter.10
  494.5 24.9 reduce-scatter.14
  532.5 26.3 reduce-scatter.16
  567.6 29.5 reduce-scatter.12

commit v5 on v4

--- a/solution.py
+++ b/solution.py
@@ -544,6 +544,76 @@
     )
 
 
+def fc_forward(own, other, up_blocks, down_blocks, bias):
+    rows, width = own.shape
+    low, both = width // 2, 2 * rows
+    hid = 4 * low
+
+    def body(own_ref, other_ref, ug, ugx, ugy, uga, ugb, dg, dgx, dgy, dga, dgb, bias_ref,
+             joined, act, slope, out_own, out_other, acc):
+        step = pl.program_id(0)
+
+        @pl.when(step == 0)
+        def _():
+            join_into(joined, own_ref, other_ref)
+
+        def product(up_one, up_two, down_one, down_two, first, last):
+            for i, sl in enumerate((slice(rows, both), slice(0, rows))):
+                pre = dot(joined[sl, :low], up_one[...], NT) + dot(joined[sl, low:], up_two[...], NT)
+                pre = pre + bias_ref[...]
+                root = 0.7978845608028654
+                square = pre * pre
+                tanh = jnp.tanh(pre * (root + (root * 0.044715) * square))
+                half = 0.5 + 0.5 * tanh
+                value = (pre * half).astype(BF)
+                act[sl, :] = value
+                inner = pre * ((0.5 * root) + (1.5 * 0.044715 * root) * square)
+                slope[sl, :] = (half + (1.0 - tanh * tanh) * inner).astype(BF)
+                for lanes, down in ((slice(0, low), down_one), (slice(low, width), down_two)):
+                    part = dot(value, matrix(down))
+                    if not first:
+                        part = part + acc[sl, lanes]
+                    if not last:
+                        acc[sl, lanes] = part
+                    elif i == 0:
+                        out_other[:, lanes] = part.astype(BF)
+                    else:
+                        out_own[:, lanes] = part
+
+        @pl.when(step == 0)
+        def _():
+            product(ug, ugy, dg, dgy, True, False)
+
+        @pl.when(step == 1)
+        def _():
+            product(ug, ugy, dg, dgy, False, False)
+
+        @pl.when(step == 2)
+        def _():
+            product(ugx, uga, dgx, dga, False, False)
+
+        @pl.when(step == 3)
+        def _():
+            product(ugx, ugb, dgx, dgb, False, True)
+
+    tiles = pl.BlockSpec((both, low), lambda t: (0, t))
+    return call(
+        body,
+        (4,),
+        [fixed((rows, width))] * 2 + weight_specs(low) + weight_specs(low, down_blocks)
+        + [pl.BlockSpec((1, low), lambda t: (0, t))],
+        [fixed((both, width)), tiles, tiles, fixed((rows, width)), fixed((rows, width))],
+        [
+            shape_of((both, width), BF), shape_of((both, hid), BF), shape_of((both, hid), BF),
+            shape_of((rows, width), F32), shape_of((rows, width), BF),
+        ],
+        [pltpu.VMEM((both, width), F32)],
+        4 * both * width * hid,
+        4 * hid * width + 6 * both * width + 4 * both * hid + 6 * rows * width,
+        (own, other, *up_blocks, *down_blocks, bias),
+    )
+
+
 def fc_back(own, other, up_blocks, down_blocks, slope, act, hidden, by_z):
     rows, width = own.shape
     low, both = width // 2, 2 * rows
@@ -690,86 +760,80 @@
     low, both = width // 2, 2 * rows
     tile = low // 2
 
-    def body(own_ref, other_ref, g, gx, gy, ga, gb, vec, ones_ref, joined, q_raw, k_raw, q_low, k_low, v_low, acc):
+    def body(own_ref, other_ref, g, gx, gy, ga, gb, vec, ones_ref, joined, q_raw, k_raw, q_low, k_low, v_low):
         step = pl.program_id(0)
-        part = step % 3
 
         @pl.when(step == 0)
         def _():
             join_into(joined, own_ref, other_ref)
-
-        def product(first, second):
-            acc[...] = dot(joined[:, :low], first, NT) + dot(joined[:, low:], second, NT)
-
-        @pl.when(step < 3)
-        def _():
-            product(g[...], gy[...])
-
-        @pl.when(jnp.logical_and(step >= 3, part < 2))
-        def _():
-            product(gx[...], ga[...])
-
-        @pl.when(step == 5)
-        def _():
-            product(gx[...], gb[...])
 
         def unit(value):
             square = dot((value * value).astype(BF), ones_ref[...])
             return value * lax.rsqrt(square + EPS_UNIT)
 
-        @pl.when(part == 0)
-        def _():
-            def finish(sl):
-                value = acc[sl, :] + vec[0:1, :]
-                q_raw[sl, :] = value.astype(BF)
-                q_low[sl, :] = (unit(value) * vec[2:3, :]).astype(BF)
-
-            row_loop(both, both // 4, finish)
-
-        @pl.when(part == 1)
-        def _():
-            def finish(sl):
-                value = acc[sl, :]
-                k_raw[sl, :] = value.astype(BF)
-                k_low[sl, :] = unit(value).astype(BF)
-
-            row_loop(both, both // 4, finish)
-
-        @pl.when(part == 2)
-        def _():
-            v_low[...] = (acc[...] + vec[1:2, :]).astype(BF)
-
-    half = lambda t: t // 3
-    kept = pl.BlockSpec((both, tile), lambda t: (0, half(t)))
+        def product(near, far):
+            for part in range(3):
+                near_rows = slice(part * tile, (part + 1) * tile)
+                far_ref, far_rows = (far[0], near_rows) if part < 2 else far[1]
+                for sl in (slice(0, rows), slice(rows, both)):
+                    value = dot(joined[sl, :low], near[near_rows, :], NT)
+                    value = value + dot(joined[sl, low:], far_ref[far_rows, :], NT)
+                    if part == 0:
+                        value = value + vec[0:1, :]
+                        q_raw[sl, :] = value.astype(BF)
+                        q_low[sl, :] = (unit(value) * vec[2:3, :]).astype(BF)
+                    elif part == 1:
+                        k_raw[sl, :] = value.astype(BF)
+                        k_low[sl, :] = unit(value).astype(BF)
+                    else:
+                        v_low[sl, :] = (value + vec[1:2, :]).astype(BF)
+
+        last = slice(2 * tile, 3 * tile)
+
+        @pl.when(step == 0)
+        def _():
+            product(g, (gy, (gy, last)))
+
+        @pl.when(step == 1)
+        def _():
+            product(gx, (ga, (gb, slice(0, tile))))
+
+    kept = pl.BlockSpec((both, tile), lambda t: (0, t))
     heads = shape_of((both, low), BF)
     return call(
         body,
-        (6,),
-        [fixed((rows, width))] * 2
-        + [
-            pl.BlockSpec((tile, low), lambda t: (jnp.minimum(t, 2), 0)),
-            pl.BlockSpec((tile, low), lambda t: (jnp.maximum(t - 3, 0), 0)),
-            pl.BlockSpec((tile, low), lambda t: (jnp.minimum(t, 2), 0)),
-            pl.BlockSpec((tile, low), lambda t: (jnp.clip(t - 3, 0, 1), 0)),
-            fixed((tile, low)),
-            pl.BlockSpec((8, tile), lambda t: (0, half(t))),
-            fixed((tile, tile)),
-        ],
+        (2,),
+        [fixed((rows, width))] * 2 + [fixed((3 * tile, low))] * 3 + [fixed((low, low)), fixed((tile, low))]
+        + [pl.BlockSpec((8, tile), lambda t: (0, t)), fixed((tile, tile))],
         [fixed((both, width))] + [kept] * 5,
         [shape_of((both, width), BF)] + [heads] * 5,
-        [pltpu.VMEM((both, tile), F32)],
+        [],
         2 * both * width * 3 * low,
         2 * 3 * low * width + 6 * both * width + 10 * both * low,
         (own, other, *blocks, vectors, ones),
     )
 
 
-def attn_mix(q_low, k_low, v_low, end_col, place_row, head_width):
+def attn_mix(q_low, k_low, v_low, end_col, place_row, blocks, head_width):
     both, low = q_low.shape
+    rows, width = both // 2, 2 * low
     pair = 2 * head_width
     chunk = both // 4
 
-    def body(q_ref, k_ref, v_ref, end_ref, place_ref, out_ref, rest_ref, log_ref):
+    def body(q_ref, k_ref, v_ref, end_ref, place_ref, g, gx, gy, gb, out_ref, rest_ref, log_ref, own, other,
+             weights, acc):
+        step = pl.program_id(0)
+
+        @pl.when(step < 2)
+        def _():
+            weights[:, :low] = g[...]
+            weights[:, low:] = gy[...]
+
+        @pl.when(step >= 2)
+        def _():
+            weights[:, :low] = gx[...]
+            weights[:, low:] = gb[...]
+
         place = place_ref[0:1, :]
         lane = lax.broadcasted_iota(jnp.int32, (both, pair), 1)
         value = v_ref[...]
@@ -783,8 +847,8 @@
             queries = q_ref[sl, :]
             found = []
             for h in range(2):
-                own = jnp.where(first if h == 0 else ~first, queries, jnp.zeros_like(queries))
-                scores = dot(own, k_ref[...], NT)
+                mine = jnp.where(first if h == 0 else ~first, queries, jnp.zeros_like(queries))
+                scores = dot(mine, k_ref[...], NT)
                 expo = jnp.where(place < end_ref[sl, :], jnp.exp(scores), 0.0).astype(BF)
                 found.append(dot(expo, wide[h]))
             out = jnp.where(first, found[0][:, :pair] / found[0][:, pair:], found[1][:, :pair] / found[1][:, pair:])
@@ -792,18 +856,35 @@
             out_ref[sl, :] = low_out
             rest_ref[sl, :] = (out - low_out.astype(F32)).astype(BF)
             log_ref[sl, :] = jnp.log(jnp.where(first, found[1][:, pair:], found[0][:, pair:]))
+        part = dot(out_ref[...], weights[...])
+
+        @pl.when(step == 0)
+        def _():
+            acc[...] = part
+
+        @pl.when(jnp.logical_and(step > 0, step < 3))
+        def _():
+            acc[...] += part
+
+        @pl.when(step == 3)
+        def _():
+            total = acc[...] + part
+            own[...] = total[:rows]
+            other[...] = total[rows:].astype(BF)
 
     block = pl.BlockSpec((both, pair), lambda t: (0, t))
+    w_specs = [early((pair, low), 6), late((pair, low), 6), early((pair, low), 6), late((pair, low), 2)]
     return call(
         body,
-        (low // pair,),
-        [block] * 3 + [fixed((both, 1)), fixed((8, both))],
-        [block] * 3,
-        [shape_of((both, low), BF)] * 2 + [shape_of((both, low), F32)],
-        [],
-        4 * both * both * low,
-        14 * both * low,
-        (q_low, k_low, v_low, end_col, place_row),
+        (4,),
+        [block] * 3 + [fixed((both, 1)), fixed((8, both))] + w_specs,
+        [block] * 3 + [fixed((rows, width))] * 2,
+        [shape_of((both, low), BF)] * 2 + [shape_of((both, low), F32)]
+        + [shape_of((rows, width), F32), shape_of((rows, width), BF)],
+        [pltpu.VMEM((pair, width), BF), pltpu.VMEM((both, width), F32)],
+        4 * both * both * low + 2 * both * width * low,
+        14 * both * low + 8 * both * low,
+        (q_low, k_low, v_low, end_col, place_row, *blocks[:3], blocks[4]),
     )
 
 
@@ -959,30 +1040,6 @@
     return found[:start], [v.reshape(-1, low) for v in found[start:]]
 
 
-def attn_down(attn, blocks):
-    both, low = attn.shape
-    rows, width, tile = both // 2, 2 * low, low // 2
-
-    def body(attn_ref, g, gx, gy, gb, own, other):
-        for lanes, first, second in ((slice(0, low), g, gx), (slice(low, width), gy, gb)):
-            value = dot(attn_ref[:, :tile], first[...]) + dot(attn_ref[:, tile:], second[...])
-            own[:, lanes] = value[:rows]
-            other[:, lanes] = value[rows:].astype(BF)
-
-    last = pl.BlockSpec((tile, low), lambda t: (3, 0))
-    return call(
-        body,
-        (1,),
-        [fixed((both, low))] + [last] * 3 + [pl.BlockSpec((tile, low), lambda t: (1, 0))],
-        [fixed((rows, width))] * 2,
-        [shape_of((rows, width), F32), shape_of((rows, width), BF)],
-        [],
-        2 * both * width * low,
-        2 * low * width + 2 * both * low + 6 * rows * width,
-        (attn, *blocks[:3], blocks[4]),
-    )
-
-
 def mix(own, got, state, vectors, last):
     rows, width = own.shape
     part = rows // 2
@@ -1164,11 +1221,10 @@
     def send(rows):
         return rows, across(rows, "x"), across(rows, "y")
 
-    def send_on(state, then):
+    def send_on(state):
         _, by_x, by_y = state
         half = by_x.shape[0] // 2
-        first, second, then = together(by_x[:half], by_y[half:], then)
-        return (across(first, "y"), across(second, "x")), then
+        return across(by_x[:half], "y"), across(by_y[half:], "x")
 
     def whole(state, halves):
         return (*state, *halves)
@@ -1205,11 +1261,12 @@
         tie(to_all.reshape(n_rows * z_size * x_size, -1), chunks[0]), ("y", "core", "z", "x"),
         split_axis=0, concat_axis=0, tiled=True,
     ).reshape(n_rows, z_size, x_size, -1)
-    *sent, from_all = together(*send(tie(chunks[0], late_far, late_y)), from_all)
+    sent = together(*send(tie(chunks[0], late_far, late_y)))
     late_blocks = lax.all_gather(
         tie(jnp.stack((late, late_y, late_x, late_far)), *sent), "z", axis=0, tiled=False
     )
-    halves, from_all = send_on(sent, from_all)
+    halves = send_on(sent)
+    from_all = tie(from_all, *sent)
     ada = jnp.sum(from_all[..., :ada_size], axis=0).reshape(z_size * x_size, layer_count, 6, d_col)
     ada = turned(jnp.transpose(ada, (1, 2, 0, 3)).reshape(layer_count, 6, width), y, 2)
     small = jnp.transpose(from_all[..., ada_size:], (1, 2, 0, 3)).reshape(z_size, x_size, -1)
@@ -1259,8 +1316,7 @@
         found = qkv_up(hidden, sibling(hidden), weights[3 * l], vectors, ones)
         return found
 
-    def attn_end(l, attn, state):
-        own, send_own = attn_down(attn, weights[3 * l])
+    def attn_end(l, own, send_own, state):
         branch, middle, hidden = mix(
             own, sibling(send_own), state,
             eight_rows(bias_proj[l], ada[l, 0], 1.0 + ada[l, 3], ada[l, 5]), False,
@@ -1282,33 +1338,41 @@
     *halves, chunks[1], hidden = together(*halves, chunks[1], hidden)
     weights[0], sent = whole(sent, halves), send(chunks[1])
     found0 = attn_start(0, hidden)
-    attn0, rest0, logs0 = attn_mix(*found0[3:6], end_col, place_row, head_width)
-    *sent, attn0 = together(*sent, attn0)
-    halves, attn0 = send_on(sent, attn0)
-    branch0, middle0, hidden2 = attn_end(0, attn0, state)
+    attn0, rest0, logs0, own, send_own = attn_mix(
+        *found0[3:6], end_col, place_row, weights[0], head_width
+    )
+    *sent, send_own = together(*sent, send_own)
+    halves = send_on(sent)
+    branch0, middle0, hidden2 = attn_end(0, own, send_own, state)
     *halves, chunks[2], hidden2 = together(*halves, chunks[2], hidden2)
     weights[1], sent = whole(sent, halves), send(chunks[2])
     joined2, act, slope = fc_start(0, hidden2)
     *sent, act = together(*sent, act)
-    halves, act = send_on(sent, act)
+    halves = send_on(sent)
     *halves, chunks[3], act = together(*halves, chunks[3], act)
     weights[2], sent = whole(sent, halves), send(chunks[3])
     feed, state1, hidden = fc_end(0, act, middle0)
     saved = [(*found0, logs0, attn0, rest0, branch0, middle0, joined2, act, slope, feed, state)]
     *sent, hidden = together(*sent, hidden)
-    halves, hidden = send_on(sent, hidden)
+    halves = send_on(sent)
     *halves, chunks[4], hidden = together(*halves, chunks[4], hidden)
     weights[3], sent = whole(sent, halves), send(chunks[4])
     found1 = attn_start(1, hidden)
-    attn1, rest1, logs1 = attn_mix(*found1[3:6], end_col, place_row, head_width)
-    *sent, attn1 = together(*sent, attn1)
-    halves, attn1 = send_on(sent, attn1)
-    branch1, middle1, hidden2 = attn_end(1, attn1, state1)
+    attn1, rest1, logs1, own, send_own = attn_mix(
+        *found1[3:6], end_col, place_row, weights[3], head_width
+    )
+    *sent, send_own = together(*sent, send_own)
+    halves = send_on(sent)
+    branch1, middle1, hidden2 = attn_end(1, own, send_own, state1)
     *halves, hidden2, grad_out = together(*halves, hidden2, grad_out)
     weights[4] = whole(sent, halves)
     grad = own_tokens(grad_out).astype(F32)
-    joined2, act, slope = fc_start(1, hidden2)
-    feed, state2, mixed = fc_end(1, act, middle1)
+    joined2, act, slope, own, send_own = fc_forward(
+        hidden2, sibling(hidden2), weights[4], weights[5], bias_fc1[1]
+    )
+    feed, state2, mixed = mix(
+        own, sibling(send_own), middle1, eight_rows(bias_fc2[1], ada[1, 1], ada[1, 2], ada[1, 4]), True
+    )
     mixed, grad = together(mixed, grad)
     saved.append((*found1, logs1, attn1, rest1, branch1, middle1, joined2, act, slope, feed, state1))
 
@@ -1320,10 +1384,11 @@
     d_low = (grad * ada[top, 1][None]).astype(BF)
     d_ada[top][1] = jnp.sum(grad * saved[1][-2].astype(F32), axis=0)
     d_biases[top][1] = jnp.sum(d_low.astype(F32), axis=0)
-    def fc_turn(l, d_low):
+    def fc_turn(l, d_low, d_other=None):
         act, slope, joined2 = saved[l][-4], saved[l][-3], saved[l][-5]
+        d_other = sibling(d_low) if d_other is None else d_other
         return fc_back(
-            d_low, sibling(d_low), weights[3 * l + 2], weights[3 * l + 1], slope, act, joined2, l == 1
+            d_low, d_other, weights[3 * l + 2], weights[3 * l + 1], slope, act, joined2, l == 1
         )
 
     def fc_norm(l, sums_pre, own, got_own, grad):
@@ -1368,54 +1433,53 @@
 
     (sums_pre, own, send_own), two, one = fc_turn(1, d_low)
     z_two = over_z(two)
-    got = halves_out(one)
+    got_one = halves_out(one)
     d_middle, d_low = fc_norm(1, sums_pre, own, sibling(send_own), grad)
-    *got, d_low = together(*got, d_low)
-    near = near_out(near_parts([one[1:3]], *got)[0])
-
     d_other = sibling(d_low)
+
     (sums_one, total), last_x = attn_turn(1, 1, d_low, d_other)
-    near_a, near_b, total, *last_x = together(*near, total, *last_x)
-    got = halves_out(last_x)
-    sum_one, total = together(summed(one[0], near_a, near_b, 1, z_size), total)
+    got_a, got_b, total, *last_x = together(*got_one, total, *last_x)
+    got_last = halves_out(last_x)
+    near_x, near_y, total = together(*near_parts([one[1:3]], got_a, got_b)[0], total)
+    near_one = across(near_x, "x"), across(near_y, "y")
     (sums_two, own, send_own), last = attn_turn(0, 1, d_low, d_other, total)
-    *got, send_own = together(*got, send_own)
-    pair = near_parts([(last_x[0], last[1])], *got)[0]
-    *pair, send_own = together(*pair, send_own)
-    near = near_out(pair)
+    *got_last, send_own = together(*got_last, send_own)
     grad, d_low = attn_norm(1, sums_one, (sums_two, own), sibling(send_own), d_middle)
-    z_two, d_low = together(z_two, d_low)
+    near_a, near_b, d_low = together(*near_one, d_low)
+    sum_one = summed(one[0], near_a, near_b, 1, z_size)
+    got_a, got_b, sum_one, d_other = together(*got_last, sum_one, sibling(d_low))
     g_one1 = over_z(sum_one)
-
-    (sums_pre, own, send_own), blocks, far = fc_turn(0, d_low)
-    near_a, near_b, send_own = together(*near, send_own)
+    near_last = near_out(near_parts([(last_x[0], last[1])], got_a, got_b)[0])
+    keep_last = last[0]
+
+    (sums_pre, own, send_own), blocks, far = fc_turn(0, d_low, d_other)
+    z_two = turned(turned(z_two.reshape(x_size, y_size, hid_core, low), x, 0), y, 1)
+    near_a, near_b, z_two, send_own = together(
+        *near_last, z_two.reshape(x_size * y_size, hid_core, low), send_own
+    )
+    g_two1 = lax.psum_scatter(z_two, ("x", "y"), scatter_dimension=0, tiled=False)
     got = across(far[0], "y"), across(far[1], "x")
     d_middle, d_low = fc_norm(0, sums_pre, own, sibling(send_own), grad)
-    sum_attn, d_low = together(summed(last[0], near_a, near_b, 4, z_size), d_low)
-    g_attn1 = over_z(sum_attn)
+    sum_last, d_low = together(summed(keep_last, near_a, near_b, 4, z_size), d_low)
+    g_attn1 = over_z(sum_last)
     d_other = sibling(d_low)
+
     (sums_one, total), last_x = attn_turn(1, 0, d_low, d_other)
-    *got, total, last_a, last_b, last_c, g_one1 = together(*got, total, *last_x, g_one1)
-    last_x = (last_a, last_b, last_c)
+    *got, total, g_one1, g_two1 = together(*got, total, g_one1, g_two1)
     one, two = near_parts([blocks[4:6], blocks[1:3]], *got)
     *one, total = together(*one, total)
     near_one, near_two = near_out(one), near_out(two)
     (sums_two, own, send_own), last = attn_turn(0, 0, d_low, d_other, total)
-    near_a, near_b, send_own, g_attn1 = together(*near_one, send_own, g_attn1)
-    got = halves_out(last_x)
+    near_a, near_b, send_own = together(*near_one, send_own)
+    got_last = halves_out(last_x)
     sum_one, send_own = together(summed(blocks[3], near_a, near_b, 1, z_size), send_own)
     g_one0 = over_z(sum_one)
     grad, d_low = attn_norm(0, sums_one, (sums_two, own), sibling(send_own), d_middle)
-    near_a, near_b, grad = together(*near_two, grad)
-    sum_two, *got = together(summed(blocks[0], near_a, near_b, 1, z_size), *got)
-    g_two0 = over_z(sum_two)
-    near = near_out(near_parts([(last_x[0], last[1])], *got)[0])
-    *near, z_two, mixed = together(*near, z_two, mixed)
-    g_attn0 = over_z(summed(last[0], *near, 4, z_size))
-    late_far, late_y = across(z_two[3], "y"), across(z_two[1], "y")
-    mixed, grad_in = given_back(mixed), given_back(grad).astype(F32)
-    late_x = across(add_low(z_two[2], late_far), "x")
-    g_two1 = add_low(z_two[0], late_x, late_y)
+    near_a, near_b, grad, g_attn1 = together(*near_two, grad, g_attn1)
+    g_two0 = over_z(summed(blocks[0], near_a, near_b, 1, z_size))
+    near_x, near_y = near_parts([(last_x[0], last[1])], *got_last)[0]
+    near_x, near_y, g_one0 = together(near_x, near_y, g_one0)
+    near_last = across(near_x, "x"), across(near_y, "y")
 
     def by_col(values):
         values = turned(values, y, values.ndim - 1)
@@ -1462,6 +1526,11 @@
     out_b_fc1 = jnp.stack([v.reshape(-1) for v in outs[3]])
     out_scale = jnp.stack([v.reshape(-1) for v in outs[4]])
 
+    near_a, near_b, out_w_ada, grad, mixed = together(*near_last, out_w_ada, grad, mixed)
+    sum_last, g_two0, grad, mixed = together(summed(last[0], near_a, near_b, 4, z_size), g_two0, grad, mixed)
+    g_attn0 = over_z(sum_last)
+    mixed, grad_in = given_back(mixed), given_back(grad).astype(F32)
+
     def both_cores(own):
         kept = jnp.where(core == 0, own[:, :, :rows_d], own[:, :, rows_d:])
         came = sibling(jnp.where(core == 0, own[:, :, rows_d:], own[:, :, :rows_d]))

time: 617 us -> 604 us (0.979)
  waiting for transfers between devices: 138 us -> 148 us
  starting transfers between devices: 93.5 us -> 84.2 us
  other arithmetic: 49.5 us -> 43 us
    ppermute x4, waiting for transfers between devices: 0.75 us -> 11.5 us  [trade(): lax.ppermute(values, ('core', 'x'), [(1, 2), (2, 1)])]
    reduce_scatter x6, waiting for transfers between devices: 15.4 us -> 7.06 us  [over_z(): return lax.psum_scatter(total, 'z', scatter_dimension=0, tiled=False)]
    pallas_call x24 -> x21, Pallas kernels: 234 us -> 229 us  [call(): pl.pallas_call(body, grid=grid, in_specs=in_specs, out_specs=out_specs, o...]
    ppermute x44 -> x41, starting transfers between devices: 39.6 us -> 34 us  [across(): return lax.ppermute(values, axis, [(0, 1), (1, 0)])]
    ppermute x44 -> x41, waiting for transfers between devices: 88.9 us -> 90.8 us  [across(): return lax.ppermute(values, axis, [(0, 1), (1, 0)])]
    unnamed x208 -> x210, local copies, waits for them, and re-layouts: 21.3 us -> 20.2 us
  transfers between devices with their start and end apart: 82 -> 80, of which waited for: 39 -> 41; matrix products, arithmetic and copies ran while one was open for 14% -> 13% of each run, Pallas kernels for 36% -> 36%
where the time goes in v5:
time: 604 us; the launch traced here: 597 us
  Pallas kernels  240 us (40%)
  waiting for transfers between devices  148 us (25%)
  starting transfers between devices  84.2 us (14%)
  local copies, waits for them, and re-layouts  56.2 us (9%)
  other arithmetic  43 us (7%)
  between operations  16 us (3%)
  blocking collectives  7.31 us (1%)
    pallas_call x21, Pallas kernels, call(): pl.pallas_call(body, grid=grid, in_specs=in_specs, out_specs=out_specs, o...  229 us
    ppermute x41, waiting for transfers between devices, across(): return lax.ppermute(values, axis, [(0, 1), (1, 0)])  90.8 us
    ppermute x41, starting transfers between devices, across(): return lax.ppermute(values, axis, [(0, 1), (1, 0)])  34 us
    ppermute x20, starting transfers between devices, sibling(): return lax.ppermute(values, 'core', [(0, 1), (1, 0)])  29.2 us
    unnamed x210, local copies, waits for them, and re-layouts  20.2 us
    ppermute x20, waiting for transfers between devices, sibling(): return lax.ppermute(values, 'core', [(0, 1), (1, 0)])  14.6 us
    all_to_all x1, waiting for transfers between devices, on_pair(): lax.all_to_all(tie(to_all.reshape(n_rows * z_size * x_size, -1), chunks[0...  13.9 us
  transfers between devices with their start and end apart: 80, of which 41 were waited for; matrix products, arithmetic and copies ran while one was open for 13% of the time, Pallas kernels for 36%

profile of v5, /device:TPU:1, one launch (start us, length us, event | category | flops | bytes accessed | tf_op | source)
XLA Modules:
  0.0 597.5 jit_solution(4147626590158734515)
XLA Ops:
  24.5 7.3 %all-gather.1 = bf16[4,4,1024]{2,1,0:T(4,128)(2,1)S(1)} all-gather(bf16[1,4,1024]{2,1,0:T(4,128)(2,1)S(1)} %bitcast.362), channel_id=1, replica_groups=mesh['y'=2,'core'=2,'z'=4,'x'=2] {'y','core'}, dimensions={0}, use_global_device_ids=true | all-gather | bytes 40960 | tf_op jit(solution)/shard_map/all_gather | solution.py:1240
  61.3 13.9 %all-to-all-done = f32[32,1,2176]{2,1,0:T(1,128)} async-done(((f32[32,1,2176]{2,1,0:T(1,128)}), f32[32,1,2176]{2,1,0:T(1,128)}, u32[]{:S(2)}, u32[]{:S(2)}) %all-to-all-start) | async-done | bytes 278560 | tf_op jit(solution)/shard_map/all_to_all | solution.py:1260
  85.2 7.0 %collective-permute-done.6.ga.refs_1_.refs_3_ = bf16[512,512]{1,0:T(8,128)(2,1)} collective-permute-done((bf16[512,512]{1,0:T(8,128)(2,1)}, bf16[512,512]{1,0:T(8,128)(2,1)}, u32[]{:S(2)}, u32[]{:S(2)}) %collective-permute-start.6) | collective-permute-done | bytes 524320 | tf_op jit(solution)/shard_map/ppermute | solution.py:415
  99.4 9.0 %shard_map.246 = (bf16[704,1024]{1,0:T(8,128)(2,1)}, bf16[704,512]{1,0:T(8,128)(2,1)}, bf16[704,512]{1,0:T(8,128)(2,1)}, bf16[704,512]{1,0:T(8,128)(2,1)}, bf16[...) custom-call(bf16[352,1024]{1,0:T(8,128)(2,1)} %add_convert_fusion.3.own_ref, ...), custom_call_target="tpu_custom_call" | custom-call | flops 34603008 | bytes 173056 | tf_op jit(solution)/shard_map/pallas_call | solution.py:436
  108.4 13.3 %shard_map.247 = (bf16[704,512]{1,0:T(8,128)(2,1)}, bf16[704,512]{1,0:T(8,128)(2,1)}, f32[704,512]{1,0:T(8,128)}, f32[352,1024]{1,0:T(8,128)}, bf16[352,1024]{1,0:T(8,128)(2,1)}) custom-call(bf16[704,512]{1,0:T(8,128)(2,1)} %get-tuple-element.240.q_ref.refs_8_, bf16[704,512]{1,0:T(8,128)(2,1)} %get-tuple-element.241.k_ref.refs_9_, ...), custom_call_target="tpu_custom_call" | custom-call | flops 27394048 | bytes 123904 | tf_op jit(solution)/shard_map/pallas_call | solution.py:436
  130.1 7.1 %collective-permute-done.13.ga.dga = bf16[512,512]{1,0:T(8,128)(2,1)S(1)} collective-permute-done((bf16[512,512]{1,0:T(8,128)(2,1)}, bf16[512,512]{1,0:T(8,128)(2,1)S(1)}, u32[]{:S(2)}, u32[]{:S(2)}) %collective-permute-start.13) | collective-permute-done | bytes 524320 | tf_op jit(solution)/shard_map/ppermute | solution.py:415
  143.9 10.5 %shard_map.249 = (bf16[704,1024]{1,0:T(8,128)(2,1)}, bf16[704,2048]{1,0:T(8,128)(2,1)}, bf16[704,2048]{1,0:T(8,128)(2,1)}) custom-call(bf16[352,1024]{1,0:T(8,128)(2,1)} %get-tuple-element.250.own_ref, bf16[352,1024]{1,0:T(8,128)(2,1)} %collective-permute-done.18.other_ref, bf16[1024,512]{1,0:T(8,128)(2,1)} %bitcast.304, bf16[1024,512]{1,0:T(8,128)(2,1)} %copy-done.14, ...), custom_call_target="tpu_custom_call" | custom-call | flops 46137344 | bytes 223232 | tf_op jit(solution)/shard_map/pallas_call | solution.py:436
  154.4 7.3 %collective-permute-done.16.gx.ugx = bf16[1024,512]{1,0:T(8,128)(2,1)S(1)} collective-permute-done((bf16[1024,512]{1,0:T(8,128)(2,1)}, bf16[1024,512]{1,0:T(8,128)(2,1)S(1)}, u32[]{:S(2)}, u32[]{:S(2)}) %collective-permute-start.16) | collective-permute-done | bytes 1048608 | tf_op jit(solution)/shard_map/ppermute | solution.py:415
  167.2 7.8 %collective-permute-done.19.ga.uga = bf16[512,512]{1,0:T(8,128)(2,1)} collective-permute-done((bf16[512,512]{1,0:T(8,128)(2,1)}, bf16[512,512]{1,0:T(8,128)(2,1)}, u32[]{:S(2)}, u32[]{:S(2)}) %collective-permute-start.19) | collective-permute-done | bytes 524320 | tf_op jit(solution)/shard_map/ppermute | solution.py:415
  177.2 7.7 %shard_map.250 = (f32[352,1024]{1,0:T(8,128)}, bf16[352,1024]{1,0:T(8,128)(2,1)}) custom-call(bf16[704,2048]{1,0:T(8,128)(2,1)} %get-tuple-element.259.left_ref.act_ref, bf16[1024,512]{1,0:T(8,128)(2,1)} %bitcast.296, bf16[1024,512]{1,0:T(8,128)(2,1)} %copy-done.12, bf16[1024,512]{1,0:T(8,128)(2,1)} %copy-done.13, ...), custom_call_target="tpu_custom_call" | custom-call | flops 46137344 | bytes 144384 | tf_op jit(solution)/shard_map/pallas_call | solution.py:436
  200.9 7.3 %collective-permute-done.24.ga.refs_1_.refs_3_ = bf16[512,512]{1,0:T(8,128)(2,1)S(1)} collective-permute-done((bf16[512,512]{1,0:T(8,128)(2,1)}, bf16[512,512]{1,0:T(8,128)(2,1)S(1)}, u32[]{:S(2)}, u32[]{:S(2)}) %collective-permute-start.24) | collective-permute-done | bytes 524320 | tf_op jit(solution)/shard_map/ppermute | solution.py:415
  210.4 9.5 %collective-permute-start.28 = (bf16[352,1024]{1,0:T(8,128)(2,1)}, bf16[352,1024]{1,0:T(8,128)(2,1)}, u32[]{:S(2)}, u32[]{:S(2)}) collective-permute-start(bf16[352,1024]{1,0:T(8,128)(2,1)} %get-tuple-element.271.own_ref), channel_id=1, source_target_pairs={{0,8},{8,0},{1,9},{9,1},{2,10},{10,2},{3,11},{11,3},{4,12},{12,4},... | collective-permute-start | bytes 2162696 | tf_op jit(solution)/shard_map/ppermute | solution.py:411
  222.0 9.2 %shard_map.252 = (bf16[704,1024]{1,0:T(8,128)(2,1)}, bf16[704,512]{1,0:T(8,128)(2,1)}, bf16[704,512]{1,0:T(8,128)(2,1)}, bf16[704,512]{1,0:T(8,128)(2,1)}, bf16[...) custom-call(bf16[352,1024]{1,0:T(8,128)(2,1)} %get-tuple-element.271.own_ref, ...), custom_call_target="tpu_custom_call" | custom-call | flops 34603008 | bytes 173056 | tf_op jit(solution)/shard_map/pallas_call | solution.py:436
  231.2 13.2 %shard_map.253 = (bf16[704,512]{1,0:T(8,128)(2,1)}, bf16[704,512]{1,0:T(8,128)(2,1)}, f32[704,512]{1,0:T(8,128)}, f32[352,1024]{1,0:T(8,128)}, bf16[352,1024]{1,0:T(8,128)(2,1)}) custom-call(bf16[704,512]{1,0:T(8,128)(2,1)} %get-tuple-element.275.q_ref.refs_8_, bf16[704,512]{1,0:T(8,128)(2,1)} %get-tuple-element.276.k_ref.refs_9_, ...), custom_call_target="tpu_custom_call" | custom-call | flops 27394048 | bytes 123904 | tf_op jit(solution)/shard_map/pallas_call | solution.py:436
  254.4 5.2 collective-permute-done.29.uga.dga
  267.9 15.3 %shard_map.255 = (bf16[704,1024]{1,0:T(8,128)(2,1)}, bf16[704,2048]{1,0:T(8,128)(2,1)}, bf16[704,2048]{1,0:T(8,128)(2,1)}, f32[352,1024]{1,0:T(8,128)}, bf16[352,1024]{1,0:T(8,128)(2,1)}) custom-call(bf16[352,1024]{1,0:T(8,128)(2,1)} %get-tuple-element.285.own_ref, bf16[352,1024]{1,0:T(8,128)(2,1)} %copy-done.39, bf16[1024,512]{1,0:T(8,128)(2,1)} %bitcast.300, ...), custom_call_target="tpu_custom_call" | custom-call | flops 92274688 | bytes 322560 | tf_op jit(solution)/shard_map/pallas_call | solution.py:436
  294.4 21.2 %shard_map.257 = (f32[8,2048]{1,0:T(8,128)}, f32[352,1024]{1,0:T(8,128)}, bf16[352,1024]{1,0:T(8,128)(2,1)}, bf16[4,4,256,512]{3,2,1,0:T(8,128)(2,1)}, bf16[1024...) custom-call(bf16[352,1024]{1,0:T(8,128)(2,1)} %copy-done.19, ...), custom_call_target="tpu_custom_call" | custom-call | flops 184549376 | bytes 453632 | tf_op jit(solution)/shard_map/pallas_call | solution.py:436
  319.9 5.7 shard_map.258
  330.5 18.0 %shard_map.259 = (f32[8,256]{1,0:T(8,128)}, f32[704,1024]{1,0:T(8,128)}, bf16[4,2,128,512]{3,2,1,0:T(8,128)(2,1)}, bf16[2,2,128,512]{3,2,1,0:T(8,128)(2,1)}, bf16[2,2,128,512]{3,2,1,0:T(8,128)(2,1)}) custom-call(bf16[352,1024]{1,0:T(8,128)(2,1)} %get-tuple-element.302.own_ref, bf16[352,1024]{1,0:T(8,128)(2,1)} %copy-done.18, bf16[1024,512]{1,0:T(8,128)(2,1)} %copy-done.5, ...), custom_call_target="tpu_custom_call" | custom-call | flops 65961984 | bytes 157696 | tf_op jit(solution)/shard_map/pallas_call | solution.py:436
  354.3 18.7 %shard_map.261 = (f32[8,256]{1,0:T(8,128)}, f32[352,1024]{1,0:T(8,128)}, bf16[352,1024]{1,0:T(8,128)(2,1)}, bf16[4,2,128,512]{3,2,1,0:T(8,128)(2,1)}, bf16[4,2,128,512]{3,2,1,0:T(8,128)(2,1)}) custom-call(bf16[352,1024]{1,0:T(8,128)(2,1)} %get-tuple-element.302.own_ref, bf16[352,1024]{1,0:T(8,128)(2,1)} %copy-done.18, bf16[1024,512]{1,0:T(8,128)(2,1)} %bitcast.289, ...), custom_call_target="tpu_custom_call" | custom-call | flops 65961984 | bytes 157696 | tf_op jit(solution)/shard_map/pallas_call | solution.py:436
  379.3 4.8 shard_map.262
  392.6 21.7 %shard_map.264 = (f32[8,2048]{1,0:T(8,128)}, f32[352,1024]{1,0:T(8,128)}, bf16[352,1024]{1,0:T(8,128)(2,1)}, bf16[1024,512]{1,0:T(8,128)(2,1)}, bf16[1024,512]{1...) custom-call(bf16[352,1024]{1,0:T(8,128)(2,1)} %get-tuple-element.341, ...), custom_call_target="tpu_custom_call" | custom-call | flops 184549376 | bytes 453632 | tf_op jit(solution)/shard_map/pallas_call | solution.py:436
  423.6 4.7 shard_map.265
  431.9 18.0 %shard_map.266 = (f32[8,256]{1,0:T(8,128)}, f32[704,1024]{1,0:T(8,128)}, bf16[4,2,128,512]{3,2,1,0:T(8,128)(2,1)}, bf16[2,2,128,512]{3,2,1,0:T(8,128)(2,1)}, bf16[2,2,128,512]{3,2,1,0:T(8,128)(2,1)}) custom-call(bf16[352,1024]{1,0:T(8,128)(2,1)} %get-tuple-element.358.own_ref, bf16[352,1024]{1,0:T(8,128)(2,1)} %copy-done.17, bf16[1024,512]{1,0:T(8,128)(2,1)} %copy-done.3, ...), custom_call_target="tpu_custom_call" | custom-call | flops 65961984 | bytes 157696 | tf_op jit(solution)/shard_map/pallas_call | solution.py:436
  451.0 4.4 reduce-scatter.22.cloned.1.call-done
  462.2 18.9 %shard_map.268 = (f32[8,256]{1,0:T(8,128)}, f32[352,1024]{1,0:T(8,128)}, bf16[352,1024]{1,0:T(8,128)(2,1)}, bf16[4,2,128,512]{3,2,1,0:T(8,128)(2,1)}, bf16[4,2,128,512]{3,2,1,0:T(8,128)(2,1)}) custom-call(bf16[352,1024]{1,0:T(8,128)(2,1)} %get-tuple-element.358.own_ref, bf16[352,1024]{1,0:T(8,128)(2,1)} %copy-done.17, bf16[1024,512]{1,0:T(8,128)(2,1)} %bitcast.281, ...), custom_call_target="tpu_custom_call" | custom-call | flops 65961984 | bytes 157696 | tf_op jit(solution)/shard_map/pallas_call | solution.py:436
  494.2 4.8 shard_map.270
  501.9 4.8 all-to-all-start.1
  509.7 10.5 %collective-permute-done.59 = bf16[1024,512]{1,0:T(8,128)(2,1)} collective-permute-done((bf16[1024,512]{1,0:T(8,128)(2,1)S(1)}, bf16[1024,512]{1,0:T(8,128)(2,1)}, u32[]{:S(2)}, u32[]{:S(2)}) %collective-permute-start.59) | collective-permute-done | bytes 1048608 | tf_op jit(solution)/shard_map/ppermute | solution.py:415
  535.2 16.7 %collective-permute-done.56 = bf16[1024,512]{1,0:T(8,128)(2,1)S(1)} collective-permute-done((bf16[1024,512]{1,0:T(8,128)(2,1)S(1)}, bf16[1024,512]{1,0:T(8,128)(2,1)S(1)}, u32[]{:S(2)}, u32[]{:S(2)}) %collective-permute-start.56) | collective-permute-done | bytes 1048608 | tf_op jit(solution)/shard_map/ppermute | solution.py:415
  564.7 11.5 %collective-permute-done.62 = bf16[340,1024]{1,0:T(8,128)(2,1)S(1)} collective-permute-done((bf16[340,1024]{1,0:T(8,128)(2,1)S(1)}, bf16[340,1024]{1,0:T(8,128)(2,1)S(1)}, u32[]{:S(2)}, u32[]{:S(2)}) %collective-permute-start.62) | collective-permute-done | bytes 696352 | tf_op jit(solution)/shard_map/ppermute | solution.py:419
  577.4 7.0 %reduce-scatter.20.cloned.1.call-done = bf16[1,256,512]{2,1,0:T(8,128)(2,1)} async-done(((bf16[4,256,512]{2,1,0:T(8,128)(2,1)}), bf16[1,256,512]{2,1,0:T(8,128)(2,1)}) %reduce-scatter.20.cloned.1.call-update) | async-done | bytes 262160 | tf_op jit(solution)/shard_map/reduce_scatter | solution.py:1168
  (647 shorter events, 239.1 us)
Async XLA Ops:
  7.2 36.8 %all-gather.9.cloned.1.call-start = ((), (), s32[]{:S(2)}) async-start(), calls=%async_computation.9 | async-start | bytes 1310720 | tf_op jit(solution)/shard_map/all_gather | solution.py:1216
  14.0 71.2 %all-gather.11.cloned.1.call-start = ((), (), s32[]{:S(2)}) async-start(), calls=%async_computation.10 | async-start | bytes 1310720 | tf_op jit(solution)/shard_map/all_gather | solution.py:1216
  14.7 115.4 %all-gather.13.cloned.1.call-start = ((), (), s32[]{:S(2)}) async-start(), calls=%async_computation.11 | async-start | bytes 1310720 | tf_op jit(solution)/shard_map/all_gather | solution.py:1216
  15.5 150.4 %all-gather.15.cloned.1.call-start = ((), (), s32[]{:S(2)}) async-start(), calls=%async_computation.12 | async-start | bytes 1310720 | tf_op jit(solution)/shard_map/all_gather | solution.py:1216
  18.5 182.5 %all-gather.17.cloned.1.call-start = ((), (), s32[]{:S(2)}) async-start(), calls=%async_computation.13 | async-start | bytes 1310720 | tf_op jit(solution)/shard_map/all_gather | solution.py:1216
  45.3 32.4 %collective-permute-start.4 = (bf16[1024,512]{1,0:T(8,128)(2,1)S(1)}, bf16[1024,512]{1,0:T(8,128)(2,1)S(1)}, u32[]{:S(2)}, u32[]{:S(2)}) collective-permute-start(bf16[1024,512]{1,0:T(8,128)(2,1)S(1)} %bitcast.277), channel_id=1, source_target_pairs={{0,1},{1,0},{2,3},{3,2},{4,5},{5,4},{6,7},{7,6},{8,9},{9,8},{10,11... | collective-permute-start | bytes 3145736 | tf_op jit(solution)/shard_map/ppermute | solution.py:415
  46.6 31.2 %collective-permute-start.5 = (bf16[1024,512]{1,0:T(8,128)(2,1)S(1)}, bf16[1024,512]{1,0:T(8,128)(2,1)S(1)}, u32[]{:S(2)}, u32[]{:S(2)}) collective-permute-start(bf16[1024,512]{1,0:T(8,128)(2,1)S(1)} %bitcast.278), channel_id=1, source_target_pairs={{0,16},{16,0},{1,17},{17,1},{2,18},{18,2},{3,19},{19,3},{4,20},{20... | collective-permute-start | bytes 3145736 | tf_op jit(solution)/shard_map/ppermute | solution.py:415
  56.8 210.1 %all-gather.19.cloned.1.call-start = ((), (), s32[]{:S(2)}) async-start(), calls=%async_computation.20 | async-start | bytes 5242880 | tf_op jit(solution)/shard_map/all_gather | solution.py:1265
  93.7 28.0 %collective-permute-start.9 = (bf16[1024,512]{1,0:T(8,128)(2,1)}, bf16[1024,512]{1,0:T(8,128)(2,1)S(1)}, u32[]{:S(2)}, u32[]{:S(2)}) collective-permute-start(bf16[1024,512]{1,0:T(8,128)(2,1)} %bitcast.302), channel_id=1, source_target_pairs={{0,1},{1,0},{2,3},{3,2},{4,5},{5,4},{6,7},{7,6},{8,9},{9,8},{10,11... | collective-permute-start | bytes 3145736 | tf_op jit(solution)/shard_map/ppermute | solution.py:415
  94.5 27.2 %collective-permute-start.10 = (bf16[1024,512]{1,0:T(8,128)(2,1)}, bf16[1024,512]{1,0:T(8,128)(2,1)S(1)}, u32[]{:S(2)}, u32[]{:S(2)}) collective-permute-start(bf16[1024,512]{1,0:T(8,128)(2,1)} %bitcast.303), channel_id=1, source_target_pairs={{0,16},{16,0},{1,17},{17,1},{2,18},{18,2},{3,19},{19,3},{4,20},{20... | collective-permute-start | bytes 3145736 | tf_op jit(solution)/shard_map/ppermute | solution.py:415
  122.2 292.1 %reduce-scatter.10.cloned.1.call-start = ((), (), s32[]{:S(2)}) async-start(), calls=%async_computation.14 | async-start | bytes 5242880 | tf_op jit(solution)/shard_map/reduce_scatter | solution.py:1168
  209.4 35.0 %collective-permute-start.26 = (bf16[1024,512]{1,0:T(8,128)(2,1)}, bf16[1024,512]{1,0:T(8,128)(2,1)}, u32[]{:S(2)}, u32[]{:S(2)}) collective-permute-start(bf16[1024,512]{1,0:T(8,128)(2,1)} %bitcast.298), channel_id=1, source_target_pairs={{0,1},{1,0},{2,3},{3,2},{4,5},{5,4},{6,7},{7,6},{8,9},{9,8},{10,11... | collective-permute-start | bytes 3145736 | tf_op jit(solution)/shard_map/ppermute | solution.py:415
  209.6 34.9 %collective-permute-start.27 = (bf16[1024,512]{1,0:T(8,128)(2,1)}, bf16[1024,512]{1,0:T(8,128)(2,1)}, u32[]{:S(2)}, u32[]{:S(2)}) collective-permute-start(bf16[1024,512]{1,0:T(8,128)(2,1)} %bitcast.299), channel_id=1, source_target_pairs={{0,16},{16,0},{1,17},{17,1},{2,18},{18,2},{3,19},{19,3},{4,20},{20... | collective-permute-start | bytes 3145736 | tf_op jit(solution)/shard_map/ppermute | solution.py:415
  315.7 135.3 %reduce-scatter.12.cloned.1.call-start = ((), (), s32[]{:S(2)}) async-start(), calls=%async_computation.15 | async-start | bytes 1310720 | tf_op jit(solution)/shard_map/reduce_scatter | solution.py:1168
  348.6 24.5 %collective-permute-start.40 = (bf16[512,512]{1,0:T(8,128)(2,1)}, bf16[512,512]{1,0:T(8,128)(2,1)S(1)}, u32[]{:S(2)}, u32[]{:S(2)}) collective-permute-start(bf16[512,512]{1,0:T(8,128)(2,1)} %bitcast.399), channel_id=1, source_target_pairs={{0,16},{16,0},{1,17},{17,1},{2,18},{18,2},{3,19},{19,3},{4,20},{20... | collective-permute-start | bytes 1572872 | tf_op jit(solution)/shard_map/ppermute | solution.py:415
  352.4 32.5 %collective-permute-start.42 = (bf16[1024,512]{1,0:T(8,128)(2,1)}, bf16[1024,512]{1,0:T(8,128)(2,1)S(1)}, u32[]{:S(2)}, u32[]{:S(2)}) collective-permute-start(bf16[1024,512]{1,0:T(8,128)(2,1)} %get-tuple-element.332), channel_id=1, source_target_pairs={{0,1},{1,0},{2,3},{3,2},{4,5},{5,4},{6,7},{7,6},{8,9},{9,8},{10,11... | collective-permute-start | bytes 3145736 | tf_op jit(solution)/shard_map/ppermute | solution.py:415
  353.8 31.1 %collective-permute-start.43 = (bf16[1024,512]{1,0:T(8,128)(2,1)}, bf16[1024,512]{1,0:T(8,128)(2,1)S(1)}, u32[]{:S(2)}, u32[]{:S(2)}) collective-permute-start(bf16[1024,512]{1,0:T(8,128)(2,1)} %get-tuple-element.333), channel_id=1, source_target_pairs={{0,16},{16,0},{1,17},{17,1},{2,18},{18,2},{3,19},{19,3},{4,20},{20... | collective-permute-start | bytes 3145736 | tf_op jit(solution)/shard_map/ppermute | solution.py:415
  388.9 66.6 %reduce-scatter.22.cloned.1.call-start = ((), (), s32[]{:S(2)}) async-start(), calls=%async_computation.21 | async-start | bytes 1310720
  391.7 25.9 %collective-permute-start.46 = (bf16[1024,512]{1,0:T(8,128)(2,1)}, bf16[1024,512]{1,0:T(8,128)(2,1)S(1)}, u32[]{:S(2)}, u32[]{:S(2)}) collective-permute-start(bf16[1024,512]{1,0:T(8,128)(2,1)} %get-tuple-element.344), channel_id=1, source_target_pairs={{0,1},{1,0},{2,3},{3,2},{4,5},{5,4},{6,7},{7,6},{8,9},{9,8},{10,11... | collective-permute-start | bytes 3145736 | tf_op jit(solution)/shard_map/ppermute | solution.py:415
  391.7 25.8 %collective-permute-start.47 = (bf16[1024,512]{1,0:T(8,128)(2,1)}, bf16[1024,512]{1,0:T(8,128)(2,1)S(1)}, u32[]{:S(2)}, u32[]{:S(2)}) collective-permute-start(bf16[1024,512]{1,0:T(8,128)(2,1)} %get-tuple-element.345), channel_id=1, source_target_pairs={{0,16},{16,0},{1,17},{17,1},{2,18},{18,2},{3,19},{19,3},{4,20},{20... | collective-permute-start | bytes 3145736 | tf_op jit(solution)/shard_map/ppermute | solution.py:415
  417.6 92.1 %reduce-scatter.16.cloned.1.call-start = ((), (), s32[]{:S(2)}) async-start(), calls=%async_computation.17 | async-start | bytes 1310720 | tf_op jit(solution)/shard_map/reduce_scatter | solution.py:1168
  419.9 30.8 %collective-permute-start.50 = (bf16[2,512,512]{2,1,0:T(8,128)(2,1)}, bf16[2,512,512]{2,1,0:T(8,128)(2,1)}, u32[]{:S(2)}, u32[]{:S(2)}) collective-permute-start(bf16[2,512,512]{2,1,0:T(8,128)(2,1)} %get-tuple-element.369), channel_id=1, source_target_pairs={{0,16},{16,0},{1,17},{17,1},{2,18},{18,2},{3,19},{19,3},{4,20},{20... | collective-permute-start | bytes 3145736 | tf_op jit(solution)/shard_map/ppermute | solution.py:415
  420.6 30.4 %collective-permute-start.51 = (bf16[2,512,512]{2,1,0:T(8,128)(2,1)}, bf16[2,512,512]{2,1,0:T(8,128)(2,1)}, u32[]{:S(2)}, u32[]{:S(2)}) collective-permute-start(bf16[2,512,512]{2,1,0:T(8,128)(2,1)} %get-tuple-element.370), channel_id=1, source_target_pairs={{0,1},{1,0},{2,3},{3,2},{4,5},{5,4},{6,7},{7,6},{8,9},{9,8},{10,11... | collective-permute-start | bytes 3145736 | tf_op jit(solution)/shard_map/ppermute | solution.py:415
  429.1 99.2 %reduce-scatter.14.cloned.1.call-start = ((), (), s32[]{:S(2)}) async-start(), calls=%async_computation.16 | async-start | bytes 1310720 | tf_op jit(solution)/shard_map/reduce_scatter | solution.py:1168
  459.1 24.6 %collective-permute-start.54 = (bf16[1024,512]{1,0:T(8,128)(2,1)}, bf16[1024,512]{1,0:T(8,128)(2,1)S(1)}, u32[]{:S(2)}, u32[]{:S(2)}) collective-permute-start(bf16[1024,512]{1,0:T(8,128)(2,1)} %get-tuple-element.388), channel_id=1, source_target_pairs={{0,1},{1,0},{2,3},{3,2},{4,5},{5,4},{6,7},{7,6},{8,9},{9,8},{10,11... | collective-permute-start | bytes 3145736 | tf_op jit(solution)/shard_map/ppermute | solution.py:415
  461.1 45.7 %collective-permute-start.52 = (bf16[512,512]{1,0:T(8,128)(2,1)}, bf16[512,512]{1,0:T(8,128)(2,1)}, u32[]{:S(2)}, u32[]{:S(2)}) collective-permute-start(bf16[512,512]{1,0:T(8,128)(2,1)} %bitcast.89), channel_id=1, source_target_pairs={{0,16},{16,0},{1,17},{17,1},{2,18},{18,2},{3,19},{19,3},{4,20},{20... | collective-permute-start | bytes 1572872 | tf_op jit(solution)/shard_map/ppermute | solution.py:415
  462.2 44.6 %collective-permute-start.53 = (bf16[512,512]{1,0:T(8,128)(2,1)}, bf16[512,512]{1,0:T(8,128)(2,1)}, u32[]{:S(2)}, u32[]{:S(2)}) collective-permute-start(bf16[512,512]{1,0:T(8,128)(2,1)} %bitcast.397), channel_id=1, source_target_pairs={{0,1},{1,0},{2,3},{3,2},{4,5},{5,4},{6,7},{7,6},{8,9},{9,8},{10,11... | collective-permute-start | bytes 1572872 | tf_op jit(solution)/shard_map/ppermute | solution.py:415
  492.1 28.1 %collective-permute-start.59 = (bf16[1024,512]{1,0:T(8,128)(2,1)S(1)}, bf16[1024,512]{1,0:T(8,128)(2,1)}, u32[]{:S(2)}, u32[]{:S(2)}) collective-permute-start(bf16[1024,512]{1,0:T(8,128)(2,1)S(1)} %copy-done.35), channel_id=1, source_target_pairs={{0,1},{1,0},{2,3},{3,2},{4,5},{5,4},{6,7},{7,6},{8,9},{9,8},{10,11... | collective-permute-start | bytes 3145736 | tf_op jit(solution)/shard_map/ppermute | solution.py:415
  492.2 29.3 %collective-permute-start.60 = (bf16[1024,512]{1,0:T(8,128)(2,1)}, bf16[1024,512]{1,0:T(8,128)(2,1)}, u32[]{:S(2)}, u32[]{:S(2)}) collective-permute-start(bf16[1024,512]{1,0:T(8,128)(2,1)} %get-tuple-element.412), channel_id=1, source_target_pairs={{0,16},{16,0},{1,17},{17,1},{2,18},{18,2},{3,19},{19,3},{4,20},{20... | collective-permute-start | bytes 3145736 | tf_op jit(solution)/shard_map/ppermute | solution.py:415
  506.7 48.6 %reduce-scatter.18.cloned.1.call-start = ((), (), s32[]{:S(2)}) async-start(), calls=%async_computation.18 | async-start | bytes 1310720 | tf_op jit(solution)/shard_map/reduce_scatter | solution.py:1168
  524.5 59.9 %reduce-scatter.20.cloned.1.call-start = ((), (), s32[]{:S(2)}) async-start(), calls=%async_computation.19 | async-start | bytes 1310720 | tf_op jit(solution)/shard_map/reduce_scatter | solution.py:1168
  555.8 30.5 %collective-permute-start.61 = (bf16[340,1024]{1,0:T(8,128)(2,1)S(1)}, bf16[340,1024]{1,0:T(8,128)(2,1)S(1)}, u32[]{:S(2)}, u32[]{:S(2)}) collective-permute-start(bf16[340,1024]{1,0:T(8,128)(2,1)S(1)} %maximum_select_fusion.3), channel_id=1, source_target_pairs={{1,8},{8,1},{3,10},{10,3},{5,12},{12,5},{7,14},{14,7},{17,24},{24,... | collective-permute-start | bytes 2088968 | tf_op jit(solution)/shard_map/ppermute | solution.py:419
  (142 other events, 1140.1 us)
Sparse Core Ops, SparseCore 0:
  14.1 29.8 all-gather.8
  45.6 34.0 all-gather.10
  81.3 26.6 all-gather.12
  109.4 27.4 all-gather.14
  138.8 27.4 all-gather.16
  167.7 80.3 all-gather.18
  315.9 75.3 reduce-scatter.9
  393.6 27.4 reduce-scatter.11
  424.0 31.4 reduce-scatter.21
  457.7 26.5 reduce-scatter.15
  491.7 31.2 reduce-scatter.13
  525.9 26.6 reduce-scatter.17
  559.5 24.8 reduce-scatter.19
